TPU v7x, 32 devices: a whole 2x2x4 slice. The times are simulated.
32 devices in a mesh: scan: 4 (over y, x), slab: 8 (over z, core).
Axes of the slice: x: 2, y: 2, z: 4, core: 2. Of those that a mesh axis runs over, the one named last changes fastest.
Arguments:
- volume: float32 [4, 4096, 1024], P('scan', 'slab'), may hold values from -108 to 108
- velocity0: float32 [4, 4096], P('scan', 'slab'), may hold values from -0.5 to 0.5
- fetch_slab: int32 [4, 2, 4096, 1], P('scan', None, 'slab'), may hold values from 0 to 7; in each aligned block of 512 rows (0 to 511, 512 to 1023, ..., all dimensions but the last counted through in order) at most 96 rows name the same one
- fetch_row: int32 [4, 2, 4096], P('scan', None, 'slab'), may hold values from 0 to 511
- modulus_class: int32 [4, 4096], P('scan', 'slab'), may hold values from 0 to 3
- modulus_table: float32 [4], replicated, may hold values from 200 to 3000
Outputs:
- velocity: float32 [4, 4096], P('scan', 'slab')
- misfit: float32 [4, 4096, 1024], P('scan', 'slab')
Inputs may be any that keep to these rules, and one draw needn't show every extreme that they name: `fetch_slab`: among the rows of one device for one direction, at most 96 name the same slab, a bound that some block reaches of them.
All inputs are finite; a program needn't handle non-finite values.
Results may differ from a plain program's by a relative error of at most 0.00011.
Values sent between devices are 32-bit elements; how exact they have to be, the bound alone decides.
No kernel may reach another device: no remote copies, remote signals or barrier semaphores. Data moves between devices by JAX's collectives and lax.ppermute only.
A program may use at most 64 MiB of HBM per device.

v0:
```python
import math

import jax
import jax.numpy as jnp
from jax import lax
from jax.sharding import PartitionSpec as P

Y = 1024
BAND = 32
ITERS = 2


root_three = math.sqrt(3.0)
pole_value = math.sqrt(3.0) - 2.0


def with_halo(cells, sides, width):
    for axis, dim in sides:
        count = lax.axis_size(axis)
        ends = count - 1
        head = lax.slice_in_dim(cells, 0, width, axis=dim)
        tail = lax.slice_in_dim(cells, cells.shape[dim] - width, cells.shape[dim], axis=dim)
        cells = jnp.concatenate(
            [
                lax.ppermute(tail, axis, [(i, (i + 1) % count) for i in range(ends)]),
                cells,
                lax.ppermute(head, axis, [((i + 1) % count, i) for i in range(ends)]),
            ],
            axis=dim,
        )
    return cells


def passed_along(block, axis, distance):
    devices = range(lax.axis_size(axis))
    route = [(i - distance, i) for i in devices if i - distance in devices]
    return lax.ppermute(block, axis, route)


def filter_block(block_width, band_reach):
    offsets = (
        lax.broadcasted_iota(jnp.int32, (3 * block_width, block_width), 0)
        - block_width
        - lax.broadcasted_iota(jnp.int32, (3 * block_width, block_width), 1)
    )
    distance = jnp.abs(offsets)
    parity = 1.0 - 2.0 * (distance % 2).astype(jnp.float32)
    magnitude = jnp.exp(distance.astype(jnp.float32) * math.log(-pole_value))
    return jnp.where(
        distance <= band_reach, root_three * parity * magnitude, jnp.zeros_like(magnitude)
    )


def prefilter(voxels):
    length = voxels.shape[1]
    block_width = min(128, length)
    matrix = filter_block(block_width, BAND)
    padded = jnp.pad(voxels, ((0, 0), (block_width, block_width)))
    pieces = []
    for number in range(length // block_width):
        window = padded[:, number * block_width : number * block_width + 3 * block_width]
        pieces.append(
            jnp.dot(
                window, matrix, preferred_element_type=jnp.float32, precision=lax.Precision.HIGHEST
            )
        )
    return jnp.concatenate(pieces, axis=1)


def taylor_terms(coeffs):
    padded = jnp.pad(coeffs, ((0, 0), (1, 1)))
    before = padded[:, :-2]
    after = padded[:, 2:]
    value = (before + 4.0 * coeffs + after) / 6.0
    slope = 0.5 * (after - before)
    bend = after - 2.0 * coeffs + before
    return (value, slope, bend)


def residuals(forward, backward, voxels, velocity):
    moved = velocity[:, None]
    fwd_value, fwd_slope, fwd_bend = taylor_terms(forward)
    bwd_value, bwd_slope, bwd_bend = taylor_terms(backward)
    res_fwd = fwd_value + moved * fwd_slope + 0.5 * moved * moved * fwd_bend - voxels
    jac_fwd = fwd_slope + moved * fwd_bend
    res_bwd = bwd_value - moved * bwd_slope + 0.5 * moved * moved * bwd_bend - voxels
    jac_bwd = moved * bwd_bend - bwd_slope
    return (res_fwd, jac_fwd, res_bwd, jac_bwd)


def row_terms(forward, backward, voxels, velocity):
    res_fwd, jac_fwd, res_bwd, jac_bwd = residuals(forward, backward, voxels, velocity)
    linear = jnp.sum(jac_fwd * res_fwd + jac_bwd * res_bwd, axis=1)
    curvature = jnp.sum(jac_fwd * jac_fwd + jac_bwd * jac_bwd, axis=1)
    return (linear, curvature)


def plane_stencil(field):
    count_rows = field.shape[0]
    hops = Y // count_rows
    rimmed = with_halo(field[None, :], (("slab", 1),), 1)[0]
    lower = passed_along(field, "slab", hops)
    upper = passed_along(field, "slab", -hops)
    return 4.0 * field - rimmed[:-2] - rimmed[2:] - lower - upper


def on_device(volume, velocity0, fetch_slab, fetch_row, modulus_class, modulus_table):
    own_scan = volume[0]
    count_rows = own_scan.shape[0]
    devices = lax.axis_size("slab")
    capacity = max(2, 3 * count_rows // (2 * devices))
    source = prefilter(own_scan)
    ahead_rows = passed_along(source, "scan", -1)
    behind = passed_along(source, "scan", 1)
    peer_ids = fetch_slab[0, :, :, 0]
    wanted_rows = fetch_row[0]
    one_hot = (peer_ids[:, :, None] == lax.broadcasted_iota(jnp.int32, (1, 1, devices), 2)).astype(
        jnp.int32
    )
    running = jnp.cumsum(one_hot, axis=1) - one_hot
    slot_ids = jnp.sum(running * one_hot, axis=2)
    direction_ids = lax.broadcasted_iota(jnp.int32, (2, count_rows), 0)
    request_table = (
        jnp.zeros((2, devices, capacity), jnp.int32)
        .at[direction_ids, peer_ids, slot_ids]
        .set(wanted_rows)
    )
    asked_rows = lax.all_to_all(request_table, "slab", split_axis=1, concat_axis=1, tiled=True)
    forward_rows = jnp.take(ahead_rows, asked_rows[0], axis=0)
    backward_rows = jnp.take(behind, asked_rows[1], axis=0)
    arrived = lax.all_to_all(
        jnp.stack([forward_rows, backward_rows]), "slab", split_axis=1, concat_axis=1, tiled=True
    )
    fetched = arrived[direction_ids, peer_ids, slot_ids]
    forward = fetched[0]
    backward = fetched[1]
    classes = lax.broadcasted_iota(jnp.int32, (1, modulus_table.shape[0]), 1)
    weight = jnp.sum(
        jnp.where(
            modulus_class[0][:, None] == classes,
            modulus_table[None, :],
            jnp.zeros_like(modulus_table)[None, :],
        ),
        axis=1,
    )
    stiffness = jnp.sqrt(weight)
    velocity = velocity0[0]
    for iteration in range(ITERS):
        linear, curvature = row_terms(forward, backward, own_scan, velocity)
        gradient = linear + stiffness * plane_stencil(stiffness * velocity)
        diagonal = curvature + 4.0 * stiffness * stiffness
        direction = gradient / diagonal
        scaled_dir = stiffness * direction
        bend_term = scaled_dir * plane_stencil(scaled_dir)
        totals = lax.psum(
            (jnp.sum(direction * gradient), jnp.sum(curvature * direction * direction + bend_term)),
            ("scan", "slab"),
        )
        velocity = velocity - totals[0] / totals[1] * direction
    res_fwd, jac_fwd, res_bwd, jac_bwd = residuals(forward, backward, own_scan, velocity)
    return (velocity[None, :], (res_fwd + res_bwd)[None])


def solution(mesh):
    return jax.shard_map(
        on_device,
        mesh=mesh,
        in_specs=(
            P("scan", "slab", None),
            P("scan", "slab"),
            P("scan", None, "slab", None),
            P("scan", None, "slab"),
            P("scan", "slab"),
            P(),
        ),
        out_specs=(P("scan", "slab"), P("scan", "slab", None)),
        check_vma=False,
    )
```

profile of v0, /device:TPU:0, one launch (start us, length us, event | category | flops | bytes accessed | tf_op | source)
XLA Modules:
  0.0 449.3 jit_solution(7488137863564150080)
XLA Ops:
  0.7 3.0 convolution_dynamic-update-slice_fusion.1
  3.7 1.9 fusion.7
  5.5 1.9 fusion.6
  7.4 1.9 fusion.5
  9.3 1.9 fusion.4
  11.2 1.9 fusion.3
  13.1 1.9 fusion.2
  14.9 1.8 convolution_dynamic-update-slice_fusion
  16.8 1.3 collective-permute-start
  18.1 6.9 %collective-permute-start.1 = (f32[512,1024]{0,1:T(8,128)}, f32[512,1024]{0,1:T(8,128)}, u32[]{:S(2)}, u32[]{:S(2)}) collective-permute-start(f32[512,1024]{0,1:T(8,128)} %convolution_dynamic-update-slice_fusion), channel_id=1, source_target_pairs={{0,8},{8,16},{16,24},{1,9},{9,17},{17,25},{2,10},{10,18},{18,26},{... | collective-permute-start | bytes 6291464 | tf_op jit(solution)/shard_map/ppermute | solution.py:37
  24.9 2.3 reduce-window.6
  27.2 0.3 slice_reduce_fusion
  27.5 0.1 fusion.31
  27.7 0.1 multiply_reduce_fusion
  27.8 0.1 and_reduce_fusion
  27.9 4.3 scatter_custom_fusion
  32.3 10.8 %all_to_all.10 = s32[2,8,96]{2,0,1:T(2,128)S(1)} all-to-all(s32[2,8,96]{2,0,1:T(2,128)S(1)} %copy.19), channel_id=1, replica_groups=mesh['scan'=4,'slab'=8] {'slab'}, dimensions={1} | all-to-all | bytes 12288 | tf_op jit(solution)/shard_map/all_to_all | solution.py:128
  43.3 25.0 %collective-permute-done = f32[512,1024]{0,1:T(8,128)} collective-permute-done((f32[512,1024]{0,1:T(8,128)}, f32[512,1024]{0,1:T(8,128)}, u32[]{:S(2)}, u32[]{:S(2)}) %collective-permute-start) | collective-permute-done | bytes 2097184 | tf_op jit(solution)/shard_map/ppermute | solution.py:37
  68.4 1.9 copy.20
  70.3 3.6 gather_fusion.1
  73.9 1.9 copy.21
  75.9 3.7 gather_fusion.2
  79.5 3.4 select_bitcast_fusion
  82.9 3.4 pad_maximum_fusion
  86.3 5.6 %all-to-all-start.1 = ((f32[2,8,96,1024]{3,2,0,1:T(8,128)}), f32[2,8,96,1024]{3,2,0,1:T(8,128)}, u32[]{:S(2)}, u32[]{:S(2)}) async-start(f32[2,8,96,1024]{3,2,0,1:T(8,128)} %pad_maximum_fusion), calls=%async_computation.1 | async-start | bytes 12582912 | tf_op jit(solution)/shard_map/all_to_all | solution.py:131
  92.0 3.9 collective-permute-start.4
  96.0 1.3 collective-permute-start.5
  97.3 0.6 fusion.121
  97.9 2.3 collective-permute-start.2
  100.2 1.3 collective-permute-start.3
  101.5 3.7 collective-permute-done.3
  105.1 1.4 pad_maximum_fusion.8
  106.5 124.5 %all-to-all-done.1 = f32[2,8,96,1024]{3,2,0,1:T(8,128)} async-done(((f32[2,8,96,1024]{3,2,0,1:T(8,128)}), f32[2,8,96,1024]{3,2,0,1:T(8,128)}, u32[]{:S(2)}, u32[]{:S(2)}) %all-to-all-start.1) | async-done | bytes 6291488 | tf_op jit(solution)/shard_map/all_to_all | solution.py:131
  231.0 6.6 %copy.22 = f32[2,8,96,1024]{3,2,1,0:T(8,128)} copy(f32[2,8,96,1024]{3,2,0,1:T(8,128)} %all-to-all-done.1) | data formatting | bytes 12582912 | tf_op jit(solution)/shard_map/all_to_all | solution.py:131
  237.6 21.5 %gather_fusion = f32[1024,1024]{1,0:T(8,128)} fusion(f32[2,8,96,1024]{3,2,1,0:T(8,128)} %copy.22, s32[1024]{0:T(1024)S(1)} %bitcast.75), kind=kCustom, calls=%fused_computation.2 | custom fusion | bytes 8400896 | tf_op jit(solution)/shard_map/gather | solution.py:134
  259.0 2.7 fusion.116
  261.7 0.2 copy-done.1
  261.9 9.8 %add_reduce_fusion.2 = (f32[512]{0:T(512)S(1)}, f32[512]{0:T(512)S(1)}, f32[512,1024]{1,0:T(8,128)}, f32[512,1024]{1,0:T(8,128)}, f32[512,1024]{1,0:T(8,128)}, /...) fusion(f32[512]{0:T(512)S(1)} %bitcast.87, f32[1,512,1024]{2,1,0:T(8,128)S(1)} %copy-done.1, ...), kind=kLoop, calls=%fused_computation.18 | loop fusion | flops 20970496 | bytes 18884608 | tf_op jit(solution)/shard_map/reduce_sum | solution.py:94
  271.7 1.3 collective-permute-start.8
  273.0 1.3 collective-permute-start.9
  274.3 0.6 fusion.120
  274.9 4.7 %collective-permute-start.6 = (f32[1,1]{1,0:T(1,128)}, f32[1,1]{1,0:T(1,128)}, u32[]{:S(2)}, u32[]{:S(2)}) collective-permute-start(f32[1,1]{1,0:T(1,128)} %get-tuple-element.50), channel_id=1, source_target_pairs={{0,1},{1,2},{2,3},{3,4},{4,5},{5,6},{6,7},{8,9},{9,10},{10,11},{11... | collective-permute-start | bytes 20 | tf_op jit(solution)/shard_map/ppermute | solution.py:25
  279.6 1.3 collective-permute-start.7
  280.9 2.0 collective-permute-done.7
  283.0 1.3 pad_maximum_fusion.6
  284.3 0.7 fusion.36
  285.0 79.9 %all-reduce.4 = (f32[]{:T(128)}, f32[]{:T(128)}) all-reduce(f32[]{:T(128)} %get-tuple-element.10, f32[]{:T(128)} %get-tuple-element.9), channel_id=1, replica_groups=mesh['scan'=4,'slab'=8] {'scan','slab'}, use_global_device_ids=true, to_apply=%region_8.10 | all-reduce | flops 2 | bytes 16 | tf_op jit(solution)/shard_map/psum | solution.py:155
  366.2 2.2 collective-permute-start.12
  368.4 1.3 collective-permute-start.13
  369.7 0.6 fusion.119
  370.3 1.8 collective-permute-start.10
  372.1 1.3 collective-permute-start.11
  373.4 5.7 %add_reduce_fusion = (f32[512]{0:T(512)S(1)}, f32[512]{0:T(512)S(1)}) fusion(f32[512,1024]{1,0:T(8,128)} %get-tuple-element.30, f32[512,1024]{1,0:T(8,128)} %get-tuple-element.29, f32[512,1024]{1,0:T(8,128)} %get-tuple-element.28, f32[512,1024]{1,0:T(8,128)} %get-tuple-element.27, f32[512]{0:T(512)S(1)} %get-tuple-element.21, ...), kind=kLoop, calls=%fused_computation.14 | loop fusion | flops 12581888 | bytes 14690304 | tf_op jit(solution)/shard_map/reduce_sum | solution.py:94
  379.1 1.3 pad_maximum_fusion.4
  380.5 7.0 %collective-permute-start.16 = (f32[512]{0:T(512)S(1)}, f32[512]{0:T(512)S(1)}, u32[]{:S(2)}, u32[]{:S(2)}) collective-permute-start(f32[512]{0:T(512)S(1)} %get-tuple-element.17), channel_id=1, source_target_pairs={{0,2},{1,3},{2,4},{3,5},{4,6},{5,7},{8,10},{9,11},{10,12},{11,13},... | collective-permute-start | bytes 6152 | tf_op jit(solution)/shard_map/ppermute | solution.py:37
  387.5 1.3 collective-permute-start.17
  388.8 0.6 fusion.118
  389.4 1.9 collective-permute-start.14
  391.3 1.3 collective-permute-start.15
  392.6 4.2 collective-permute-done.15
  396.7 1.3 pad_maximum_fusion.2
  398.1 0.7 fusion.38
  398.8 42.3 %all-reduce.3 = (f32[]{:T(128)}, f32[]{:T(128)}) all-reduce(f32[]{:T(128)} %get-tuple-element.8, f32[]{:T(128)} %get-tuple-element.7), channel_id=1, replica_groups=mesh['scan'=4,'slab'=8] {'scan','slab'}, use_global_device_ids=true, to_apply=%region_14.16 | all-reduce | flops 2 | bytes 16 | tf_op jit(solution)/shard_map/psum | solution.py:155
  442.4 6.9 %add_bitcast_fusion = f32[1,512,1024]{2,1,0:T(8,128)} fusion(f32[512,1024]{1,0:T(8,128)} %get-tuple-element.29, f32[512,1024]{1,0:T(8,128)} %get-tuple-element.26, f32[512,1024]{1,0:T(8,128)} %get-tuple-element.30, f32[512,1024]{1,0:T(8,128)} %get-tuple-element.28, f32[512,1024]{1,0:T(8,128)} %get-tuple-element.25, f32[512,1024]{1,0:T(8,128)} %get-tuple-element.27, ...), kind=kLoop, calls=%fused_computation.13 | loop fusion | flops 5767168 | bytes 16781312 | tf_op jit(solution)/shard_map/broadcast_in_dim | solution.py:161
  (63 shorter events, 0.6 us)
Async XLA Ops:
  0.6 3.0 copy-start
  13.1 11.9 %copy-start.3 = (s32[1,2,512,1]{2,3,1,0:T(1,128)S(1)}, s32[1,2,512,1]{2,3,1,0:T(1,128)}, u32[]{:S(2)}) copy-start(s32[1,2,512,1]{2,3,1,0:T(1,128)} %param.10) | copy-start | bytes 12292
  13.1 14.6 %copy-start.8 = (s32[3]{0:T(128)S(1)}, s32[3]{0:T(128)}, u32[]{:S(2)}) copy-start(s32[3]{0:T(128)} %constant.79) | copy-start | bytes 40
  13.1 14.7 %copy-start.9 = (s32[3]{0:T(128)S(1)}, s32[3]{0:T(128)}, u32[]{:S(2)}) copy-start(s32[3]{0:T(128)} %constant.82) | copy-start | bytes 40
  13.1 14.8 %copy-start.5 = (s32[1,2,512]{2,1,0:T(2,128)S(1)}, s32[1,2,512]{2,1,0:T(2,128)}, u32[]{:S(2)}) copy-start(s32[1,2,512]{2,1,0:T(2,128)} %param.11) | copy-start | bytes 12292
  16.8 51.6 %collective-permute-start = (f32[512,1024]{0,1:T(8,128)}, f32[512,1024]{0,1:T(8,128)}, u32[]{:S(2)}, u32[]{:S(2)}) collective-permute-start(f32[512,1024]{0,1:T(8,128)} %convolution_dynamic-update-slice_fusion), channel_id=1, source_target_pairs={{8,0},{16,8},{24,16},{9,1},{17,9},{25,17},{10,2},{18,10},{26,18},{... | collective-permute-start | bytes 6291464 | tf_op jit(solution)/shard_map/ppermute | solution.py:37
  18.1 55.9 %collective-permute-start.1 = (f32[512,1024]{0,1:T(8,128)}, f32[512,1024]{0,1:T(8,128)}, u32[]{:S(2)}, u32[]{:S(2)}) collective-permute-start(f32[512,1024]{0,1:T(8,128)} %convolution_dynamic-update-slice_fusion), channel_id=1, source_target_pairs={{0,8},{8,16},{16,24},{1,9},{9,17},{17,25},{2,10},{10,18},{18,26},{... | collective-permute-start | bytes 6291464 | tf_op jit(solution)/shard_map/ppermute | solution.py:37
  86.3 5.6 %copy-start.6 = (s32[1,512]{1,0:T(1,128)S(1)}, s32[1,512]{1,0:T(1,128)}, u32[]{:S(2)}) copy-start(s32[1,512]{1,0:T(1,128)} %param.12) | copy-start | bytes 6148
  86.3 5.6 %copy-start.7 = (f32[4]{0:T(128)S(1)}, f32[4]{0:T(128)}, u32[]{:S(2)}) copy-start(f32[4]{0:T(128)} %param.13) | copy-start | bytes 52
  86.3 5.7 %copy-start.2 = (f32[1,512]{1,0:T(1,128)S(1)}, f32[1,512]{1,0:T(1,128)}, u32[]{:S(2)}) copy-start(f32[1,512]{1,0:T(1,128)} %param.9) | copy-start | bytes 6148
  86.3 144.7 %all-to-all-start.1 = ((f32[2,8,96,1024]{3,2,0,1:T(8,128)}), f32[2,8,96,1024]{3,2,0,1:T(8,128)}, u32[]{:S(2)}, u32[]{:S(2)}) async-start(f32[2,8,96,1024]{3,2,0,1:T(8,128)} %pad_maximum_fusion), calls=%async_computation.1 | async-start | bytes 12582912 | tf_op jit(solution)/shard_map/all_to_all | solution.py:131
  92.0 179.7 %collective-permute-start.4 = (f32[512]{0:T(512)S(1)}, f32[512]{0:T(512)S(1)}, u32[]{:S(2)}, u32[]{:S(2)}) collective-permute-start(f32[512]{0:T(512)S(1)} %get-tuple-element.57), channel_id=1, source_target_pairs={{0,2},{1,3},{2,4},{3,5},{4,6},{5,7},{8,10},{9,11},{10,12},{11,13},... | collective-permute-start | bytes 6152 | tf_op jit(solution)/shard_map/ppermute | solution.py:37
  96.0 175.7 %collective-permute-start.5 = (f32[512]{0:T(512)S(1)}, f32[512]{0:T(512)S(1)}, u32[]{:S(2)}, u32[]{:S(2)}) collective-permute-start(f32[512]{0:T(512)S(1)} %get-tuple-element.57), channel_id=1, source_target_pairs={{2,0},{3,1},{4,2},{5,3},{6,4},{7,5},{10,8},{11,9},{12,10},{13,11},... | collective-permute-start | bytes 6152 | tf_op jit(solution)/shard_map/ppermute | solution.py:37
  97.9 3.6 collective-permute-start.2
  100.2 5.0 %collective-permute-start.3 = (f32[1,1]{1,0:T(1,128)}, f32[1,1]{1,0:T(1,128)}, u32[]{:S(2)}, u32[]{:S(2)}) collective-permute-start(f32[1,1]{1,0:T(1,128)} %get-tuple-element.55), channel_id=1, source_target_pairs={{1,0},{2,1},{3,2},{4,3},{5,4},{6,5},{7,6},{9,8},{10,9},{11,10},{12... | collective-permute-start | bytes 20 | tf_op jit(solution)/shard_map/ppermute | solution.py:27
  259.0 2.9 copy-start.1
  271.7 12.6 %collective-permute-start.8 = (f32[512]{0:T(512)S(1)}, f32[512]{0:T(512)S(1)}, u32[]{:S(2)}, u32[]{:S(2)}) collective-permute-start(f32[512]{0:T(512)S(1)} %get-tuple-element.22), channel_id=1, source_target_pairs={{0,2},{1,3},{2,4},{3,5},{4,6},{5,7},{8,10},{9,11},{10,12},{11,13},... | collective-permute-start | bytes 6152 | tf_op jit(solution)/shard_map/ppermute | solution.py:37
  273.0 11.3 %collective-permute-start.9 = (f32[512]{0:T(512)S(1)}, f32[512]{0:T(512)S(1)}, u32[]{:S(2)}, u32[]{:S(2)}) collective-permute-start(f32[512]{0:T(512)S(1)} %get-tuple-element.22), channel_id=1, source_target_pairs={{2,0},{3,1},{4,2},{5,3},{6,4},{7,5},{10,8},{11,9},{12,10},{13,11},... | collective-permute-start | bytes 6152 | tf_op jit(solution)/shard_map/ppermute | solution.py:37
  274.9 6.0 %collective-permute-start.6 = (f32[1,1]{1,0:T(1,128)}, f32[1,1]{1,0:T(1,128)}, u32[]{:S(2)}, u32[]{:S(2)}) collective-permute-start(f32[1,1]{1,0:T(1,128)} %get-tuple-element.50), channel_id=1, source_target_pairs={{0,1},{1,2},{2,3},{3,4},{4,5},{5,6},{6,7},{8,9},{9,10},{10,11},{11... | collective-permute-start | bytes 20 | tf_op jit(solution)/shard_map/ppermute | solution.py:25
  279.6 3.3 collective-permute-start.7
  366.2 14.2 %collective-permute-start.12 = (f32[512]{0:T(512)S(1)}, f32[512]{0:T(512)S(1)}, u32[]{:S(2)}, u32[]{:S(2)}) collective-permute-start(f32[512]{0:T(512)S(1)} %get-tuple-element.20), channel_id=1, source_target_pairs={{0,2},{1,3},{2,4},{3,5},{4,6},{5,7},{8,10},{9,11},{10,12},{11,13},... | collective-permute-start | bytes 6152 | tf_op jit(solution)/shard_map/ppermute | solution.py:37
  368.4 12.1 %collective-permute-start.13 = (f32[512]{0:T(512)S(1)}, f32[512]{0:T(512)S(1)}, u32[]{:S(2)}, u32[]{:S(2)}) collective-permute-start(f32[512]{0:T(512)S(1)} %get-tuple-element.20), channel_id=1, source_target_pairs={{2,0},{3,1},{4,2},{5,3},{6,4},{7,5},{10,8},{11,9},{12,10},{13,11},... | collective-permute-start | bytes 6152 | tf_op jit(solution)/shard_map/ppermute | solution.py:37
  370.3 8.8 %collective-permute-start.10 = (f32[1,1]{1,0:T(1,128)}, f32[1,1]{1,0:T(1,128)}, u32[]{:S(2)}, u32[]{:S(2)}) collective-permute-start(f32[1,1]{1,0:T(1,128)} %get-tuple-element.44), channel_id=1, source_target_pairs={{0,1},{1,2},{2,3},{3,4},{4,5},{5,6},{6,7},{8,9},{9,10},{10,11},{11... | collective-permute-start | bytes 20 | tf_op jit(solution)/shard_map/ppermute | solution.py:25
  372.1 7.0 %collective-permute-start.11 = (f32[1,1]{1,0:T(1,128)}, f32[1,1]{1,0:T(1,128)}, u32[]{:S(2)}, u32[]{:S(2)}) collective-permute-start(f32[1,1]{1,0:T(1,128)} %get-tuple-element.45), channel_id=1, source_target_pairs={{1,0},{2,1},{3,2},{4,3},{5,4},{6,5},{7,6},{9,8},{10,9},{11,10},{12... | collective-permute-start | bytes 20 | tf_op jit(solution)/shard_map/ppermute | solution.py:27
  380.5 17.6 %collective-permute-start.16 = (f32[512]{0:T(512)S(1)}, f32[512]{0:T(512)S(1)}, u32[]{:S(2)}, u32[]{:S(2)}) collective-permute-start(f32[512]{0:T(512)S(1)} %get-tuple-element.17), channel_id=1, source_target_pairs={{0,2},{1,3},{2,4},{3,5},{4,6},{5,7},{8,10},{9,11},{10,12},{11,13},... | collective-permute-start | bytes 6152 | tf_op jit(solution)/shard_map/ppermute | solution.py:37
  387.5 10.6 %collective-permute-start.17 = (f32[512]{0:T(512)S(1)}, f32[512]{0:T(512)S(1)}, u32[]{:S(2)}, u32[]{:S(2)}) collective-permute-start(f32[512]{0:T(512)S(1)} %get-tuple-element.17), channel_id=1, source_target_pairs={{2,0},{3,1},{4,2},{5,3},{6,4},{7,5},{10,8},{11,9},{12,10},{13,11},... | collective-permute-start | bytes 6152 | tf_op jit(solution)/shard_map/ppermute | solution.py:37
  389.4 3.2 collective-permute-start.14
  391.3 5.5 %collective-permute-start.15 = (f32[1,1]{1,0:T(1,128)}, f32[1,1]{1,0:T(1,128)}, u32[]{:S(2)}, u32[]{:S(2)}) collective-permute-start(f32[1,1]{1,0:T(1,128)} %get-tuple-element.41), channel_id=1, source_target_pairs={{1,0},{2,1},{3,2},{4,3},{5,4},{6,5},{7,6},{9,8},{10,9},{11,10},{12... | collective-permute-start | bytes 20 | tf_op jit(solution)/shard_map/ppermute | solution.py:27
  442.4 6.9 %copy-start.4 = (f32[512]{0:T(512)}, f32[512]{0:T(512)S(1)}, u32[]{:S(2)}) copy-start(f32[512]{0:T(512)S(1)} %get-tuple-element.16) | copy-start | bytes 6148
where the time goes:
time: 451 us; the launch traced here: 449 us
  waiting for transfers between devices  159 us (35%)
  blocking collectives  133 us (29%)
  local copies, waits for them, and re-layouts  49.2 us (11%)
  starting transfers between devices  49.2 us (11%)
  other arithmetic  38.7 us (9%)
  matrix products  16.1 us (4%)
    all_to_all x1, waiting for transfers between devices, on_device(): lax.all_to_all(jnp.stack([forward_rows, backward_rows]), 'slab', split_ax...  124 us
    psum x2, blocking collectives, on_device(): lax.psum((jnp.sum(direction * gradient), jnp.sum(curvature * direction *...  122 us
    ppermute x10, starting transfers between devices, passed_along(): return lax.ppermute(block, axis, route)  27.7 us
    ppermute x10, waiting for transfers between devices, passed_along(): return lax.ppermute(block, axis, route)  25.1 us
    gather x1, local copies, waits for them, and re-layouts, on_device(): fetched = arrived[direction_ids, peer_ids, slot_ids]  21.5 us
    dot_general x8, matrix products, prefilter(): jnp.dot(window, matrix, preferred_element_type=jnp.float32, precision=lax...  16.1 us
    reduce_sum x2, other arithmetic, row_terms(): curvature = jnp.sum(jac_fwd * jac_fwd + jac_bwd * jac_bwd, axis=1)  15.5 us
    all_to_all x1, blocking collectives, on_device(): lax.all_to_all(request_table, 'slab', split_axis=1, concat_axis=1, tiled=...  10.8 us
  transfers between devices with their start and end apart: 19, of which 5 were waited for; matrix products, arithmetic and copies ran while one was open for 15% of the time, Pallas kernels for 0%

commit v1 on v0

v1 whole, which is shorter than its diff:
```python
import functools
import math

import jax
import jax.numpy as jnp
import numpy as np
from jax import lax
from jax.experimental import pallas as pl
from jax.experimental.pallas import tpu as pltpu
from jax.sharding import PartitionSpec as P

Y = 1024
BAND = 32
ITERS = 2
SUMS = 5
FIELDS = 7
VMEM = pl.BlockSpec(memory_space=pltpu.VMEM)
SMEM = pl.BlockSpec(memory_space=pltpu.SMEM)
LIMIT = pltpu.CompilerParams(vmem_limit_bytes=32 * 1024 * 1024)


def filter_parts(width, rim):
    offsets = np.arange(width + 2 * rim)[:, None] - rim - np.arange(width)[None, :]
    distance = np.abs(offsets)
    pole = math.sqrt(3.0) - 2.0
    exact = np.where(distance <= BAND, math.sqrt(3.0) * pole ** np.minimum(distance, BAND), 0.0)
    exact = exact.astype(np.float32)
    high = exact.astype(jnp.bfloat16)
    low = (exact - high.astype(np.float32)).astype(jnp.bfloat16)
    return high, low


def prefilter_kernel(width, rim, vol_ref, high_ref, low_ref, left_ref, right_ref):
    columns = vol_ref.shape[1]
    half = columns // 2
    voxels = vol_ref[...]
    high = voxels.astype(jnp.bfloat16)
    low = (voxels - high.astype(jnp.float32)).astype(jnp.bfloat16)
    for start in range(0, columns, width):
        first, last = max(0, start - rim), min(columns, start + width + rim)
        top = first - (start - rim)
        rows = slice(top, top + last - first)
        dot = functools.partial(jnp.dot, preferred_element_type=jnp.float32)
        out = dot(high[:, first:last], low_ref[rows, :]) + dot(low[:, first:last], high_ref[rows, :])
        out = out + dot(high[:, first:last], high_ref[rows, :])
        if start < half:
            left_ref[:, start : start + width] = out
        else:
            right_ref[:, start - half : start - half + width] = out


def prefilter(voxels):
    rows, columns = voxels.shape
    width, rim, block = 256, 128, 128
    high, low = filter_parts(width, rim)
    whole = pl.BlockSpec((width + 2 * rim, width), lambda i: (0, 0))
    halves = jax.ShapeDtypeStruct((rows, columns // 2), jnp.float32)
    return pl.pallas_call(
        functools.partial(prefilter_kernel, width, rim),
        grid=(rows // block,),
        in_specs=[pl.BlockSpec((block, columns), lambda i: (i, 0)), whole, whole],
        out_specs=[pl.BlockSpec((block, columns // 2), lambda i: (i, 0))] * 2,
        out_shape=[halves, halves],
        compiler_params=LIMIT,
        name="prefilter",
    )(voxels, jnp.asarray(high), jnp.asarray(low))


def request_kernel(devices, capacity, names_ref, table_ref, place_ref):
    sets, rows = names_ref.shape
    before = lax.broadcasted_iota(jnp.int32, (rows, rows), 0)
    after = lax.broadcasted_iota(jnp.int32, (rows, rows), 1)
    earlier = jnp.where(before < after, 1.0, 0.0).astype(jnp.bfloat16)
    peers = lax.broadcasted_iota(jnp.int32, (devices, rows), 0)
    slots = lax.broadcasted_iota(jnp.int32, (devices * capacity, rows), 0)
    digit = lax.broadcasted_iota(jnp.int32, (8, rows), 0)
    for number in range(sets):
        name = names_ref[number : number + 1, :]
        peer = name // rows
        row = name - peer * rows
        hit = jnp.where(peers == peer, 1.0, 0.0)
        running = jnp.dot(hit.astype(jnp.bfloat16), earlier, preferred_element_type=jnp.float32)
        slot = jnp.sum(hit * running, axis=0, keepdims=True).astype(jnp.int32)
        place = peer * capacity + slot
        place_ref[number : number + 1, :] = place
        taken = jnp.where(slots == place, 1.0, 0.0).astype(jnp.bfloat16)
        digits = jnp.where(digit == 0, row // 16, jnp.where(digit == 1, row % 16, 0))
        found = lax.dot_general(
            digits.astype(jnp.float32).astype(jnp.bfloat16),
            taken,
            (((1,), (1,)), ((), ())),
            preferred_element_type=jnp.float32,
        )
        table_ref[number : number + 1, :] = (16.0 * found[0:1] + found[1:2]).astype(jnp.int32)


def requests(names, devices, capacity):
    sets, rows = names.shape
    return pl.pallas_call(
        functools.partial(request_kernel, devices, capacity),
        in_specs=[VMEM],
        out_specs=[VMEM, VMEM],
        out_shape=[
            jax.ShapeDtypeStruct((sets, devices * capacity), jnp.int32),
            jax.ShapeDtypeStruct((sets, rows), jnp.int32),
        ],
        compiler_params=LIMIT,
        name="requests",
    )(names)


def taylor(coeffs):
    columns = coeffs.shape[1]
    column = lax.broadcasted_iota(jnp.int32, coeffs.shape, 1)
    before = jnp.where(column == 0, 0.0, pltpu.roll(coeffs, 1, 1))
    after = jnp.where(column == columns - 1, 0.0, pltpu.roll(coeffs, columns - 1, 1))
    bend = after - 2.0 * coeffs + before
    return (before + 4.0 * coeffs + after) * (1.0 / 6.0), 0.5 * (after - before), bend


def pair(left_ref, right_ref):
    return jnp.concatenate([left_ref[...], right_ref[...]], axis=1)


def lanes(values):
    rows, columns = values.shape
    total = values[:, 0:128]
    for start in range(128, columns, 128):
        total = total + values[:, start : start + 128]
    return jnp.sum(total.T, axis=0, keepdims=True)


def sums_kernel(sign_ref, near0, near1, far0, far1, vol_ref, out_ref):
    sign = sign_ref[0]
    voxels = vol_ref[...]
    value, slope, bend = taylor(pair(near0, near1))
    other_value, other_slope, other_bend = taylor(pair(far0, far1))
    value = value - voxels
    other_value = other_value - voxels
    slope = sign * slope
    other_slope = -sign * other_slope
    c0 = slope * slope + other_slope * other_slope
    out_ref[0:1, :] = lanes(slope * value + other_slope * other_value)
    out_ref[1:2, :] = lanes(c0 + bend * value + other_bend * other_value)
    out_ref[2:3, :] = lanes(c0)
    out_ref[3:4, :] = lanes(2.0 * (slope * bend + other_slope * other_bend))
    out_ref[4:5, :] = lanes(bend * bend + other_bend * other_bend)


def row_sums(sign, streams, voxels):
    rows, columns = voxels.shape
    block = 128
    half = pl.BlockSpec((block, columns // 2), lambda i: (i, 0))
    return pl.pallas_call(
        sums_kernel,
        grid=(rows // block,),
        in_specs=[SMEM, half, half, half, half, pl.BlockSpec((block, columns), lambda i: (i, 0))],
        out_specs=pl.BlockSpec((SUMS, block), lambda i: (0, i)),
        out_shape=jax.ShapeDtypeStruct((SUMS, rows), jnp.float32),
        compiler_params=LIMIT,
        name="row_sums",
    )(sign, *streams, voxels)


def plane_stencil(field, slabs):
    rows = field.shape[1]
    hops = Y // rows
    slab = lax.broadcasted_iota(jnp.int32, field.shape, 0) % slabs
    row = lax.broadcasted_iota(jnp.int32, field.shape, 1)

    def moved(cells, by):
        kept = slab >= by if by > 0 else slab < slabs + by
        return jnp.where(kept, pltpu.roll(cells, by % cells.shape[0], 0), 0.0)

    low = pltpu.roll(field, 1, 1)
    high = pltpu.roll(field, rows - 1, 1)
    low = jnp.where(row == 0, moved(low, 1), low)
    high = jnp.where(row == rows - 1, moved(high, -1), high)
    return 4.0 * field - low - high - moved(field, hops) - moved(field, -hops)


def final_kernel(slabs, where_ref, sign_ref, fields_ref, near0, near1, far0, far1, vol_ref, velocity_ref, misfit_ref, moved_ref):
    step = pl.program_id(0)
    rows = velocity_ref.shape[1]
    block = vol_ref.shape[0]

    @pl.when(step == 0)
    def _():
        l0, l1, c0, c1, c2, velocity, stiffness = [
            fields_ref[:, i * rows : (i + 1) * rows] for i in range(FIELDS)
        ]
        for _ in range(ITERS):
            linear = l0 + velocity * (l1 + velocity * (0.75 * c1 + velocity * (0.5 * c2)))
            curvature = c0 + velocity * (c1 + velocity * c2)
            gradient = linear + stiffness * plane_stencil(stiffness * velocity, slabs)
            direction = gradient / (curvature + 4.0 * stiffness * stiffness)
            scaled = stiffness * direction
            bent = curvature * direction * direction + scaled * plane_stencil(scaled, slabs)
            upper = jnp.sum(direction * gradient, keepdims=True)
            lower = jnp.sum(bent, keepdims=True)
            velocity = velocity - upper / lower * direction
        device = lax.broadcasted_iota(jnp.int32, velocity.shape, 0)
        own = jnp.sum(jnp.where(device == where_ref[0], velocity, 0.0), axis=0, keepdims=True)
        velocity_ref[...] = own
        for start in range(0, rows, 128):
            moved_ref[start : start + 128, :] = jnp.broadcast_to(own[:, start : start + 128], (128, 128)).T

    moved = moved_ref[pl.ds(pl.multiple_of(step * block, block), block), :]
    moved = jnp.concatenate([moved] * (vol_ref.shape[1] // 128), axis=1)
    near, far = pair(near0, near1), pair(far0, far1)
    value, _, bend = taylor(near + far)
    _, slope, _ = taylor(sign_ref[0] * (near - far))
    misfit_ref[...] = value + moved * (slope + 0.5 * moved * bend) - 2.0 * vol_ref[...]


def finish(where, sign, fields, streams, voxels, slabs):
    rows, columns = voxels.shape
    block = 128
    half = pl.BlockSpec((block, columns // 2), lambda i: (i, 0))
    full = pl.BlockSpec((block, columns), lambda i: (i, 0))
    return pl.pallas_call(
        functools.partial(final_kernel, slabs),
        grid=(rows // block,),
        in_specs=[SMEM, SMEM, pl.BlockSpec(fields.shape, lambda i: (0, 0)), half, half, half, half, full],
        out_specs=[pl.BlockSpec((1, rows), lambda i: (0, 0)), full],
        out_shape=[
            jax.ShapeDtypeStruct((1, rows), jnp.float32),
            jax.ShapeDtypeStruct((rows, columns), jnp.float32),
        ],
        scratch_shapes=[pltpu.VMEM((rows, 128), jnp.float32)],
        compiler_params=LIMIT,
        name="finish",
    )(where, sign, fields, *streams, voxels)


def swapped(block, axis):
    return lax.all_to_all(block, axis, split_axis=0, concat_axis=0, tiled=True)


def on_device(volume, velocity0, fetch_slab, fetch_row, modulus_class, modulus_table):
    voxels = volume[0]
    rows = voxels.shape[0]
    slabs = lax.axis_size("slab")
    scans = lax.axis_size("scan")
    capacity = max(2, 3 * rows // (2 * slabs))
    scan = lax.axis_index("scan")
    inner = (scan == 1) | (scan == 2)
    sign = jnp.where(scan % 2 == 0, 1.0, -1.0).astype(jnp.float32).reshape(1)

    names = fetch_slab[0, :, :, 0] * rows + fetch_row[0]
    partner = lax.ppermute(names[1], "scan", [(1, 0), (2, 1)]) + lax.ppermute(
        names[0], "scan", [(1, 2), (2, 3)]
    )
    own = jnp.where(scan % 2 == 0, names[0], names[1])
    tables, places = requests(jnp.stack([partner, own]), slabs, capacity)
    asked = swapped(tables.reshape(2, slabs, capacity).transpose(1, 0, 2), "slab")
    asked = asked.transpose(1, 0, 2).reshape(2, slabs * capacity)

    left, right = prefilter(voxels)
    near_left = lax.ppermute(left, "scan", [(1, 0), (2, 3)])
    near_right = lax.ppermute(right, "scan", [(1, 0), (2, 3), (0, 1), (3, 2)])

    def fetched(source, wanted, place):
        picked = jnp.take(source, wanted, axis=0).reshape(slabs, capacity, source.shape[1])
        arrived = swapped(picked, "slab").reshape(slabs * capacity, source.shape[1])
        return jnp.take(arrived, place, axis=0)

    first = fetched(left, asked[0], places[0])
    back_left = lax.ppermute(first, "scan", [(0, 1), (1, 2)])
    fore_left = lax.ppermute(first, "scan", [(2, 1), (3, 2)])
    second = fetched(
        jnp.where(inner, right, near_left),
        jnp.where(inner, asked[0], asked[1]),
        jnp.where(inner, places[0], places[1]),
    )
    far_right = lax.ppermute(second, "scan", [(1, 2), (2, 1)])
    third = fetched(near_right, asked[1], places[1])

    near_half = jnp.where(inner, jnp.where(scan == 1, back_left, fore_left), second)
    far_half = jnp.where(scan == 1, fore_left, back_left)
    streams = (near_half, third, far_half, far_right)

    classes = lax.broadcasted_iota(jnp.int32, (modulus_table.shape[0], 1), 0)
    weight = jnp.sum(jnp.where(modulus_class == classes, modulus_table[:, None], 0.0), axis=0)
    stiffness = jnp.sqrt(weight)

    sums = row_sums(sign, streams, voxels)
    payload = jnp.concatenate([sums, velocity0, stiffness[None]], axis=0).reshape(1, FIELDS * rows)
    everywhere = swapped(
        jnp.broadcast_to(payload, (scans * slabs, FIELDS * rows)), ("scan", "slab")
    )
    where = (scan * slabs + lax.axis_index("slab")).astype(jnp.int32).reshape(1)
    velocity, misfit = finish(where, sign, everywhere, streams, voxels, slabs)
    return velocity, misfit[None]


def solution(mesh):
    return jax.shard_map(
        on_device,
        mesh=mesh,
        in_specs=(
            P("scan", "slab", None),
            P("scan", "slab"),
            P("scan", None, "slab", None),
            P("scan", None, "slab"),
            P("scan", "slab"),
            P(),
        ),
        out_specs=(P("scan", "slab"), P("scan", "slab", None)),
        check_vma=False,
    )
```

time: 451 us -> 227 us (0.50)
  blocking collectives: 133 us -> 0 us
  waiting for transfers between devices: 159 us -> 101 us
  other arithmetic: 38.7 us -> 15.5 us
  local copies, waits for them, and re-layouts: 49.2 us -> 30.2 us
  matrix products: 16.1 us -> 0 us
  Pallas kernels: 0 us -> 15.6 us
  starting transfers between devices: 49.2 us -> 62.6 us
    psum x2 -> x0, blocking collectives: 122 us -> none  [on_device(): lax.psum((jnp.sum(direction * gradient), jnp.sum(curvature * direction *...]
    all_to_all x1 -> x5, waiting for transfers between devices: 124 us -> 24.2 us  [swapped(): return lax.all_to_all(block, axis, split_axis=0, concat_axis=0, tiled=True)]
    ppermute x18 -> x7, waiting for transfers between devices: 34.9 us -> 77 us  [the longest x1 26.7 us: on_device(): near_left = lax.ppermute(left, 'scan', [(1, 0), (2, 3)])]
    all_to_all x1 -> x5, starting transfers between devices: 5.58 us -> 47.6 us  [swapped(): return lax.all_to_all(block, axis, split_axis=0, concat_axis=0, tiled=True)]
    ppermute x18 -> x7, starting transfers between devices: 43.6 us -> 15 us  [the longest x1 5.48 us: on_device(): back_left = lax.ppermute(first, 'scan', [(0, 1), (1, 2)])]
    reduce_sum x6 -> x1, other arithmetic: 17.1 us -> 0.08 us  [on_device(): jnp.sum(jnp.where(modulus_class == classes, modulus_table[:, None], 0.0),...]
    dot_general x8 -> x0, matrix products: 16.1 us -> none  [prefilter(): jnp.dot(window, matrix, preferred_element_type=jnp.float32, precision=lax...]
    pallas_call x0 -> x4, Pallas kernels: none -> 15.6 us  [the longest x1 6.2 us: finish(): pl.pallas_call(functools.partial(final_kernel, slabs), grid=(rows // bloc...]
  transfers between devices with their start and end apart: 19 -> 12, of which waited for: 5 -> 7; matrix products, arithmetic and copies ran while one was open for 15% -> 12% of each run, Pallas kernels for 0% -> 1%
where the time goes in v1:
time: 227 us; the launch traced here: 226 us
  waiting for transfers between devices  101 us (44%)
  starting transfers between devices  62.6 us (28%)
  local copies, waits for them, and re-layouts  30.2 us (13%)
  Pallas kernels  15.6 us (7%)
  other arithmetic  15.5 us (7%)
    all_to_all x5, starting transfers between devices, swapped(): return lax.all_to_all(block, axis, split_axis=0, concat_axis=0, tiled=True)  47.6 us
    ppermute x1, waiting for transfers between devices, on_device(): near_left = lax.ppermute(left, 'scan', [(1, 0), (2, 3)])  26.7 us
    all_to_all x5, waiting for transfers between devices, swapped(): return lax.all_to_all(block, axis, split_axis=0, concat_axis=0, tiled=True)  24.2 us
    ppermute x1, waiting for transfers between devices, on_device(): near_right = lax.ppermute(right, 'scan', [(1, 0), (2, 3), (0, 1), (3, 2)])  23.6 us
    ppermute x1, waiting for transfers between devices, on_device(): back_left = lax.ppermute(first, 'scan', [(0, 1), (1, 2)])  18.9 us
    unnamed x23, local copies, waits for them, and re-layouts  9.81 us
    gather x3, local copies, waits for them, and re-layouts, fetched(): jnp.take(source, wanted, axis=0).reshape(slabs, capacity, source.shape[1])  9.31 us
    gather x3, local copies, waits for them, and re-layouts, fetched(): return jnp.take(arrived, place, axis=0)  9.19 us
  transfers between devices with their start and end apart: 12, of which 7 were waited for; matrix products, arithmetic and copies ran while one was open for 12% of the time, Pallas kernels for 1%

profile of v1, /device:TPU:0, one launch (start us, length us, event | category | flops | bytes accessed | tf_op | source)
XLA Modules:
  0.0 225.9 jit_solution(17512415712083484505)
XLA Ops:
  0.6 0.7 bitcast_add_fusion
  1.4 0.7 collective-permute-start.1
  2.0 1.3 collective-permute-start
  3.3 0.0 collective-permute-done.1
  3.3 7.8 %collective-permute-done = s32[512]{0:T(512)S(1)} collective-permute-done((s32[512]{0:T(512)S(1)}, s32[512]{0:T(512)S(1)}, u32[]{:S(2)}, u32[]{:S(2)}) %collective-permute-start) | collective-permute-done | bytes 2080 | tf_op jit(solution)/shard_map/ppermute | solution.py:251
  11.2 1.0 requests.1
  12.2 0.1 reshape.68
  12.3 0.6 copy.22
  12.9 4.9 %all-to-all-start = ((s32[8,2,96]{2,1,0:T(2,128)}), s32[8,2,96]{2,1,0:T(2,128)S(1)}, u32[]{:S(2)}, u32[]{:S(2)}) async-start(s32[8,2,96]{2,1,0:T(2,128)} %bitcast.27), calls=%async_computation | async-start | bytes 16384 | tf_op jit(solution)/shard_map/all_to_all | solution.py:237
  17.8 0.0 copy-start
  17.8 1.6 copy-done
  19.4 0.0 copy-start.6
  19.4 0.9 copy-done.6
  20.3 0.0 copy-start.7
  20.3 0.9 copy-done.7
  21.3 2.3 %prefilter.1 = (f32[512,512]{1,0:T(8,128)S(1)}, f32[512,512]{1,0:T(8,128)S(1)}) custom-call(f32[512,1024]{1,0:T(8,128)S(1)} %bitcast.28, bf16[512,256]{1,0:T(8,128)(2,1)S(1)} %copy-done.7, bf16[512,256]{1,0:T(8,128)(2,1)S(1)} %copy-done.6), custom_call_target="tpu_custom_call" | custom-call | tf_op jit(solution)/shard_map/prefilter/pallas_call | solution.py:58
  23.6 0.0 all-to-all-done
  23.7 0.1 squeeze.37
  23.7 0.1 squeeze.35
  23.8 3.1 %gather_fusion = f32[768,512]{1,0:T(8,128)} fusion(f32[512,512]{1,0:T(8,128)S(1)} %get-tuple-element.10, s32[1024]{0:T(1024)S(1)} %pad_clamp_fusion.5), kind=kCustom, calls=%fused_computation.clone | custom fusion | bytes 3148800 | tf_op jit(solution)/shard_map/jit(_take)/gather | solution.py:264
  26.9 2.7 %broadcast_select_fusion.2 = f32[768,512]{1,0:T(8,128)} fusion(f32[768,512]{1,0:T(8,128)} %gather_fusion, pred[768]{0:T(1024)(128)(4,1)S(1)} %get-tuple-element.26), kind=kLoop, calls=%fused_computation.9 | loop fusion | flops 393216 | bytes 3146496 | tf_op jit(solution)/shard_map/jit(_take)/select_n | solution.py:264
  29.7 5.1 %all-to-all-start.1 = ((f32[8,96,512]{2,1,0:T(8,128)}), f32[8,96,512]{2,1,0:T(8,128)}, u32[]{:S(2)}, u32[]{:S(2)}) async-start(f32[8,96,512]{2,1,0:T(8,128)} %bitcast.33), calls=%async_computation.1 | async-start | bytes 3145728 | tf_op jit(solution)/shard_map/all_to_all | solution.py:237
  34.8 1.3 collective-permute-start.4
  36.1 26.7 %collective-permute-done.4 = f32[512,512]{1,0:T(8,128)S(1)} collective-permute-done((f32[512,512]{1,0:T(8,128)S(1)}, f32[512,512]{1,0:T(8,128)S(1)}, u32[]{:S(2)}, u32[]{:S(2)}) %collective-permute-start.4) | collective-permute-done | bytes 1048608 | tf_op jit(solution)/shard_map/ppermute | solution.py:260
  62.8 0.2 broadcast_select_fusion.7
  63.0 3.1 %gather_fusion.2 = f32[768,512]{1,0:T(8,128)} fusion(f32[512,512]{1,0:T(8,128)S(1)} %broadcast_select_fusion.7, s32[1024]{0:T(1024)S(1)} %pad_clamp_fusion.3), kind=kCustom, calls=%fused_computation.2.clone | custom fusion | bytes 3148800 | tf_op jit(solution)/shard_map/jit(_take)/gather | solution.py:264
  66.1 2.7 %broadcast_select_fusion.1 = f32[768,512]{1,0:T(8,128)} fusion(f32[768,512]{1,0:T(8,128)} %gather_fusion.2, pred[768]{0:T(1024)(128)(4,1)S(1)} %get-tuple-element.22), kind=kLoop, calls=%fused_computation.8 | loop fusion | flops 393216 | bytes 3146496 | tf_op jit(solution)/shard_map/jit(_take)/select_n | solution.py:264
  68.8 3.9 %all-to-all-done.1 = f32[8,96,512]{2,1,0:T(8,128)} async-done(((f32[8,96,512]{2,1,0:T(8,128)}), f32[8,96,512]{2,1,0:T(8,128)}, u32[]{:S(2)}, u32[]{:S(2)}) %all-to-all-start.1) | async-done | bytes 1572896 | tf_op jit(solution)/shard_map/all_to_all | solution.py:237
  72.7 4.3 %all-to-all-start.2 = ((f32[8,96,512]{2,1,0:T(8,128)}), f32[8,96,512]{2,1,0:T(8,128)}, u32[]{:S(2)}, u32[]{:S(2)}) async-start(f32[8,96,512]{2,1,0:T(8,128)} %bitcast.14), calls=%async_computation.2 | async-start | bytes 3145728 | tf_op jit(solution)/shard_map/all_to_all | solution.py:237
  77.0 3.0 %collective-permute-start.5 = (f32[512,512]{1,0:T(8,128)S(1)}, f32[512,512]{1,0:T(8,128)S(1)}, u32[]{:S(2)}, u32[]{:S(2)}) collective-permute-start(f32[512,512]{1,0:T(8,128)S(1)} %get-tuple-element.13), channel_id=1, source_target_pairs={{8,0},{16,24},{0,8},{24,16},{9,1},{17,25},{1,9},{25,17},{10,2},{18... | collective-permute-start | bytes 3145736 | tf_op jit(solution)/shard_map/ppermute | solution.py:261
  80.1 23.6 %collective-permute-done.5 = f32[512,512]{1,0:T(8,128)S(1)} collective-permute-done((f32[512,512]{1,0:T(8,128)S(1)}, f32[512,512]{1,0:T(8,128)S(1)}, u32[]{:S(2)}, u32[]{:S(2)}) %collective-permute-start.5) | collective-permute-done | bytes 1048608 | tf_op jit(solution)/shard_map/ppermute | solution.py:261
  103.7 3.1 %gather_fusion.4 = f32[768,512]{1,0:T(8,128)} fusion(f32[512,512]{1,0:T(8,128)S(1)} %collective-permute-done.5, s32[1024]{0:T(1024)S(1)} %pad_clamp_fusion.1), kind=kCustom, calls=%fused_computation.3.clone | custom fusion | bytes 3148800 | tf_op jit(solution)/shard_map/jit(_take)/gather | solution.py:264
  106.8 2.7 %broadcast_select_fusion = f32[768,512]{1,0:T(8,128)} fusion(f32[768,512]{1,0:T(8,128)} %gather_fusion.4, pred[768]{0:T(1024)(128)(4,1)S(1)} %get-tuple-element.25), kind=kLoop, calls=%fused_computation.7 | loop fusion | flops 393216 | bytes 3146496 | tf_op jit(solution)/shard_map/jit(_take)/select_n | solution.py:264
  109.5 5.4 %all-to-all-done.2 = f32[8,96,512]{2,1,0:T(8,128)} async-done(((f32[8,96,512]{2,1,0:T(8,128)}), f32[8,96,512]{2,1,0:T(8,128)}, u32[]{:S(2)}, u32[]{:S(2)}) %all-to-all-start.2) | async-done | bytes 1572896 | tf_op jit(solution)/shard_map/all_to_all | solution.py:237
  114.9 3.6 %all-to-all-start.3 = ((f32[8,96,512]{2,1,0:T(8,128)}), f32[8,96,512]{2,1,0:T(8,128)S(1)}, u32[]{:S(2)}, u32[]{:S(2)}) async-start(f32[8,96,512]{2,1,0:T(8,128)} %bitcast.16), calls=%async_computation.3 | async-start | bytes 3145728 | tf_op jit(solution)/shard_map/all_to_all | solution.py:237
  118.5 3.4 %gather_fusion.1 = f32[512,512]{1,0:T(8,128)S(1)} fusion(f32[768,512]{1,0:T(8,128)} %bitcast.12, s32[1024]{0:T(1024)S(1)} %pad_clamp_fusion.4), kind=kCustom, calls=%fused_computation.1.clone | custom fusion | bytes 2099200 | tf_op jit(solution)/shard_map/jit(_take)/gather | solution.py:266
  121.9 1.2 broadcast_select_fusion.5
  123.1 1.6 collective-permute-start.3
  124.7 5.5 %collective-permute-start.2 = (f32[512,512]{1,0:T(8,128)}, f32[512,512]{1,0:T(8,128)}, u32[]{:S(2)}, u32[]{:S(2)}) collective-permute-start(f32[512,512]{1,0:T(8,128)} %broadcast_select_fusion.5), channel_id=1, source_target_pairs={{0,8},{8,16},{1,9},{9,17},{2,10},{10,18},{3,11},{11,19},{4,12},{12... | collective-permute-start | bytes 3145736 | tf_op jit(solution)/shard_map/ppermute | solution.py:269
  130.2 3.4 %gather_fusion.3 = f32[512,512]{1,0:T(8,128)S(1)} fusion(f32[768,512]{1,0:T(8,128)} %bitcast.15, s32[1024]{0:T(1024)S(1)} %pad_clamp_fusion.2), kind=kCustom, calls=%fused_computation.4.clone | custom fusion | bytes 2099200 | tf_op jit(solution)/shard_map/jit(_take)/gather | solution.py:266
  133.6 0.0 collective-permute-done.3
  133.7 18.9 %collective-permute-done.2 = f32[512,512]{1,0:T(8,128)} collective-permute-done((f32[512,512]{1,0:T(8,128)}, f32[512,512]{1,0:T(8,128)}, u32[]{:S(2)}, u32[]{:S(2)}) %collective-permute-start.2) | collective-permute-done | bytes 1048608 | tf_op jit(solution)/shard_map/ppermute | solution.py:269
  152.5 3.5 %select_select_fusion = (f32[512,512]{1,0:T(8,128)}, f32[512,512]{1,0:T(8,128)}, f32[512,512]{1,0:T(8,128)}) fusion(f32[512,512]{1,0:T(8,128)} %collective-permute-done.2, f32[512,512]{1,0:T(8,128)} %collective-permute-done.3, pred[]{:T(512)S(6)} %eq.31, pred[]{:T(512)S(6)} %or.3, f32[512,512]{1,0:T(8,128)S(1)} %gather_fusion.3, ...), kind=kLoop, calls=%fused_computation.6 | loop fusion | flops 1048576 | bytes 6291970 | tf_op jit(solution)/shard_map/jit(_where)/select_n | solution.py:279
  156.0 1.6 collective-permute-start.6
  157.7 0.0 copy-done.9
  157.7 0.0 copy-done.10
  157.7 0.1 select_reduce_fusion
  157.8 0.0 all-to-all-done.3
  157.8 2.3 %gather_fusion.5 = f32[512,512]{1,0:T(8,128)} fusion(f32[768,512]{1,0:T(8,128)S(1)} %bitcast.32, s32[1024]{0:T(1024)S(1)} %pad_clamp_fusion), kind=kCustom, calls=%fused_computation.5.clone | custom fusion | bytes 2099200 | tf_op jit(solution)/shard_map/jit(_take)/gather | solution.py:266
  160.1 1.5 broadcast_select_fusion.3.near1
  161.6 0.0 collective-permute-done.6.far1
  161.7 0.4 copy-done.1
  162.0 1.2 copy-done.2
  163.3 1.2 copy-done.4
  164.5 6.0 %row_sums.1 = f32[5,512]{1,0:T(8,128)S(1)} custom-call(f32[1]{0:T(128)} %bitcast.1.sign_ref, f32[512,512]{1,0:T(8,128)S(1)} %copy-done.2, f32[512,512]{1,0:T(8,128)S(1)} %broadcast_select_fusion.3.near1, f32[512,512]{1,0:T(8,128)S(1)} %copy-done.4, f32[512,512]{1,0:T(8,128)} %collective-permute-done.6.far1, f32[512,1024]{1,0:T(8,128)S(1)} %bitcast.29), custom_call_target="tpu_custom_call" | custom-call | tf_op jit(solution)/shard_map/row_sums/pallas_call | solution.py:154
  170.5 0.0 copy-done.8
  170.6 1.0 broadcast_in_dim.45
  171.6 29.7 %all-to-all-start.4 = ((f32[32,1,3584]{2,1,0:T(1,128)}), f32[32,1,3584]{2,1,0:T(1,128)}, u32[]{:S(2)}, u32[]{:S(2)}) async-start(f32[32,1,3584]{2,1,0:T(1,128)} %broadcast_in_dim.45), calls=%async_computation.4 | async-start | bytes 917504 | tf_op jit(solution)/shard_map/all_to_all | solution.py:237
  201.3 14.9 %all-to-all-done.4 = f32[32,1,3584]{2,1,0:T(1,128)} async-done(((f32[32,1,3584]{2,1,0:T(1,128)}), f32[32,1,3584]{2,1,0:T(1,128)}, u32[]{:S(2)}, u32[]{:S(2)}) %all-to-all-start.4) | async-done | bytes 458784 | tf_op jit(solution)/shard_map/all_to_all | solution.py:237
  216.2 1.0 copy.21
  217.3 0.0 copy-start.3
  217.3 1.2 copy-done.3
  218.5 1.2 copy-done.5
  219.7 6.2 %finish.1 = (f32[1,512]{1,0:T(1,128)}, f32[512,1024]{1,0:T(8,128)}) custom-call(s32[1]{0:T(128)} %bitcast.where_ref, f32[1]{0:T(128)} %bitcast.1.sign_ref, f32[32,3584]{1,0:T(8,128)S(1)} %bitcast.31, f32[512,512]{1,0:T(8,128)S(1)} %copy-done.3, f32[512,512]{1,0:T(8,128)S(1)} %broadcast_select_fusion.3.near1, f32[512,512]{1,0:T(8,128)S(1)} %copy-done.5, ...), custom_call_target="tpu_custom_call" | custom-call | tf_op jit(solution)/shard_map/finish/pallas_call | solution.py:221
  (27 shorter events, 0.2 us)
Async XLA Ops:
  1.4 2.0 collective-permute-start.1
  2.0 9.1 %collective-permute-start = (s32[512]{0:T(512)S(1)}, s32[512]{0:T(512)S(1)}, u32[]{:S(2)}, u32[]{:S(2)}) collective-permute-start(s32[512]{0:T(512)S(1)} %bitcast.42), channel_id=1, source_target_pairs={{8,0},{16,8},{9,1},{17,9},{10,2},{18,10},{11,3},{19,11},{12,4},{20... | collective-permute-start | bytes 6152 | tf_op jit(solution)/shard_map/ppermute | solution.py:251
  12.9 10.7 %all-to-all-start = ((s32[8,2,96]{2,1,0:T(2,128)}), s32[8,2,96]{2,1,0:T(2,128)S(1)}, u32[]{:S(2)}, u32[]{:S(2)}) async-start(s32[8,2,96]{2,1,0:T(2,128)} %bitcast.27), calls=%async_computation | async-start | bytes 16384 | tf_op jit(solution)/shard_map/all_to_all | solution.py:237
  17.8 1.6 copy-start
  19.4 0.9 copy-start.6
  20.3 0.9 copy-start.7
  29.7 43.0 %all-to-all-start.1 = ((f32[8,96,512]{2,1,0:T(8,128)}), f32[8,96,512]{2,1,0:T(8,128)}, u32[]{:S(2)}, u32[]{:S(2)}) async-start(f32[8,96,512]{2,1,0:T(8,128)} %bitcast.33), calls=%async_computation.1 | async-start | bytes 3145728 | tf_op jit(solution)/shard_map/all_to_all | solution.py:237
  34.8 28.0 %collective-permute-start.4 = (f32[512,512]{1,0:T(8,128)S(1)}, f32[512,512]{1,0:T(8,128)S(1)}, u32[]{:S(2)}, u32[]{:S(2)}) collective-permute-start(f32[512,512]{1,0:T(8,128)S(1)} %get-tuple-element.10), channel_id=1, source_target_pairs={{8,0},{16,24},{9,1},{17,25},{10,2},{18,26},{11,3},{19,27},{12,4},{... | collective-permute-start | bytes 3145736 | tf_op jit(solution)/shard_map/ppermute | solution.py:260
  72.7 42.2 %all-to-all-start.2 = ((f32[8,96,512]{2,1,0:T(8,128)}), f32[8,96,512]{2,1,0:T(8,128)}, u32[]{:S(2)}, u32[]{:S(2)}) async-start(f32[8,96,512]{2,1,0:T(8,128)} %bitcast.14), calls=%async_computation.2 | async-start | bytes 3145728 | tf_op jit(solution)/shard_map/all_to_all | solution.py:237
  77.0 26.6 %collective-permute-start.5 = (f32[512,512]{1,0:T(8,128)S(1)}, f32[512,512]{1,0:T(8,128)S(1)}, u32[]{:S(2)}, u32[]{:S(2)}) collective-permute-start(f32[512,512]{1,0:T(8,128)S(1)} %get-tuple-element.13), channel_id=1, source_target_pairs={{8,0},{16,24},{0,8},{24,16},{9,1},{17,25},{1,9},{25,17},{10,2},{18... | collective-permute-start | bytes 3145736 | tf_op jit(solution)/shard_map/ppermute | solution.py:261
  114.9 42.9 %all-to-all-start.3 = ((f32[8,96,512]{2,1,0:T(8,128)}), f32[8,96,512]{2,1,0:T(8,128)S(1)}, u32[]{:S(2)}, u32[]{:S(2)}) async-start(f32[8,96,512]{2,1,0:T(8,128)} %bitcast.16), calls=%async_computation.3 | async-start | bytes 3145728 | tf_op jit(solution)/shard_map/all_to_all | solution.py:237
  123.1 10.6 %collective-permute-start.3 = (f32[512,512]{1,0:T(8,128)}, f32[512,512]{1,0:T(8,128)}, u32[]{:S(2)}, u32[]{:S(2)}) collective-permute-start(f32[512,512]{1,0:T(8,128)} %broadcast_select_fusion.5), channel_id=1, source_target_pairs={{16,8},{24,16},{17,9},{25,17},{18,10},{26,18},{19,11},{27,19},{20,... | collective-permute-start | bytes 3145736 | tf_op jit(solution)/shard_map/ppermute | solution.py:270
  124.7 27.8 %collective-permute-start.2 = (f32[512,512]{1,0:T(8,128)}, f32[512,512]{1,0:T(8,128)}, u32[]{:S(2)}, u32[]{:S(2)}) collective-permute-start(f32[512,512]{1,0:T(8,128)} %broadcast_select_fusion.5), channel_id=1, source_target_pairs={{0,8},{8,16},{1,9},{9,17},{2,10},{10,18},{3,11},{11,19},{4,12},{12... | collective-permute-start | bytes 3145736 | tf_op jit(solution)/shard_map/ppermute | solution.py:269
  152.5 5.1 %copy-start.9 = (s32[1,512]{1,0:T(1,128)S(1)}, s32[1,512]{1,0:T(1,128)}, u32[]{:S(2)}) copy-start(s32[1,512]{1,0:T(1,128)} %param.16) | copy-start | bytes 6148
  152.5 5.1 %copy-start.10 = (f32[4]{0:T(128)S(1)}, f32[4]{0:T(128)}, u32[]{:S(2)}) copy-start(f32[4]{0:T(128)} %param.17) | copy-start | bytes 52
  156.0 5.6 %collective-permute-start.6 = (f32[512,512]{1,0:T(8,128)}, f32[512,512]{1,0:T(8,128)}, u32[]{:S(2)}, u32[]{:S(2)}) collective-permute-start(f32[512,512]{1,0:T(8,128)} %get-tuple-element.19), channel_id=1, source_target_pairs={{8,16},{16,8},{9,17},{17,9},{10,18},{18,10},{11,19},{19,11},{12,20... | collective-permute-start | bytes 3145736 | tf_op jit(solution)/shard_map/ppermute | solution.py:276
  160.1 1.9 copy-start.1
  162.0 1.2 copy-start.2
  163.3 1.2 copy-start.4
  164.5 6.1 %copy-start.8 = (f32[1,512]{1,0:T(1,128)S(1)}, f32[1,512]{1,0:T(1,128)}, u32[]{:S(2)}) copy-start(f32[1,512]{1,0:T(1,128)} %param.13) | copy-start | bytes 6148
  171.6 44.7 %all-to-all-start.4 = ((f32[32,1,3584]{2,1,0:T(1,128)}), f32[32,1,3584]{2,1,0:T(1,128)}, u32[]{:S(2)}, u32[]{:S(2)}) async-start(f32[32,1,3584]{2,1,0:T(1,128)} %broadcast_in_dim.45), calls=%async_computation.4 | async-start | bytes 917504 | tf_op jit(solution)/shard_map/all_to_all | solution.py:237
  217.3 1.2 copy-start.3
  218.5 1.2 copy-start.5

commit v2 on v1

v2 whole, which is shorter than its diff:
```python
import functools
import math

import jax
import jax.numpy as jnp
from jax import lax
from jax.experimental import pallas as pl
from jax.experimental.pallas import tpu as pltpu
from jax.sharding import PartitionSpec as P

Y = 1024
BAND = 32
ITERS = 2
FIELDS = 8
HINT = 16
VMEM = pl.BlockSpec(memory_space=pltpu.VMEM)
SMEM = pl.BlockSpec(memory_space=pltpu.SMEM)
LIMIT = pltpu.CompilerParams(vmem_limit_bytes=16 * 1024 * 1024)


def cost(flops, values):
    return pl.CostEstimate(flops=flops, bytes_accessed=4 * values, transcendentals=0)


def store_filter(rim, high_ref, low_ref):
    shape = high_ref.shape
    distance = jnp.abs(lax.broadcasted_iota(jnp.int32, shape, 0) - rim - lax.broadcasted_iota(jnp.int32, shape, 1))
    parity = 1.0 - 2.0 * (distance % 2).astype(jnp.float32)
    size = jnp.exp(distance.astype(jnp.float32) * math.log(2.0 - math.sqrt(3.0)))
    exact = jnp.where(distance <= BAND, math.sqrt(3.0) * parity * size, 0.0)
    high = exact.astype(jnp.bfloat16)
    high_ref[...] = high
    low_ref[...] = (exact - high.astype(jnp.float32)).astype(jnp.bfloat16)


def prefilter_kernel(width, rim, vol_ref, early_ref, left_ref, right_ref, high_ref, low_ref):
    columns = vol_ref.shape[1]
    half = columns // 2

    @pl.when(pl.program_id(0) == 0)
    def _():
        store_filter(rim, high_ref, low_ref)

    voxels = vol_ref[...]
    high = voxels.astype(jnp.bfloat16)
    low = (voxels - high.astype(jnp.float32)).astype(jnp.bfloat16)
    for start in range(0, columns, width):
        first, last = max(0, start - rim), min(columns, start + width + rim)
        top = first - (start - rim)
        rows = slice(top, top + last - first)
        dot = functools.partial(jnp.dot, preferred_element_type=jnp.float32)
        out = dot(high[:, first:last], low_ref[rows, :]) + dot(low[:, first:last], high_ref[rows, :])
        out = out + dot(high[:, first:last], high_ref[rows, :])
        if start < half:
            left_ref[:, start : start + width] = out
        else:
            right_ref[:, start - half : start - half + width] = out


def prefilter(voxels, early):
    rows, columns = voxels.shape
    width, rim, block = 256, 128, 256
    halves = jax.ShapeDtypeStruct((rows, columns // 2), jnp.float32)
    matrix = pltpu.VMEM((width + 2 * rim, width), jnp.bfloat16)
    return pl.pallas_call(
        functools.partial(prefilter_kernel, width, rim),
        grid=(rows // block,),
        in_specs=[pl.BlockSpec((block, columns), lambda i: (i, 0)), pl.BlockSpec(memory_space=pl.ANY)],
        out_specs=[pl.BlockSpec((block, columns // 2), lambda i: (i, 0))] * 2,
        out_shape=[halves, halves],
        scratch_shapes=[matrix, matrix],
        cost_estimate=cost(3 * 2 * rows * columns * (width + 2 * rim), 2 * rows * columns),
        compiler_params=LIMIT,
        name="prefilter",
    )(voxels, early)


def column(line):
    parts = [
        jnp.broadcast_to(line[:, start : start + 128], (128, 128)).T for start in range(0, line.shape[1], 128)
    ]
    return parts[0] if len(parts) == 1 else jnp.concatenate(parts, axis=0)


def request_kernel(devices, capacity, direct, at_ref, inner_ref, side_ref, inward_ref, own_ref, table_ref, place_ref):
    rows = own_ref.shape[1]
    before = lax.broadcasted_iota(jnp.int32, (rows, rows), 0)
    after = lax.broadcasted_iota(jnp.int32, (rows, rows), 1)
    earlier = jnp.where(before < after, 1.0, 0.0).astype(jnp.bfloat16)
    peers = lax.broadcasted_iota(jnp.int32, (devices, rows), 0)
    core = at_ref[0] % 2
    slots = lax.broadcasted_iota(jnp.int32, (128, rows), 0)
    against = (((1,), (1,)), ((), ()))
    side = side_ref[...]
    for number, name in enumerate((side, jnp.where(inner_ref[0] != 0, inward_ref[...], side), own_ref[...])):
        peer = name // rows
        row = name - peer * rows
        if direct:
            peer = 2 * (peer // 2) + (peer + core) % 2
        hit = jnp.where(peers == peer, 1.0, 0.0)
        running = jnp.dot(hit.astype(jnp.bfloat16), earlier, preferred_element_type=jnp.float32)
        slot = jnp.sum(hit * running, axis=0, keepdims=True).astype(jnp.int32)
        if direct:
            peer = peer % 2 + 2 * ((at_ref[0] // 2 - peer // 2 + devices // 2) % (devices // 2))
        place_ref[number] = column(peer * capacity + slot)
        taken = jnp.where(slots == slot, 1.0, 0.0).astype(jnp.bfloat16)
        upper = (hit * (row // 16).astype(jnp.float32)).astype(jnp.bfloat16)
        lower = (hit * (row % 16).astype(jnp.float32)).astype(jnp.bfloat16)
        found = 16.0 * lax.dot_general(upper, taken, against, preferred_element_type=jnp.float32)
        found = found + lax.dot_general(lower, taken, against, preferred_element_type=jnp.float32)
        table_ref[:, 128 * number : 128 * number + 128] = found.astype(jnp.int32)


def requests(at, inner, partners, own, devices, capacity, direct):
    rows = own.shape[1]
    return pl.pallas_call(
        functools.partial(request_kernel, devices, capacity, direct),
        in_specs=[SMEM, SMEM, VMEM, VMEM, VMEM],
        out_specs=[VMEM, VMEM],
        out_shape=[
            jax.ShapeDtypeStruct((devices, 3 * 128), jnp.int32),
            jax.ShapeDtypeStruct((3, rows, 128), jnp.int32),
        ],
        compiler_params=LIMIT,
        name="requests",
    )(at, inner, *partners, own)


def terms(values):
    high = values.astype(jnp.bfloat16)
    rest = values - high.astype(jnp.float32)
    middle = rest.astype(jnp.bfloat16)
    low = (rest - middle.astype(jnp.float32)).astype(jnp.bfloat16)
    return high, middle, low


def picked(chosen, parts):
    dot = functools.partial(jnp.dot, preferred_element_type=jnp.float32)
    return (dot(chosen, parts[2]) + dot(chosen, parts[1])) + dot(chosen, parts[0])


def pick_kernel(chips, capacity, number, inner_ref, at_ref, asked_ref, *refs):
    sources, outs, chosen_ref = refs[: -1 - chips], refs[-1 - chips : -1], refs[-1]
    rows = sources[0].shape[0]
    row = lax.broadcasted_iota(jnp.int32, (128, rows), 1)
    for core in range(2):
        for turn in range(chips):
            line = asked_ref[pl.ds(2 * ((at_ref[0] // 2 + turn) % chips) + core, 1), :]
            line = line[:, 128 * number : 128 * number + 128]
            wanted = jnp.concatenate([column(line)] * (rows // 128), axis=1)
            hit = jnp.where(wanted == row, 1.0, 0.0)[:capacity]
            chosen_ref[turn * capacity : (turn + 1) * capacity, :] = hit.astype(jnp.bfloat16)
        source = sources[core][...]
        if len(sources) > 2:
            source = jnp.where(inner_ref[0] != 0, source, sources[2 + core][...])
        rows_out = picked(chosen_ref[...], terms(source))
        for turn in range(chips):
            outs[turn][core * capacity : (core + 1) * capacity, :] = rows_out[
                turn * capacity : (turn + 1) * capacity
            ]


def pick(inner, at, asked, number, sources, chips, capacity):
    rows, width = sources[0].shape
    block = jax.ShapeDtypeStruct((2 * capacity, width), jnp.float32)
    return pl.pallas_call(
        functools.partial(pick_kernel, chips, capacity, number),
        in_specs=[SMEM, SMEM] + [VMEM] * (1 + len(sources)),
        out_specs=[VMEM] * chips,
        out_shape=[block] * chips,
        scratch_shapes=[pltpu.VMEM((chips * capacity, rows), jnp.bfloat16)],
        cost_estimate=cost(HINT * 12 * chips * capacity * rows * width, 5 * rows * width),
        compiler_params=LIMIT,
        name="pick",
    )(inner, at, asked, *sources)


def store_terms(blocks, terms_ref):
    start = 0
    for block in blocks:
        for number, part in enumerate(terms(block[...])):
            terms_ref[number, start : start + block.shape[0], :] = part
        start += block.shape[0]


def placed(place, terms_ref):
    count = terms_ref.shape[1]
    lane = lax.broadcasted_iota(jnp.int32, place.shape, 1)
    chosen = [jnp.where(place - start == lane, 1.0, 0.0) for start in range(0, count, 128)]
    chosen = jnp.concatenate(chosen, axis=1).astype(jnp.bfloat16)
    return picked(chosen, [terms_ref[number] for number in range(3)])


def place_kernel(place_ref, *refs):
    blocks, out_ref, terms_ref = refs[:-2], refs[-2], refs[-1]

    @pl.when(pl.program_id(0) == 0)
    def _():
        store_terms(blocks, terms_ref)

    out_ref[...] = placed(place_ref[0], terms_ref)


def place(number, places, blocks):
    rows = places.shape[1]
    width = blocks[0].shape[1]
    total = sum(block.shape[0] for block in blocks)
    step = 256
    whole = [pl.BlockSpec(block.shape, lambda i: (0, 0)) for block in blocks]
    return pl.pallas_call(
        place_kernel,
        grid=(rows // step,),
        in_specs=[pl.BlockSpec((1, step, 128), lambda i: (number, i, 0))] + whole,
        out_specs=pl.BlockSpec((step, width), lambda i: (i, 0)),
        out_shape=jax.ShapeDtypeStruct((rows, width), jnp.float32),
        scratch_shapes=[pltpu.VMEM((3, total, width), jnp.bfloat16)],
        cost_estimate=cost(HINT * 3 * 2 * total * rows * width, 3 * rows * width),
        compiler_params=LIMIT,
        name="place",
    )(places, *blocks)


def taylor(coeffs):
    columns = coeffs.shape[1]
    lane = lax.broadcasted_iota(jnp.int32, coeffs.shape, 1)
    before = jnp.where(lane == 0, 0.0, pltpu.roll(coeffs, 1, 1))
    after = jnp.where(lane == columns - 1, 0.0, pltpu.roll(coeffs, columns - 1, 1))
    bend = after - 2.0 * coeffs + before
    return (before + 4.0 * coeffs + after) * (1.0 / 6.0), 0.5 * (after - before), bend


def lanes(values):
    rows, columns = values.shape
    total = values[:, 0:128]
    for start in range(128, columns, 128):
        total = total + values[:, start : start + 128]
    sums = [jnp.sum(total[start : start + 128].T, axis=0, keepdims=True) for start in range(0, rows, 128)]
    return jnp.concatenate(sums, axis=1)


def row_sums(sign, near, far, voxels, counted):
    kept = [jnp.where(counted, part, 0.0) for part in (*taylor(near), *taylor(far), voxels)]
    value, slope, bend, other_value, other_slope, other_bend, voxels = kept
    value = value - voxels
    other_value = other_value - voxels
    slope = sign * slope
    other_slope = -sign * other_slope
    c0 = slope * slope + other_slope * other_slope
    return (
        lanes(slope * value + other_slope * other_value),
        lanes(c0 + bend * value + other_bend * other_value),
        lanes(c0),
        lanes(2.0 * (slope * bend + other_slope * other_bend)),
        lanes(bend * bend + other_bend * other_bend),
    )


def left_sums_kernel(sign_ref, table_ref, near_ref, far_ref, vol_ref, start_ref, class_ref, out_ref):
    counted = lax.broadcasted_iota(jnp.int32, near_ref.shape, 1) < near_ref.shape[1] - 1
    lines = row_sums(sign_ref[0], near_ref[...], far_ref[...], vol_ref[...], counted)
    for number, line in enumerate(lines):
        out_ref[number : number + 1, :] = line
    weight = jnp.zeros(start_ref.shape, jnp.float32)
    for kind in range(table_ref.shape[0]):
        weight = jnp.where(class_ref[...] == kind, table_ref[kind], weight)
    out_ref[5:6, :] = start_ref[...]
    out_ref[6:7, :] = jnp.sqrt(weight)
    out_ref[7:8, :] = jnp.zeros(start_ref.shape, jnp.float32)


def left_sums(sign, table, near, far, voxels, start, classes):
    rows, half = near.shape
    step = 256
    block = pl.BlockSpec((step, half), lambda i: (i, 0))
    line = pl.BlockSpec((1, step), lambda i: (0, i))
    return pl.pallas_call(
        left_sums_kernel,
        grid=(rows // step,),
        in_specs=[SMEM, SMEM, block, block, block, line, line],
        out_specs=pl.BlockSpec((FIELDS, step), lambda i: (0, i)),
        out_shape=jax.ShapeDtypeStruct((FIELDS, rows), jnp.float32),
        cost_estimate=cost(60 * rows * half, 6 * rows * half),
        compiler_params=LIMIT,
        name="left_sums",
    )(sign, table, near, far, voxels, start, classes)


def right_sums_kernel(
    inner_ref, sign_ref, place_ref, near_rim, far_rim, vol_rim, hop_ref, vol_ref, so_far_ref, *refs
):
    blocks, fields_ref, third_ref, terms_ref = refs[:-3], refs[-3], refs[-2], refs[-1]

    @pl.when(pl.program_id(0) == 0)
    def _():
        store_terms(blocks, terms_ref)

    third = placed(place_ref[0], terms_ref)
    third_ref[...] = third
    inner = inner_ref[0] != 0
    near = jnp.concatenate([near_rim[...], jnp.where(inner, hop_ref[...], third)], axis=1)
    far = jnp.concatenate([far_rim[...], jnp.where(inner, third, 0.0)], axis=1)
    voxels = jnp.concatenate([vol_rim[...], vol_ref[...]], axis=1)
    counted = lax.broadcasted_iota(jnp.int32, far.shape, 1) >= 127
    for number, line in enumerate(row_sums(sign_ref[0], near, far, voxels, counted)):
        fields_ref[number : number + 1, :] = so_far_ref[number : number + 1, :] + line
    fields_ref[5:8, :] = so_far_ref[5:8, :]


def right_sums(inner, sign, places, near, far, voxels, hop, so_far, blocks):
    rows, half = near.shape
    step = 256
    total = sum(block.shape[0] for block in blocks)
    rim = pl.BlockSpec((step, 128), lambda i: (i, half // 128 - 1))
    block = pl.BlockSpec((step, half), lambda i: (i, 0))
    whole = [pl.BlockSpec(part.shape, lambda i: (0, 0)) for part in blocks]
    fields = pl.BlockSpec((FIELDS, step), lambda i: (0, i))
    return pl.pallas_call(
        right_sums_kernel,
        grid=(rows // step,),
        in_specs=[
            SMEM,
            SMEM,
            pl.BlockSpec((1, step, 128), lambda i: (2, i, 0)),
            rim,
            rim,
            rim,
            block,
            pl.BlockSpec((step, half), lambda i: (i, 1)),
            fields,
            *whole,
        ],
        out_specs=[fields, block],
        out_shape=[
            jax.ShapeDtypeStruct((FIELDS, rows), jnp.float32),
            jax.ShapeDtypeStruct((rows, half), jnp.float32),
        ],
        scratch_shapes=[pltpu.VMEM((3, total, half), jnp.bfloat16)],
        cost_estimate=cost(3 * 2 * total * rows * half, 5 * rows * half),
        compiler_params=LIMIT,
        name="right_sums",
    )(inner, sign, places, near, far, voxels, hop, voxels, so_far, *blocks)


def plane_stencil(field):
    slabs, rows = field.shape
    hops = Y // rows
    slab = lax.broadcasted_iota(jnp.int32, field.shape, 0)
    row = lax.broadcasted_iota(jnp.int32, field.shape, 1)

    def moved(cells, by):
        kept = slab >= by if by > 0 else slab < slabs + by
        return jnp.where(kept, pltpu.roll(cells, by % slabs, 0), 0.0)

    low = pltpu.roll(field, 1, 1)
    high = pltpu.roll(field, rows - 1, 1)
    low = jnp.where(row == 0, moved(low, 1), low)
    high = jnp.where(row == rows - 1, moved(high, -1), high)
    return 4.0 * field - low - high - moved(field, hops) - moved(field, -hops)


def total(parts):
    return jnp.sum(functools.reduce(jnp.add, parts), keepdims=True)


def iterate(groups):
    velocities = [group[5] for group in groups]
    for _ in range(ITERS):
        uppers, lowers, directions = [], [], []
        for (l0, l1, c0, c1, c2, _, stiffness, _), velocity in zip(groups, velocities):
            linear = l0 + velocity * (l1 + velocity * (0.75 * c1 + velocity * (0.5 * c2)))
            curvature = c0 + velocity * (c1 + velocity * c2)
            gradient = linear + stiffness * plane_stencil(stiffness * velocity)
            direction = gradient / (curvature + 4.0 * stiffness * stiffness)
            scaled = stiffness * direction
            uppers.append(direction * gradient)
            lowers.append(curvature * direction * direction + scaled * plane_stencil(scaled))
            directions.append(direction)
        alpha = total(uppers) / total(lowers)
        velocities = [velocity - alpha * direction for velocity, direction in zip(velocities, directions)]
    return velocities[0]


def final_kernel(scans, at_ref, inner_ref, sign_ref, *refs):
    fields_refs = refs[:scans]
    near0, far0, hop, third, vol_ref, velocity_ref, misfit_ref, moved_ref = refs[scans:]
    step = pl.program_id(0)
    rows = velocity_ref.shape[1]
    block = vol_ref.shape[0]

    @pl.when(step == 0)
    def _():
        groups = [[ref[:, i, :] for i in range(FIELDS)] for ref in fields_refs]
        velocity = iterate(groups)
        slab = lax.broadcasted_iota(jnp.int32, velocity.shape, 0)
        own = jnp.sum(jnp.where(slab == at_ref[0], velocity, 0.0), axis=0, keepdims=True)
        velocity_ref[...] = own
        moved_ref[...] = column(own)

    moved = moved_ref[pl.ds(pl.multiple_of(step * block, block), block), :]
    moved = jnp.concatenate([moved] * (vol_ref.shape[1] // 128), axis=1)
    inner = inner_ref[0] != 0
    near = jnp.concatenate([near0[...], jnp.where(inner, hop[...], third[...])], axis=1)
    far = jnp.concatenate([far0[...], jnp.where(inner, third[...], 0.0)], axis=1)
    value, _, bend = taylor(near + far)
    _, slope, _ = taylor(sign_ref[0] * (near - far))
    misfit_ref[...] = value + moved * (slope + 0.5 * moved * bend) - 2.0 * vol_ref[...]


def finish(at, inner, sign, groups, streams, voxels):
    rows, columns = voxels.shape
    step = 256
    half = pl.BlockSpec((step, columns // 2), lambda i: (i, 0))
    full = pl.BlockSpec((step, columns), lambda i: (i, 0))
    whole = [pl.BlockSpec(group.shape, lambda i: (0, 0, 0)) for group in groups]
    return pl.pallas_call(
        functools.partial(final_kernel, len(groups)),
        grid=(rows // step,),
        in_specs=[SMEM, SMEM, SMEM, *whole, half, half, half, half, full],
        out_specs=[pl.BlockSpec((1, rows), lambda i: (0, 0)), full],
        out_shape=[
            jax.ShapeDtypeStruct((1, rows), jnp.float32),
            jax.ShapeDtypeStruct((rows, columns), jnp.float32),
        ],
        scratch_shapes=[pltpu.VMEM((rows, 128), jnp.float32)],
        compiler_params=LIMIT,
        name="finish",
    )(at, inner, sign, *groups, *streams, voxels)


def swapped(block, axis):
    return lax.all_to_all(block, axis, split_axis=0, concat_axis=0, tiled=True)


def after(block, *earlier):
    return lax.optimization_barrier((block, *earlier))[0]


ORDER = (2, 1, 3)


def on_device(volume, velocity0, fetch_slab, fetch_row, modulus_class, modulus_table):
    voxels = volume[0]
    rows = voxels.shape[0]
    slabs = lax.axis_size("slab")
    scans = lax.axis_size("scan")
    capacity = max(2, 3 * rows // (2 * slabs))
    direct = slabs == 8
    scan = lax.axis_index("scan")
    slab = lax.axis_index("slab")
    at = slab.astype(jnp.int32).reshape(1)
    inner = ((scan == 1) | (scan == 2)).astype(jnp.int32).reshape(1)
    sign = jnp.where(scan % 2 == 0, 1.0, -1.0).astype(jnp.float32).reshape(1)
    sides = [(0, 1), (1, 0), (2, 3), (3, 2)]
    middle = [(1, 2), (2, 1)]

    names = fetch_slab[0, :, :, 0] * rows + fetch_row[0]
    lent = jnp.where(scan % 2 == 0, names[0:1], names[1:2])
    own = jnp.where(scan < 2, names[0:1], names[1:2])
    partners = [lax.ppermute(lent, "scan", sides), lax.ppermute(own, "scan", middle)]
    table, places = requests(at, inner, partners, own, slabs, capacity, direct)
    chips = slabs // 2
    if direct:
        same_core = [list(range(core, slabs, 2)) for core in range(2)]
        asked = lax.all_to_all(table, "slab", 0, 0, axis_index_groups=same_core, tiled=True)
    else:
        asked = swapped(table, "slab")

    def other_core(block):
        return lax.ppermute(block, "slab", [(p, p ^ 1) for p in range(slabs)]) if direct else block

    left, right = prefilter(voxels, names)
    left, right, _ = lax.optimization_barrier((left, right, table))
    left_other, right_other = other_core(left), other_core(right)
    from_inner = lax.ppermute(right, "scan", [(1, 0), (2, 3)])
    from_middle = lax.ppermute(right, "scan", middle)

    def picks(number, sources):
        if direct:
            return pick(inner, at, asked, number, sources, chips, capacity)
        source = sources[0] if len(sources) == 2 else jnp.where(inner[0] != 0, sources[0], sources[2])
        wanted = asked[:, 128 * number : 128 * number + capacity]
        return [jnp.take(source, wanted.reshape(-1), axis=0)]

    sent = []

    def fetched(blocks):
        if not direct:
            arrived = swapped(blocks[0].reshape(slabs, capacity, -1), "slab")
            return [arrived.reshape(slabs * capacity, -1)]
        arrived = [blocks[0]] + [None] * (chips - 1)
        for turn in ORDER:
            held = sent[-3:-2]
            block = after(blocks[turn], *held) if held else blocks[turn]
            route = [(p, (p + 2 * turn) % slabs) for p in range(slabs)]
            arrived[turn] = lax.ppermute(block, "slab", route)
            sent.append(arrived[turn])
        return arrived

    arrived = fetched(picks(0, [left, left_other]))
    first = place(0, places, arrived)
    lender = jnp.where(inner == 1, after(from_middle, *arrived), from_inner)
    near = lax.ppermute(first, "scan", sides)
    arrived = fetched(picks(1, [left, left_other, right, right_other]))
    blocks = picks(2, [lender, other_core(lender)])
    second = place(1, places, [after(arrived[0], blocks[0]), *arrived[1:]])
    hop = lax.ppermute(second, "scan", [(0, 1), (3, 2)])
    far = lax.ppermute(second, "scan", middle)
    arrived = fetched(blocks)
    so_far = left_sums(sign, modulus_table, near, far, voxels, velocity0, modulus_class)
    sums, third = right_sums(inner, sign, places, near, far, voxels, hop, so_far, arrived)

    column_sums = swapped(jnp.broadcast_to(sums[None], (slabs, FIELDS, rows)), "slab")
    groups = [column_sums]
    for turn in range(1, scans):
        groups.append(lax.ppermute(column_sums, "scan", [(p, (p + turn) % scans) for p in range(scans)]))
    velocity, misfit = finish(
        at, inner, sign, groups, (near, far, hop, third), after(voxels, sums)
    )
    return velocity, misfit[None]


def solution(mesh):
    return jax.shard_map(
        on_device,
        mesh=mesh,
        in_specs=(
            P("scan", "slab", None),
            P("scan", "slab"),
            P("scan", None, "slab", None),
            P("scan", None, "slab"),
            P("scan", "slab"),
            P(),
        ),
        out_specs=(P("scan", "slab"), P("scan", "slab", None)),
        check_vma=False,
    )
```

time: 227 us -> 176 us (0.78)
  local copies, waits for them, and re-layouts: 30.2 us -> 2.34 us
  starting transfers between devices: 62.6 us -> 37.5 us
  Pallas kernels: 15.6 us -> 32.6 us
  other arithmetic: 15.5 us -> 2.15 us
  waiting for transfers between devices: 101 us -> 90.6 us
  blocking collectives: 0 us -> 9.17 us
    all_to_all x5 -> x1, starting transfers between devices: 47.6 us -> 4.87 us  [on_device(): lax.all_to_all(table, 'slab', 0, 0, axis_index_groups=same_core, tiled=True)]
    all_to_all x5 -> x1, waiting for transfers between devices: 24.2 us -> 2.54 us  [on_device(): lax.all_to_all(table, 'slab', 0, 0, axis_index_groups=same_core, tiled=True)]
    gather x6 -> x0, local copies, waits for them, and re-layouts: 18.5 us -> none  [the longest x3 9.31 us: fetched(): jnp.take(source, wanted, axis=0).reshape(slabs, capacity, source.shape[1])]
    ppermute x7 -> x22, starting transfers between devices: 15 us -> 32.6 us  [the longest x9 11.6 us: fetched(): arrived[turn] = lax.ppermute(block, 'slab', route)]
    pallas_call x3 -> x9, Pallas kernels: 13.3 us -> 30.2 us  [the longest x3 8.35 us: pick(): pl.pallas_call(functools.partial(pick_kernel, chips, capacity, number), i...]
    select_n x11 -> x2, other arithmetic: 14.6 us -> 1.44 us  [the longest x1 1.44 us: on_device(): lender = jnp.where(inner == 1, after(from_middle, *arrived), from_inner)]
    ppermute x7 -> x22, waiting for transfers between devices: 77 us -> 88.1 us  [the longest x9 76.4 us: fetched(): arrived[turn] = lax.ppermute(block, 'slab', route)]
    all_to_all x0 -> x1, blocking collectives: none -> 9.17 us  [swapped(): return lax.all_to_all(block, axis, split_axis=0, concat_axis=0, tiled=True)]
  transfers between devices with their start and end apart: 12 -> 23, of which waited for: 7 -> 10; matrix products, arithmetic and copies ran while one was open for 12% -> 1% of each run, Pallas kernels for 1% -> 11%
where the time goes in v2:
time: 176 us; the launch traced here: 175 us
  waiting for transfers between devices  90.6 us (51%)
  starting transfers between devices  37.5 us (21%)
  Pallas kernels  32.6 us (19%)
  blocking collectives  9.17 us (5%)
  local copies, waits for them, and re-layouts  2.34 us (1%)
  other arithmetic  2.15 us (1%)
    ppermute x9, waiting for transfers between devices, fetched(): arrived[turn] = lax.ppermute(block, 'slab', route)  76.4 us
    ppermute x9, starting transfers between devices, fetched(): arrived[turn] = lax.ppermute(block, 'slab', route)  11.6 us
    all_to_all x1, blocking collectives, swapped(): return lax.all_to_all(block, axis, split_axis=0, concat_axis=0, tiled=True)  9.17 us
    pallas_call x3, Pallas kernels, pick(): pl.pallas_call(functools.partial(pick_kernel, chips, capacity, number), i...  8.35 us
    ppermute x1, waiting for transfers between devices, on_device(): from_inner = lax.ppermute(right, 'scan', [(1, 0), (2, 3)])  6.86 us
    pallas_call x1, Pallas kernels, finish(): pl.pallas_call(functools.partial(final_kernel, len(groups)), grid=(rows /...  6.32 us
    pallas_call x1, Pallas kernels, right_sums(): pl.pallas_call(right_sums_kernel, grid=(rows // step,), in_specs=[SMEM, S...  6.06 us
    ppermute x1, starting transfers between devices, on_device(): hop = lax.ppermute(second, 'scan', [(0, 1), (3, 2)])  5.32 us
  transfers between devices with their start and end apart: 23, of which 10 were waited for; matrix products, arithmetic and copies ran while one was open for 1% of the time, Pallas kernels for 11%

profile of v2, /device:TPU:0, one launch (start us, length us, event | category | flops | bytes accessed | tf_op | source)
XLA Modules:
  0.0 175.2 jit_solution(13943566054556914506)
XLA Ops:
  0.6 0.7 bitcast_add_fusion.early_ref
  1.4 3.0 %collective-permute-start = (s32[1,512]{1,0:T(1,128)S(1)}, s32[1,512]{1,0:T(1,128)S(1)}, u32[]{:S(2)}, u32[]{:S(2)}) collective-permute-start(s32[1,512]{1,0:T(1,128)S(1)} %get-tuple-element.65), channel_id=1, source_target_pairs={{0,8},{8,0},{16,24},{24,16},{1,9},{9,1},{17,25},{25,17},{2,10},{10... | collective-permute-start | bytes 6152 | tf_op jit(solution)/shard_map/ppermute | solution.py:459
  4.4 0.6 collective-permute-start.1
  5.0 0.0 copy-start
  5.0 1.6 copy-done
  6.6 2.3 %prefilter.1 = (f32[512,512]{1,0:T(8,128)S(1)}, f32[512,512]{1,0:T(8,128)S(1)}) custom-call(f32[512,1024]{1,0:T(8,128)S(1)} %bitcast.10, s32[2,512]{1,0:T(2,128)S(1)} %bitcast_add_fusion.early_ref), custom_call_target="tpu_custom_call" | custom-call | flops 1610612736 | bytes 4194304 | tf_op jit(solution)/shard_map/prefilter/pallas_call | solution.py:65
  9.0 0.0 collective-permute-done.side_ref
  9.0 0.0 collective-permute-done.1.inward_ref
  9.0 0.9 requests.1
  9.9 0.1 collective-permute-start.2
  9.9 0.7 all_to_all.10
  10.6 4.9 %all-to-all-start = ((s32[4,2,384]{2,1,0:T(2,128)}), s32[4,2,384]{2,1,0:T(2,128)S(1)}, u32[]{:S(2)}, u32[]{:S(2)}) async-start(s32[4,2,384]{2,1,0:T(2,128)} %all_to_all.10), calls=%async_computation | async-start | bytes 24576 | tf_op jit(solution)/shard_map/all_to_all | solution.py:464
  15.5 0.1 collective-permute-start.7
  15.6 1.6 collective-permute-start.8
  17.3 1.3 collective-permute-start.9
  18.6 2.5 %all-to-all-done = s32[4,2,384]{2,1,0:T(2,128)S(1)} async-done(((s32[4,2,384]{2,1,0:T(2,128)}), s32[4,2,384]{2,1,0:T(2,128)S(1)}, u32[]{:S(2)}, u32[]{:S(2)}) %all-to-all-start) | async-done | bytes 12320 | tf_op jit(solution)/shard_map/all_to_all | solution.py:464
  21.1 0.0 collective-permute-done.2.refs_1_
  21.1 2.7 %pick.3 = (f32[192,512]{1,0:T(8,128)S(1)}, f32[192,512]{1,0:T(8,128)S(1)}, f32[192,512]{1,0:T(8,128)S(1)}, f32[192,512]{1,0:T(8,128)S(1)}) custom-call(s32[1]{0:T(128)} %bitcast.1.inner_ref, s32[1]{0:T(128)} %bitcast.at_ref, s32[8,384]{1,0:T(8,128)S(1)} %all_to_all.12.asked_ref, f32[512,512]{1,0:T(8,128)S(1)} %get-tuple-element.37.refs_0_, ...), custom_call_target="tpu_custom_call" | custom-call | flops 19327352832 | bytes 5242880 | tf_op jit(solution)/shard_map/pick/pallas_call | solution.py:166
  23.9 1.2 collective-permute-start.5
  25.1 0.9 collective-permute-start.3
  26.0 0.0 collective-permute-done.7.refs_3_
  26.0 0.6 collective-permute-start.4
  26.6 3.1 %pick.4 = (f32[192,512]{1,0:T(8,128)S(1)}, f32[192,512]{1,0:T(8,128)S(1)}, f32[192,512]{1,0:T(8,128)S(1)}, f32[192,512]{1,0:T(8,128)S(1)}) custom-call(s32[1]{0:T(128)} %bitcast.1.inner_ref, s32[1]{0:T(128)} %bitcast.at_ref, s32[8,384]{1,0:T(8,128)S(1)} %all_to_all.12.asked_ref, f32[512,512]{1,0:T(8,128)S(1)} %get-tuple-element.37.refs_0_, ...), custom_call_target="tpu_custom_call" | custom-call | flops 19327352832 | bytes 5242880 | tf_op jit(solution)/shard_map/pick/pallas_call | solution.py:166
  29.7 13.5 %collective-permute-done.5.refs_3_ = f32[192,512]{1,0:T(8,128)S(1)} collective-permute-done((f32[192,512]{1,0:T(8,128)S(1)}, f32[192,512]{1,0:T(8,128)S(1)}, u32[]{:S(2)}, u32[]{:S(2)}) %collective-permute-start.5) | collective-permute-done | bytes 393248 | tf_op jit(solution)/shard_map/ppermute | solution.py:495
  43.1 0.0 collective-permute-start.13
  43.1 0.0 collective-permute-done.8
  43.1 1.3 collective-permute-done.3.refs_1_
  44.5 16.9 %collective-permute-done.4.refs_2_ = f32[192,512]{1,0:T(8,128)S(1)} collective-permute-done((f32[192,512]{1,0:T(8,128)S(1)}, f32[192,512]{1,0:T(8,128)S(1)}, u32[]{:S(2)}, u32[]{:S(2)}) %collective-permute-start.4) | collective-permute-done | bytes 393248 | tf_op jit(solution)/shard_map/ppermute | solution.py:495
  61.4 6.9 %collective-permute-done.9 = f32[512,512]{1,0:T(8,128)} collective-permute-done((f32[512,512]{1,0:T(8,128)S(1)}, f32[512,512]{1,0:T(8,128)}, u32[]{:S(2)}, u32[]{:S(2)}) %collective-permute-start.9) | collective-permute-done | bytes 1048608 | tf_op jit(solution)/shard_map/ppermute | solution.py:474
  68.2 1.4 broadcast_select_fusion.refs_0_
  69.7 0.1 collective-permute-start.10
  69.8 3.0 %collective-permute-start.12 = (f32[192,512]{1,0:T(8,128)S(1)}, f32[192,512]{1,0:T(8,128)S(1)}, u32[]{:S(2)}, u32[]{:S(2)}) collective-permute-start(f32[192,512]{1,0:T(8,128)S(1)} %get-tuple-element.50), channel_id=1, source_target_pairs={{0,4},{1,5},{2,6},{3,7},{4,0},{5,1},{6,2},{7,3},{8,12},{9,13},{10,... | collective-permute-start | bytes 1179656 | tf_op jit(solution)/shard_map/ppermute | solution.py:495
  72.7 1.5 collective-permute-start.11
  74.2 2.0 %place.2 = f32[512,512]{1,0:T(8,128)S(1)} custom-call(s32[3,512,128]{2,1,0:T(8,128)S(1)} %get-tuple-element.33.place_ref, f32[192,512]{1,0:T(8,128)S(1)} %get-tuple-element.38.refs_0_, f32[192,512]{1,0:T(8,128)S(1)} %collective-permute-done.3.refs_1_, f32[192,512]{1,0:T(8,128)S(1)} %collective-permute-done.4.refs_2_, ...), custom_call_target="tpu_custom_call" | custom-call | flops 19327352832 | bytes 3145728 | tf_op jit(solution)/shard_map/place/pallas_call | solution.py:210
  76.2 4.3 %collective-permute-start.6 = (f32[512,512]{1,0:T(8,128)S(1)}, f32[512,512]{1,0:T(8,128)S(1)}, u32[]{:S(2)}, u32[]{:S(2)}) collective-permute-start(f32[512,512]{1,0:T(8,128)S(1)} %place.2), channel_id=1, source_target_pairs={{0,8},{8,0},{16,24},{24,16},{1,9},{9,1},{17,25},{25,17},{2,10},{10... | collective-permute-start | bytes 3145736 | tf_op jit(solution)/shard_map/ppermute | solution.py:502
  80.6 0.0 collective-permute-done.10.refs_1_
  80.6 2.5 %pick.5 = (f32[192,512]{1,0:T(8,128)S(1)}, f32[192,512]{1,0:T(8,128)}, f32[192,512]{1,0:T(8,128)}, f32[192,512]{1,0:T(8,128)}) custom-call(s32[1]{0:T(128)} %bitcast.1.inner_ref, s32[1]{0:T(128)} %bitcast.at_ref, s32[8,384]{1,0:T(8,128)S(1)} %all_to_all.12.asked_ref, f32[512,512]{1,0:T(8,128)S(1)} %broadcast_select_fusion.refs_0_, ...), custom_call_target="tpu_custom_call" | custom-call | flops 19327352832 | bytes 5242880 | tf_op jit(solution)/shard_map/pick/pallas_call | solution.py:166
  83.1 0.0 collective-permute-done.13.refs_3_
  83.1 16.2 %collective-permute-done.12.refs_2_ = f32[192,512]{1,0:T(8,128)S(1)} collective-permute-done((f32[192,512]{1,0:T(8,128)S(1)}, f32[192,512]{1,0:T(8,128)S(1)}, u32[]{:S(2)}, u32[]{:S(2)}) %collective-permute-start.12) | collective-permute-done | bytes 393248 | tf_op jit(solution)/shard_map/ppermute | solution.py:495
  99.3 0.0 collective-permute-done.11.refs_1_
  99.3 2.8 %place.3 = f32[512,512]{1,0:T(8,128)} custom-call(s32[3,512,128]{2,1,0:T(8,128)S(1)} %copy-done.3, f32[192,512]{1,0:T(8,128)S(1)} %get-tuple-element.46.refs_0_, f32[192,512]{1,0:T(8,128)S(1)} %collective-permute-done.11.refs_1_, f32[192,512]{1,0:T(8,128)S(1)} %collective-permute-done.12.refs_2_, f32[192,512]{1,0:T(8,128)S(1)} %collective-permute-done.13.refs_3_), custom_call_target="tpu_custom_call" | custom-call | flops 19327352832 | bytes 3145728 | tf_op jit(solution)/shard_map/place/pallas_call | solution.py:210
  102.1 1.6 collective-permute-start.14
  103.7 5.3 %collective-permute-start.15 = (f32[512,512]{1,0:T(8,128)}, f32[512,512]{1,0:T(8,128)}, u32[]{:S(2)}, u32[]{:S(2)}) collective-permute-start(f32[512,512]{1,0:T(8,128)} %place.3), channel_id=1, source_target_pairs={{0,8},{24,16},{1,9},{25,17},{2,10},{26,18},{3,11},{27,19},{4,12},{... | collective-permute-start | bytes 3145736 | tf_op jit(solution)/shard_map/ppermute | solution.py:506
  109.1 0.0 collective-permute-start.18
  109.1 2.4 %collective-permute-start.17 = (f32[192,512]{1,0:T(8,128)}, f32[192,512]{1,0:T(8,128)}, u32[]{:S(2)}, u32[]{:S(2)}) collective-permute-start(f32[192,512]{1,0:T(8,128)} %get-tuple-element.56), channel_id=1, source_target_pairs={{0,4},{1,5},{2,6},{3,7},{4,0},{5,1},{6,2},{7,3},{8,12},{9,13},{10,... | collective-permute-start | bytes 1179656 | tf_op jit(solution)/shard_map/ppermute | solution.py:495
  111.5 0.0 collective-permute-done.6.near_ref.near_rim.refs_4_
  111.5 2.0 %collective-permute-start.16 = (f32[192,512]{1,0:T(8,128)}, f32[192,512]{1,0:T(8,128)}, u32[]{:S(2)}, u32[]{:S(2)}) collective-permute-start(f32[192,512]{1,0:T(8,128)} %get-tuple-element.54), channel_id=1, source_target_pairs={{0,2},{1,3},{2,4},{3,5},{4,6},{5,7},{6,0},{7,1},{8,10},{9,11},{10,... | collective-permute-start | bytes 1179656 | tf_op jit(solution)/shard_map/ppermute | solution.py:495
  113.5 0.0 collective-permute-done.14.far_ref.far_rim.refs_5_
  113.5 0.0 copy-done.5
  113.5 0.0 copy-done.6
  113.6 3.9 %left_sums.1.so_far_ref = f32[8,512]{1,0:T(8,128)S(1)} custom-call(f32[1]{0:T(128)} %bitcast.2.sign_ref, f32[4]{0:T(128)S(1)} %copy-done.7, f32[512,512]{1,0:T(8,128)S(1)} %collective-permute-done.6.near_ref.near_rim.refs_4_, f32[512,512]{1,0:T(8,128)} %collective-permute-done.14.far_ref.far_rim.refs_5_, f32[512,1024]{1,0:T(8,128)S(1)} %bitcast.11, ...), custom_call_target="tpu_custom_call" | custom-call | flops 15728640 | bytes 6291456 | tf_op jit(solution)/shard_map/left_sums/pallas_call | solution.py:276
  117.4 2.7 %collective-permute-done.18.refs_3_ = f32[192,512]{1,0:T(8,128)} collective-permute-done((f32[192,512]{1,0:T(8,128)}, f32[192,512]{1,0:T(8,128)}, u32[]{:S(2)}, u32[]{:S(2)}) %collective-permute-start.18) | collective-permute-done | bytes 393248 | tf_op jit(solution)/shard_map/ppermute | solution.py:495
  120.1 25.8 %collective-permute-done.17.refs_2_ = f32[192,512]{1,0:T(8,128)} collective-permute-done((f32[192,512]{1,0:T(8,128)}, f32[192,512]{1,0:T(8,128)}, u32[]{:S(2)}, u32[]{:S(2)}) %collective-permute-start.17) | collective-permute-done | bytes 393248 | tf_op jit(solution)/shard_map/ppermute | solution.py:495
  145.9 0.0 collective-permute-done.16.refs_1_
  145.9 0.0 collective-permute-done.15.hop_ref.refs_6_
  145.9 6.1 %right_sums.1 = (f32[8,512]{1,0:T(8,128)S(1)}, f32[512,512]{1,0:T(8,128)S(1)}) custom-call(s32[1]{0:T(128)} %bitcast.1.inner_ref, f32[1]{0:T(128)} %bitcast.2.sign_ref, s32[3,512,128]{2,1,0:T(8,128)S(1)} %copy-done.4, f32[512,512]{1,0:T(8,128)S(1)} %collective-permute-done.6.near_ref.near_rim.refs_4_, ...), custom_call_target="tpu_custom_call" | custom-call | flops 1207959552 | bytes 5242880 | tf_op jit(solution)/shard_map/right_sums/pallas_call | solution.py:317
  152.0 9.2 %all_to_all.16.refs_0_ = f32[8,8,512]{2,1,0:T(8,128)S(1)} all-to-all(f32[8,8,512]{2,1,0:T(8,128)S(1)} %broadcast_in_dim.18), channel_id=1, replica_groups=mesh['scan'=4,'slab'=8] {'slab'}, dimensions={0} | all-to-all | bytes 262144 | tf_op jit(solution)/shard_map/all_to_all | solution.py:431
  161.1 0.0 collective-permute-start.19
  161.1 1.1 collective-permute-start.20
  162.2 1.9 %collective-permute-start.21 = (f32[8,8,512]{2,1,0:T(8,128)S(1)}, f32[8,8,512]{2,1,0:T(8,128)S(1)}, u32[]{:S(2)}, u32[]{:S(2)}) collective-permute-start(f32[8,8,512]{2,1,0:T(8,128)S(1)} %all_to_all.16.refs_0_), channel_id=1, source_target_pairs={{0,24},{8,0},{16,8},{24,16},{1,25},{9,1},{17,9},{25,17},{2,26},{10... | collective-permute-start | bytes 393224 | tf_op jit(solution)/shard_map/ppermute | solution.py:515
  164.1 4.4 %collective-permute-done.19.refs_1_ = f32[8,8,512]{2,1,0:T(8,128)S(1)} collective-permute-done((f32[8,8,512]{2,1,0:T(8,128)S(1)}, f32[8,8,512]{2,1,0:T(8,128)S(1)}, u32[]{:S(2)}, u32[]{:S(2)}) %collective-permute-start.19) | collective-permute-done | bytes 131104 | tf_op jit(solution)/shard_map/ppermute | solution.py:515
  168.4 0.5 collective-permute-done.20.refs_2_
  168.9 0.0 collective-permute-done.21.refs_3_
  168.9 6.3 %finish.1 = (f32[1,512]{1,0:T(1,128)}, f32[512,1024]{1,0:T(8,128)}) custom-call(s32[1]{0:T(128)} %bitcast.at_ref, s32[1]{0:T(128)} %bitcast.1.inner_ref, f32[1]{0:T(128)} %bitcast.2.sign_ref, f32[8,8,512]{2,1,0:T(8,128)S(1)} %all_to_all.16.refs_0_, f32[8,8,512]{2,1,0:T(8,128)S(1)} %collective-permute-done.19.refs_1_, ...), custom_call_target="tpu_custom_call" | custom-call | tf_op jit(solution)/shard_map/finish/pallas_call | solution.py:415
  (15 shorter events, 0.1 us)
Async XLA Ops:
  1.4 7.6 %collective-permute-start = (s32[1,512]{1,0:T(1,128)S(1)}, s32[1,512]{1,0:T(1,128)S(1)}, u32[]{:S(2)}, u32[]{:S(2)}) collective-permute-start(s32[1,512]{1,0:T(1,128)S(1)} %get-tuple-element.65), channel_id=1, source_target_pairs={{0,8},{8,0},{16,24},{24,16},{1,9},{9,1},{17,25},{25,17},{2,10},{10... | collective-permute-start | bytes 6152 | tf_op jit(solution)/shard_map/ppermute | solution.py:459
  4.4 4.6 %collective-permute-start.1 = (s32[1,512]{1,0:T(1,128)S(1)}, s32[1,512]{1,0:T(1,128)S(1)}, u32[]{:S(2)}, u32[]{:S(2)}) collective-permute-start(s32[1,512]{1,0:T(1,128)S(1)} %get-tuple-element.64.own_ref), channel_id=1, source_target_pairs={{8,16},{16,8},{9,17},{17,9},{10,18},{18,10},{11,19},{19,11},{12,20... | collective-permute-start | bytes 6152 | tf_op jit(solution)/shard_map/ppermute | solution.py:459
  5.0 1.6 copy-start
  9.9 64.4 %copy-start.2 = (s32[3,512,128]{2,1,0:T(8,128)}, s32[3,512,128]{2,1,0:T(8,128)S(1)}, u32[]{:S(2)}) copy-start(s32[3,512,128]{2,1,0:T(8,128)S(1)} %get-tuple-element.33.place_ref) | copy-start | bytes 2359300
  9.9 11.3 %collective-permute-start.2 = (f32[512,512]{1,0:T(8,128)S(1)}, f32[512,512]{1,0:T(8,128)}, u32[]{:S(2)}, u32[]{:S(2)}) collective-permute-start(f32[512,512]{1,0:T(8,128)S(1)} %get-tuple-element.37.refs_0_), channel_id=1, source_target_pairs={{0,1},{1,0},{2,3},{3,2},{4,5},{5,4},{6,7},{7,6},{8,9},{9,8},{10,11... | collective-permute-start | bytes 3145736 | tf_op jit(solution)/shard_map/ppermute | solution.py:469
  10.6 10.5 %all-to-all-start = ((s32[4,2,384]{2,1,0:T(2,128)}), s32[4,2,384]{2,1,0:T(2,128)S(1)}, u32[]{:S(2)}, u32[]{:S(2)}) async-start(s32[4,2,384]{2,1,0:T(2,128)} %all_to_all.10), calls=%async_computation | async-start | bytes 24576 | tf_op jit(solution)/shard_map/all_to_all | solution.py:464
  15.5 10.5 %collective-permute-start.7 = (f32[512,512]{1,0:T(8,128)S(1)}, f32[512,512]{1,0:T(8,128)}, u32[]{:S(2)}, u32[]{:S(2)}) collective-permute-start(f32[512,512]{1,0:T(8,128)S(1)} %get-tuple-element.42.refs_2_), channel_id=1, source_target_pairs={{0,1},{1,0},{2,3},{3,2},{4,5},{5,4},{6,7},{7,6},{8,9},{9,8},{10,11... | collective-permute-start | bytes 3145736 | tf_op jit(solution)/shard_map/ppermute | solution.py:469
  15.6 27.5 %collective-permute-start.8 = (f32[512,512]{1,0:T(8,128)S(1)}, f32[512,512]{1,0:T(8,128)}, u32[]{:S(2)}, u32[]{:S(2)}) collective-permute-start(f32[512,512]{1,0:T(8,128)S(1)} %get-tuple-element.42.refs_2_), channel_id=1, source_target_pairs={{8,16},{16,8},{9,17},{17,9},{10,18},{18,10},{11,19},{19,11},{12,20... | collective-permute-start | bytes 3145736 | tf_op jit(solution)/shard_map/ppermute | solution.py:475
  17.3 51.0 %collective-permute-start.9 = (f32[512,512]{1,0:T(8,128)S(1)}, f32[512,512]{1,0:T(8,128)}, u32[]{:S(2)}, u32[]{:S(2)}) collective-permute-start(f32[512,512]{1,0:T(8,128)S(1)} %get-tuple-element.42.refs_2_), channel_id=1, source_target_pairs={{8,0},{16,24},{9,1},{17,25},{10,2},{18,26},{11,3},{19,27},{12,4},{... | collective-permute-start | bytes 3145736 | tf_op jit(solution)/shard_map/ppermute | solution.py:474
  23.9 19.2 %collective-permute-start.5 = (f32[192,512]{1,0:T(8,128)S(1)}, f32[192,512]{1,0:T(8,128)S(1)}, u32[]{:S(2)}, u32[]{:S(2)}) collective-permute-start(f32[192,512]{1,0:T(8,128)S(1)} %get-tuple-element.41), channel_id=1, source_target_pairs={{0,6},{1,7},{2,0},{3,1},{4,2},{5,3},{6,4},{7,5},{8,14},{9,15},{10,... | collective-permute-start | bytes 1179656 | tf_op jit(solution)/shard_map/ppermute | solution.py:495
  25.1 19.4 %collective-permute-start.3 = (f32[192,512]{1,0:T(8,128)S(1)}, f32[192,512]{1,0:T(8,128)S(1)}, u32[]{:S(2)}, u32[]{:S(2)}) collective-permute-start(f32[192,512]{1,0:T(8,128)S(1)} %get-tuple-element.39), channel_id=1, source_target_pairs={{0,2},{1,3},{2,4},{3,5},{4,6},{5,7},{6,0},{7,1},{8,10},{9,11},{10,... | collective-permute-start | bytes 1179656 | tf_op jit(solution)/shard_map/ppermute | solution.py:495
  26.0 35.4 %collective-permute-start.4 = (f32[192,512]{1,0:T(8,128)S(1)}, f32[192,512]{1,0:T(8,128)S(1)}, u32[]{:S(2)}, u32[]{:S(2)}) collective-permute-start(f32[192,512]{1,0:T(8,128)S(1)} %get-tuple-element.40), channel_id=1, source_target_pairs={{0,4},{1,5},{2,6},{3,7},{4,0},{5,1},{6,2},{7,3},{8,12},{9,13},{10,... | collective-permute-start | bytes 1179656 | tf_op jit(solution)/shard_map/ppermute | solution.py:495
  43.1 40.0 %collective-permute-start.13 = (f32[192,512]{1,0:T(8,128)S(1)}, f32[192,512]{1,0:T(8,128)S(1)}, u32[]{:S(2)}, u32[]{:S(2)}) collective-permute-start(f32[192,512]{1,0:T(8,128)S(1)} %get-tuple-element.52), channel_id=1, source_target_pairs={{0,6},{1,7},{2,0},{3,1},{4,2},{5,3},{6,4},{7,5},{8,14},{9,15},{10,... | collective-permute-start | bytes 1179656 | tf_op jit(solution)/shard_map/ppermute | solution.py:495
  69.7 10.9 %collective-permute-start.10 = (f32[512,512]{1,0:T(8,128)S(1)}, f32[512,512]{1,0:T(8,128)S(1)}, u32[]{:S(2)}, u32[]{:S(2)}) collective-permute-start(f32[512,512]{1,0:T(8,128)S(1)} %broadcast_select_fusion.refs_0_), channel_id=1, source_target_pairs={{0,1},{1,0},{2,3},{3,2},{4,5},{5,4},{6,7},{7,6},{8,9},{9,8},{10,11... | collective-permute-start | bytes 3145736 | tf_op jit(solution)/shard_map/ppermute | solution.py:469
  69.8 29.5 %collective-permute-start.12 = (f32[192,512]{1,0:T(8,128)S(1)}, f32[192,512]{1,0:T(8,128)S(1)}, u32[]{:S(2)}, u32[]{:S(2)}) collective-permute-start(f32[192,512]{1,0:T(8,128)S(1)} %get-tuple-element.50), channel_id=1, source_target_pairs={{0,4},{1,5},{2,6},{3,7},{4,0},{5,1},{6,2},{7,3},{8,12},{9,13},{10,... | collective-permute-start | bytes 1179656 | tf_op jit(solution)/shard_map/ppermute | solution.py:495
  72.7 26.6 %collective-permute-start.11 = (f32[192,512]{1,0:T(8,128)S(1)}, f32[192,512]{1,0:T(8,128)S(1)}, u32[]{:S(2)}, u32[]{:S(2)}) collective-permute-start(f32[192,512]{1,0:T(8,128)S(1)} %get-tuple-element.48), channel_id=1, source_target_pairs={{0,2},{1,3},{2,4},{3,5},{4,6},{5,7},{6,0},{7,1},{8,10},{9,11},{10,... | collective-permute-start | bytes 1179656 | tf_op jit(solution)/shard_map/ppermute | solution.py:495
  76.2 23.1 %copy-start.3 = (s32[3,512,128]{2,1,0:T(8,128)S(1)}, s32[3,512,128]{2,1,0:T(8,128)}, u32[]{:S(2)}) copy-start(s32[3,512,128]{2,1,0:T(8,128)} %copy-done.2) | copy-start | bytes 2359300
  76.2 35.3 %collective-permute-start.6 = (f32[512,512]{1,0:T(8,128)S(1)}, f32[512,512]{1,0:T(8,128)S(1)}, u32[]{:S(2)}, u32[]{:S(2)}) collective-permute-start(f32[512,512]{1,0:T(8,128)S(1)} %place.2), channel_id=1, source_target_pairs={{0,8},{8,0},{16,24},{24,16},{1,9},{9,1},{17,25},{25,17},{2,10},{10... | collective-permute-start | bytes 3145736 | tf_op jit(solution)/shard_map/ppermute | solution.py:502
  83.1 30.4 %copy-start.1 = (f32[1,512,1024]{2,1,0:T(8,128)S(1)}, f32[1,512,1024]{2,1,0:T(8,128)}, u32[]{:S(2)}) copy-start(f32[1,512,1024]{2,1,0:T(8,128)} %param.6) | copy-start | bytes 6291460
  83.1 30.4 %copy-start.5 = (f32[1,512]{1,0:T(1,128)S(1)}, f32[1,512]{1,0:T(1,128)}, u32[]{:S(2)}) copy-start(f32[1,512]{1,0:T(1,128)} %start_ref.1) | copy-start | bytes 6148
  83.1 30.4 %copy-start.6 = (s32[1,512]{1,0:T(1,128)S(1)}, s32[1,512]{1,0:T(1,128)}, u32[]{:S(2)}) copy-start(s32[1,512]{1,0:T(1,128)} %class_ref.1) | copy-start | bytes 6148
  83.1 30.5 %copy-start.7 = (f32[4]{0:T(128)S(1)}, f32[4]{0:T(128)}, u32[]{:S(2)}) copy-start(f32[4]{0:T(128)} %table_ref.1) | copy-start | bytes 52
  102.1 11.4 %collective-permute-start.14 = (f32[512,512]{1,0:T(8,128)}, f32[512,512]{1,0:T(8,128)}, u32[]{:S(2)}, u32[]{:S(2)}) collective-permute-start(f32[512,512]{1,0:T(8,128)} %place.3), channel_id=1, source_target_pairs={{8,16},{16,8},{9,17},{17,9},{10,18},{18,10},{11,19},{19,11},{12,20... | collective-permute-start | bytes 3145736 | tf_op jit(solution)/shard_map/ppermute | solution.py:507
  103.7 42.1 %collective-permute-start.15 = (f32[512,512]{1,0:T(8,128)}, f32[512,512]{1,0:T(8,128)}, u32[]{:S(2)}, u32[]{:S(2)}) collective-permute-start(f32[512,512]{1,0:T(8,128)} %place.3), channel_id=1, source_target_pairs={{0,8},{24,16},{1,9},{25,17},{2,10},{26,18},{3,11},{27,19},{4,12},{... | collective-permute-start | bytes 3145736 | tf_op jit(solution)/shard_map/ppermute | solution.py:506
  109.1 11.0 %collective-permute-start.18 = (f32[192,512]{1,0:T(8,128)}, f32[192,512]{1,0:T(8,128)}, u32[]{:S(2)}, u32[]{:S(2)}) collective-permute-start(f32[192,512]{1,0:T(8,128)} %get-tuple-element.58), channel_id=1, source_target_pairs={{0,6},{1,7},{2,0},{3,1},{4,2},{5,3},{6,4},{7,5},{8,14},{9,15},{10,... | collective-permute-start | bytes 1179656 | tf_op jit(solution)/shard_map/ppermute | solution.py:495
  109.1 36.8 %collective-permute-start.17 = (f32[192,512]{1,0:T(8,128)}, f32[192,512]{1,0:T(8,128)}, u32[]{:S(2)}, u32[]{:S(2)}) collective-permute-start(f32[192,512]{1,0:T(8,128)} %get-tuple-element.56), channel_id=1, source_target_pairs={{0,4},{1,5},{2,6},{3,7},{4,0},{5,1},{6,2},{7,3},{8,12},{9,13},{10,... | collective-permute-start | bytes 1179656 | tf_op jit(solution)/shard_map/ppermute | solution.py:495
  111.5 34.4 %collective-permute-start.16 = (f32[192,512]{1,0:T(8,128)}, f32[192,512]{1,0:T(8,128)}, u32[]{:S(2)}, u32[]{:S(2)}) collective-permute-start(f32[192,512]{1,0:T(8,128)} %get-tuple-element.54), channel_id=1, source_target_pairs={{0,2},{1,3},{2,4},{3,5},{4,6},{5,7},{6,0},{7,1},{8,10},{9,11},{10,... | collective-permute-start | bytes 1179656 | tf_op jit(solution)/shard_map/ppermute | solution.py:495
  113.5 32.3 %copy-start.4 = (s32[3,512,128]{2,1,0:T(8,128)S(1)}, s32[3,512,128]{2,1,0:T(8,128)}, u32[]{:S(2)}) copy-start(s32[3,512,128]{2,1,0:T(8,128)} %copy-done.2) | copy-start | bytes 2359300
  161.1 7.3 %collective-permute-start.19 = (f32[8,8,512]{2,1,0:T(8,128)S(1)}, f32[8,8,512]{2,1,0:T(8,128)S(1)}, u32[]{:S(2)}, u32[]{:S(2)}) collective-permute-start(f32[8,8,512]{2,1,0:T(8,128)S(1)} %all_to_all.16.refs_0_), channel_id=1, source_target_pairs={{0,8},{8,16},{16,24},{24,0},{1,9},{9,17},{17,25},{25,1},{2,10},{10... | collective-permute-start | bytes 393224 | tf_op jit(solution)/shard_map/ppermute | solution.py:515
  161.1 7.7 %collective-permute-start.20 = (f32[8,8,512]{2,1,0:T(8,128)S(1)}, f32[8,8,512]{2,1,0:T(8,128)S(1)}, u32[]{:S(2)}, u32[]{:S(2)}) collective-permute-start(f32[8,8,512]{2,1,0:T(8,128)S(1)} %all_to_all.16.refs_0_), channel_id=1, source_target_pairs={{0,16},{8,24},{16,0},{24,8},{1,17},{9,25},{17,1},{25,9},{2,18},{10... | collective-permute-start | bytes 393224 | tf_op jit(solution)/shard_map/ppermute | solution.py:515
  162.2 6.7 %collective-permute-start.21 = (f32[8,8,512]{2,1,0:T(8,128)S(1)}, f32[8,8,512]{2,1,0:T(8,128)S(1)}, u32[]{:S(2)}, u32[]{:S(2)}) collective-permute-start(f32[8,8,512]{2,1,0:T(8,128)S(1)} %all_to_all.16.refs_0_), channel_id=1, source_target_pairs={{0,24},{8,0},{16,8},{24,16},{1,25},{9,1},{17,9},{25,17},{2,26},{10... | collective-permute-start | bytes 393224 | tf_op jit(solution)/shard_map/ppermute | solution.py:515

commit v3 on v2

v3 whole, which is shorter than its diff:
```python
import functools
import math

import jax
import jax.numpy as jnp
from jax import lax
from jax.experimental import pallas as pl
from jax.experimental.pallas import tpu as pltpu
from jax.sharding import PartitionSpec as P

Y = 1024
BAND = 32
ITERS = 2
FIELDS = 8
HINT = 16
VMEM = pl.BlockSpec(memory_space=pltpu.VMEM)
SMEM = pl.BlockSpec(memory_space=pltpu.SMEM)
LIMIT = pltpu.CompilerParams(vmem_limit_bytes=20 * 1024 * 1024)


def cost(flops, values):
    return pl.CostEstimate(flops=flops, bytes_accessed=4 * values, transcendentals=0)


def store_filter(rim, high_ref, low_ref):
    shape = high_ref.shape
    distance = jnp.abs(lax.broadcasted_iota(jnp.int32, shape, 0) - rim - lax.broadcasted_iota(jnp.int32, shape, 1))
    parity = 1.0 - 2.0 * (distance % 2).astype(jnp.float32)
    size = jnp.exp(distance.astype(jnp.float32) * math.log(2.0 - math.sqrt(3.0)))
    exact = jnp.where(distance <= BAND, math.sqrt(3.0) * parity * size, 0.0)
    high = exact.astype(jnp.bfloat16)
    high_ref[...] = high
    low_ref[...] = (exact - high.astype(jnp.float32)).astype(jnp.bfloat16)


def prefilter_kernel(width, rim, vol_ref, early_ref, left_ref, right_ref, high_ref, low_ref, held_ref, sent):
    rows, columns = vol_ref.shape
    half = columns // 2
    steps = held_ref.shape[0]
    block = rows // steps
    copies = [
        pltpu.make_async_copy(vol_ref.at[pl.ds(number * block, block)], held_ref.at[number], sent.at[number])
        for number in range(steps)
    ]
    for copy in copies:
        copy.start()
    store_filter(rim, high_ref, low_ref)
    for number, copy in enumerate(copies):
        copy.wait()
        at = slice(number * block, (number + 1) * block)
        voxels = held_ref[number]
        high = voxels.astype(jnp.bfloat16)
        low = (voxels - high.astype(jnp.float32)).astype(jnp.bfloat16)
        for start in range(0, columns, width):
            first, last = max(0, start - rim), min(columns, start + width + rim)
            top = first - (start - rim)
            band = slice(top, top + last - first)
            dot = functools.partial(jnp.dot, preferred_element_type=jnp.float32)
            out = dot(high[:, first:last], low_ref[band, :]) + dot(low[:, first:last], high_ref[band, :])
            out = out + dot(high[:, first:last], high_ref[band, :])
            if start < half:
                left_ref[at, start : start + width] = out
            else:
                right_ref[at, start - half : start - half + width] = out


def prefilter(voxels, early):
    rows, columns = voxels.shape
    width, rim, steps = 256, 128, 2
    halves = jax.ShapeDtypeStruct((rows, columns // 2), jnp.float32)
    matrix = pltpu.VMEM((width + 2 * rim, width), jnp.bfloat16)
    anywhere = pl.BlockSpec(memory_space=pl.ANY)
    return pl.pallas_call(
        functools.partial(prefilter_kernel, width, rim),
        in_specs=[pl.BlockSpec(memory_space=pltpu.HBM), anywhere],
        out_specs=[VMEM, VMEM],
        out_shape=[halves, halves],
        scratch_shapes=[
            matrix,
            matrix,
            pltpu.VMEM((steps, rows // steps, columns), jnp.float32),
            pltpu.SemaphoreType.DMA((steps,)),
        ],
        cost_estimate=cost(3 * 2 * rows * columns * (width + 2 * rim), 2 * rows * columns),
        compiler_params=LIMIT,
        name="prefilter",
    )(voxels, early)


def column(line):
    parts = [
        jnp.broadcast_to(line[:, start : start + 128], (128, 128)).T for start in range(0, line.shape[1], 128)
    ]
    return parts[0] if len(parts) == 1 else jnp.concatenate(parts, axis=0)


def request_kernel(devices, capacity, direct, inner_ref, at_ref, side_ref, inward_ref, own_ref, place_ref, *table_refs):
    rows = own_ref.shape[1]
    before = lax.broadcasted_iota(jnp.int32, (rows, rows), 0)
    after = lax.broadcasted_iota(jnp.int32, (rows, rows), 1)
    earlier = jnp.where(before < after, 1.0, 0.0).astype(jnp.bfloat16)
    peers = lax.broadcasted_iota(jnp.int32, (devices, rows), 0)
    chip, core, chips = at_ref[0] // 2, at_ref[0] % 2, devices // 2
    slots = lax.broadcasted_iota(jnp.int32, (128, rows), 0)
    against = (((1,), (1,)), ((), ()))
    side = side_ref[...]
    for number, name in enumerate((side, jnp.where(inner_ref[0] != 0, inward_ref[...], side), own_ref[...])):
        peer = name // rows
        row = name - peer * rows
        turn = peer
        if direct:
            other = (peer + core) % 2
            turn = 2 * ((chip - peer // 2 + chips) % chips) + other
            peer = 2 * ((peer // 2 - chip + chips) % chips) + other
        hit = jnp.where(peers == peer, 1.0, 0.0)
        running = jnp.dot(hit.astype(jnp.bfloat16), earlier, preferred_element_type=jnp.float32)
        slot = jnp.sum(hit * running, axis=0, keepdims=True).astype(jnp.int32)
        place_ref[number] = column(turn * capacity + slot)
        taken = jnp.where(slots == slot, 1.0, 0.0).astype(jnp.bfloat16)
        upper = (hit * (row // 16).astype(jnp.float32)).astype(jnp.bfloat16)
        lower = (hit * (row % 16).astype(jnp.float32)).astype(jnp.bfloat16)
        found = 16.0 * lax.dot_general(upper, taken, against, preferred_element_type=jnp.float32)
        found = found + lax.dot_general(lower, taken, against, preferred_element_type=jnp.float32)
        share = devices // len(table_refs)
        for turn, table_ref in enumerate(table_refs):
            lines = found[turn * share : (turn + 1) * share].astype(jnp.int32)
            table_ref[:, 128 * number : 128 * number + 128] = lines


def requests(inner, at, side, inward, own, devices, capacity, direct):
    rows = own.shape[1]
    parts = devices // 2 if direct else 1
    places, *tables = pl.pallas_call(
        functools.partial(request_kernel, devices, capacity, direct),
        in_specs=[SMEM, SMEM, VMEM, VMEM, VMEM],
        out_specs=[VMEM] * (1 + parts),
        out_shape=[jax.ShapeDtypeStruct((3, rows, 128), jnp.int32)]
        + [jax.ShapeDtypeStruct((devices // parts, 3 * 128), jnp.int32)] * parts,
        compiler_params=LIMIT,
        name="requests",
    )(inner, at, side, inward, own)
    return places, tables


def terms(values):
    high = values.astype(jnp.bfloat16)
    rest = values - high.astype(jnp.float32)
    middle = rest.astype(jnp.bfloat16)
    low = (rest - middle.astype(jnp.float32)).astype(jnp.bfloat16)
    return high, middle, low


def picked(chosen, parts):
    dot = functools.partial(jnp.dot, preferred_element_type=jnp.float32)
    return (dot(chosen, parts[2]) + dot(chosen, parts[1])) + dot(chosen, parts[0])


def pick_kernel(chips, capacity, number, inner_ref, *refs):
    asked_refs, refs = refs[:chips], refs[chips:]
    sources, outs, chosen_ref = refs[: -1 - chips], refs[-1 - chips : -1], refs[-1]
    rows = sources[0].shape[0]
    row = lax.broadcasted_iota(jnp.int32, (128, rows), 1)
    for core in range(2):
        for turn in range(chips):
            back = (chips - turn) % chips
            line = asked_refs[back][core : core + 1, 128 * number : 128 * number + 128]
            wanted = jnp.concatenate([column(line)] * (rows // 128), axis=1)
            hit = jnp.where(wanted == row, 1.0, 0.0)[:capacity]
            chosen_ref[turn * capacity : (turn + 1) * capacity, :] = hit.astype(jnp.bfloat16)
        source = sources[core][...]
        if len(sources) > 2:
            source = jnp.where(inner_ref[0] != 0, source, sources[2 + core][...])
        rows_out = picked(chosen_ref[...], terms(source))
        for turn in range(chips):
            outs[turn][core * capacity : (core + 1) * capacity, :] = rows_out[
                turn * capacity : (turn + 1) * capacity
            ]


def pick(inner, asked, number, sources, chips, capacity):
    rows, width = sources[0].shape
    block = jax.ShapeDtypeStruct((2 * capacity, width), jnp.float32)
    return pl.pallas_call(
        functools.partial(pick_kernel, chips, capacity, number),
        in_specs=[SMEM] + [VMEM] * (len(asked) + len(sources)),
        out_specs=[VMEM] * chips,
        out_shape=[block] * chips,
        scratch_shapes=[pltpu.VMEM((chips * capacity, rows), jnp.bfloat16)],
        cost_estimate=cost(HINT * 12 * chips * capacity * rows * width, 5 * rows * width),
        compiler_params=LIMIT,
        name="pick",
    )(inner, *asked, *sources)


def store_terms(blocks, terms_ref):
    start = 0
    for block in blocks:
        for number, part in enumerate(terms(block[...])):
            terms_ref[number, start : start + block.shape[0], :] = part
        start += block.shape[0]


def placed(place, terms_ref):
    count = terms_ref.shape[1]
    lane = lax.broadcasted_iota(jnp.int32, place.shape, 1)
    chosen = [jnp.where(place - start == lane, 1.0, 0.0) for start in range(0, count, 128)]
    chosen = jnp.concatenate(chosen, axis=1).astype(jnp.bfloat16)
    return picked(chosen, [terms_ref[number] for number in range(3)])


def place_kernel(number, place_ref, *refs):
    blocks, out_ref, terms_ref = refs[:-2], refs[-2], refs[-1]
    store_terms(blocks, terms_ref)
    out_ref[...] = placed(place_ref[number], terms_ref)


def place(number, places, blocks):
    rows = places.shape[1]
    width = blocks[0].shape[1]
    total = sum(block.shape[0] for block in blocks)
    return pl.pallas_call(
        functools.partial(place_kernel, number),
        in_specs=[VMEM] * (1 + len(blocks)),
        out_specs=VMEM,
        out_shape=jax.ShapeDtypeStruct((rows, width), jnp.float32),
        scratch_shapes=[pltpu.VMEM((3, total, width), jnp.bfloat16)],
        cost_estimate=cost(HINT * 3 * 2 * total * rows * width, 3 * rows * width),
        compiler_params=LIMIT,
        name="place",
    )(places, *blocks)


def on_tile(values, at, change):
    parts = [values[:, :at], change(values[:, at : at + 128]), values[:, at + 128 :]]
    return jnp.concatenate([part for part in parts if part.shape[1]], axis=1)


def cleared(lane):
    return lambda tile: jnp.where(lax.broadcasted_iota(jnp.int32, tile.shape, 1) == lane, 0.0, tile)


def before_of(values):
    return on_tile(pltpu.roll(values, 1, 1), 0, cleared(0))


def after_of(values):
    columns = values.shape[1]
    return on_tile(pltpu.roll(values, columns - 1, 1), columns - 128, cleared(127))


def taylor(coeffs, counted):
    before, after = before_of(coeffs), after_of(coeffs)
    bend = after - 2.0 * coeffs + before
    return counted(coeffs + bend * (1.0 / 6.0)), counted(0.5 * (after - before)), counted(bend)


def lanes(values):
    rows, columns = values.shape
    total = values[:, 0:128]
    for start in range(128, columns, 128):
        total = total + values[:, start : start + 128]
    sums = [jnp.sum(total[start : start + 128].T, axis=0, keepdims=True) for start in range(0, rows, 128)]
    return jnp.concatenate(sums, axis=1)


def row_sums(sign, near, far, voxels, counted):
    voxels = counted(voxels)
    value, slope, bend = taylor(near, counted)
    other_value, other_slope, other_bend = taylor(far, counted)
    value = value - voxels
    other_value = other_value - voxels
    slope = sign * slope
    other_slope = -sign * other_slope
    c0 = slope * slope + other_slope * other_slope
    return (
        lanes(slope * value + other_slope * other_value),
        lanes(c0 + bend * value + other_bend * other_value),
        lanes(c0),
        lanes(2.0 * (slope * bend + other_slope * other_bend)),
        lanes(bend * bend + other_bend * other_bend),
    )


STEP = 128


def left_sums_kernel(sign_ref, table_ref, near_ref, far_ref, vol_ref, start_ref, class_ref, out_ref):
    rows, half = near_ref.shape

    def counted(values):
        return on_tile(values, half - 128, cleared(127))

    for start in range(0, rows, STEP):
        at = slice(start, start + STEP)
        lines = row_sums(sign_ref[0], near_ref[at], far_ref[at], vol_ref[at, :half], counted)
        for number, line in enumerate(lines):
            out_ref[number : number + 1, at] = line
    weight = jnp.zeros(start_ref.shape, jnp.float32)
    for kind in range(table_ref.shape[0]):
        weight = jnp.where(class_ref[...] == kind, table_ref[kind], weight)
    out_ref[5:6, :] = start_ref[...]
    out_ref[6:7, :] = jnp.sqrt(weight)
    out_ref[7:8, :] = jnp.zeros(start_ref.shape, jnp.float32)


def left_sums(sign, table, near, far, voxels, start, classes):
    rows, half = near.shape
    return pl.pallas_call(
        left_sums_kernel,
        in_specs=[SMEM, SMEM] + [VMEM] * 5,
        out_specs=VMEM,
        out_shape=jax.ShapeDtypeStruct((FIELDS, rows), jnp.float32),
        cost_estimate=cost(60 * rows * half, 6 * rows * half),
        compiler_params=LIMIT,
        name="left_sums",
    )(sign, table, near, far, voxels, start, classes)


def right_sums_kernel(inner_ref, sign_ref, place_ref, near_ref, far_ref, hop_ref, vol_ref, so_far_ref, *refs):
    blocks, fields_ref, third_ref, terms_ref = refs[:-3], refs[-3], refs[-2], refs[-1]
    rows, half = near_ref.shape
    inner = inner_ref[0] != 0
    store_terms(blocks, terms_ref)
    third_ref[...] = placed(place_ref[2], terms_ref)

    def counted(values):
        lane = lax.broadcasted_iota(jnp.int32, (STEP, 128), 1)
        return on_tile(values, 0, lambda tile: jnp.where(lane == 127, tile, 0.0))

    for start in range(0, rows, STEP):
        at = slice(start, start + STEP)
        third = third_ref[at]
        near = jnp.concatenate([near_ref[at, half - 128 :], jnp.where(inner, hop_ref[at], third)], axis=1)
        far = jnp.concatenate([far_ref[at, half - 128 :], jnp.where(inner, third, 0.0)], axis=1)
        lines = row_sums(sign_ref[0], near, far, vol_ref[at, half - 128 :], counted)
        for number, line in enumerate(lines):
            fields_ref[number : number + 1, at] = so_far_ref[number : number + 1, at] + line
    fields_ref[5:8, :] = so_far_ref[5:8, :]


def right_sums(inner, sign, places, near, far, hop, voxels, so_far, blocks):
    rows, half = near.shape
    total = sum(block.shape[0] for block in blocks)
    return pl.pallas_call(
        right_sums_kernel,
        in_specs=[SMEM, SMEM] + [VMEM] * (6 + len(blocks)),
        out_specs=[VMEM, VMEM],
        out_shape=[
            jax.ShapeDtypeStruct((FIELDS, rows), jnp.float32),
            jax.ShapeDtypeStruct((rows, half), jnp.float32),
        ],
        scratch_shapes=[pltpu.VMEM((3, total, half), jnp.bfloat16)],
        cost_estimate=cost(3 * 2 * total * rows * half, 5 * rows * half),
        compiler_params=LIMIT,
        name="right_sums",
    )(inner, sign, places, near, far, hop, voxels, so_far, *blocks)


def plane_stencil(field):
    slabs, rows = field.shape
    hops = Y // rows
    slab = lax.broadcasted_iota(jnp.int32, field.shape, 0)
    row = lax.broadcasted_iota(jnp.int32, field.shape, 1)

    def moved(cells, by):
        kept = slab >= by if by > 0 else slab < slabs + by
        return jnp.where(kept, pltpu.roll(cells, by % slabs, 0), 0.0)

    low = pltpu.roll(field, 1, 1)
    high = pltpu.roll(field, rows - 1, 1)
    low = jnp.where(row == 0, moved(low, 1), low)
    high = jnp.where(row == rows - 1, moved(high, -1), high)
    return 4.0 * field - low - high - moved(field, hops) - moved(field, -hops)


def total(parts):
    return jnp.sum(functools.reduce(jnp.add, parts), keepdims=True)


def iterate(groups):
    velocities = [group[5] for group in groups]
    for _ in range(ITERS):
        uppers, lowers, directions = [], [], []
        for (l0, l1, c0, c1, c2, _, stiffness, _), velocity in zip(groups, velocities):
            linear = l0 + velocity * (l1 + velocity * (0.75 * c1 + velocity * (0.5 * c2)))
            curvature = c0 + velocity * (c1 + velocity * c2)
            gradient = linear + stiffness * plane_stencil(stiffness * velocity)
            direction = gradient / (curvature + 4.0 * stiffness * stiffness)
            scaled = stiffness * direction
            uppers.append(direction * gradient)
            lowers.append(curvature * direction * direction + scaled * plane_stencil(scaled))
            directions.append(direction)
        alpha = total(uppers) / total(lowers)
        velocities = [velocity - alpha * direction for velocity, direction in zip(velocities, directions)]
    return velocities[0]


def final_kernel(chips, at_ref, inner_ref, sign_ref, *refs):
    fields_refs = refs[:-10]
    near_ref, far_ref, hop_ref, third_ref, vol_ref, velocity_ref, misfit_ref = refs[-10:-3]
    fields_ref, tile_ref, sent = refs[-3:]
    rows, half = near_ref.shape
    if chips:
        scans = len(fields_refs) // 2
        for number, ref in enumerate(fields_refs):
            core = (at_ref[0] + number // scans) % 2
            for turn in range(chips):
                slab = 2 * ((at_ref[0] // 2 - turn + chips) % chips) + core
                fields_ref[number % scans, slab] = ref[FIELDS * turn : FIELDS * turn + FIELDS, :]
        groups = [[fields_ref[scan, :, i, :] for i in range(FIELDS)] for scan in range(scans)]
    else:
        groups = [[ref[:, i, :] for i in range(FIELDS)] for ref in fields_refs]
    velocity = iterate(groups)
    slab = lax.broadcasted_iota(jnp.int32, velocity.shape, 0)
    own = jnp.sum(jnp.where(slab == at_ref[0], velocity, 0.0), axis=0, keepdims=True)
    velocity_ref[...] = own

    inner = inner_ref[0] != 0
    copies = []
    for number, start in enumerate(range(0, rows, STEP)):
        at = slice(start, start + STEP)
        moved = column(own[:, at])
        weight = 1.0 / 6.0 + 0.5 * moved * moved
        drift = (0.5 * sign_ref[0]) * moved
        wide = lambda tile: jnp.concatenate([tile] * (2 * half // 128), axis=1)
        up, down, middle = wide(weight + drift), wide(weight - drift), wide(1.0 - 2.0 * weight)
        third = third_ref[at]
        near = jnp.concatenate([near_ref[at], jnp.where(inner, hop_ref[at], third)], axis=1)
        far = jnp.concatenate([far_ref[at], jnp.where(inner, third, 0.0)], axis=1)
        after = after_of(up * near + down * far)
        before = before_of(down * near + up * far)
        tile_ref[number] = middle * (near + far) + after + before - 2.0 * vol_ref[at]
        copies.append(pltpu.make_async_copy(tile_ref.at[number], misfit_ref.at[pl.ds(start, STEP)], sent.at[number]))
        copies[-1].start()
    for copy in copies:
        copy.wait()


def finish(at, inner, sign, groups, streams, voxels, chips):
    rows, columns = voxels.shape
    steps = rows // STEP
    shape = (len(groups) // 2, 2 * chips, FIELDS, rows) if chips else (1, 1, 8, 128)
    return pl.pallas_call(
        functools.partial(final_kernel, chips),
        in_specs=[SMEM, SMEM, SMEM] + [VMEM] * (len(groups) + 5),
        out_specs=[VMEM, pl.BlockSpec(memory_space=pl.ANY)],
        out_shape=[
            jax.ShapeDtypeStruct((1, rows), jnp.float32),
            jax.ShapeDtypeStruct((rows, columns), jnp.float32),
        ],
        scratch_shapes=[
            pltpu.VMEM(shape, jnp.float32),
            pltpu.VMEM((steps, STEP, columns), jnp.float32),
            pltpu.SemaphoreType.DMA((steps,)),
        ],
        compiler_params=LIMIT,
        name="finish",
    )(at, inner, sign, *groups, *streams, voxels)


def swapped(block, axis):
    return lax.all_to_all(block, axis, split_axis=0, concat_axis=0, tiled=True)


def after(block, *earlier):
    return lax.optimization_barrier((block, *earlier))[0]


ORDER = (2, 1, 3)


def on_device(volume, velocity0, fetch_slab, fetch_row, modulus_class, modulus_table):
    voxels = volume[0]
    rows = voxels.shape[0]
    slabs = lax.axis_size("slab")
    scans = lax.axis_size("scan")
    capacity = max(2, 3 * rows // (2 * slabs))
    direct = slabs == 8
    scan = lax.axis_index("scan")
    slab = lax.axis_index("slab")
    at = slab.astype(jnp.int32).reshape(1)
    inner = ((scan == 1) | (scan == 2)).astype(jnp.int32).reshape(1)
    sign = jnp.where(scan % 2 == 0, 1.0, -1.0).astype(jnp.float32).reshape(1)
    sides = [(0, 1), (1, 0), (2, 3), (3, 2)]
    middle = [(1, 2), (2, 1)]

    names = fetch_slab[0, :, :, 0] * rows + fetch_row[0]
    lent = jnp.where(scan % 2 == 0, names[0:1], names[1:2])
    own = jnp.where(scan < 2, names[0:1], names[1:2])
    side, inward = lax.ppermute(lent, "scan", sides), lax.ppermute(own, "scan", middle)
    places, tables = requests(inner, at, side, inward, own, slabs, capacity, direct)
    chips = slabs // 2
    turns = [[(p, (p + 2 * turn) % slabs) for p in range(slabs)] for turn in range(chips)]
    if direct:
        asked = tables[:1] + [lax.ppermute(tables[turn], "slab", turns[turn]) for turn in range(1, chips)]
    else:
        asked = [swapped(tables[0], "slab")]

    def other_core(block):
        return lax.ppermute(block, "slab", [(p, p ^ 1) for p in range(slabs)]) if direct else block

    left, right = prefilter(voxels, names)
    left, right, _ = lax.optimization_barrier((left, right, tables[0]))
    left_other, right_other = other_core(left), other_core(right)
    from_inner = lax.ppermute(right, "scan", [(1, 0), (2, 3)])
    from_middle = lax.ppermute(right, "scan", middle)

    def picks(number, sources):
        if direct:
            return pick(inner, asked, number, sources, chips, capacity)
        source = sources[0] if len(sources) == 2 else jnp.where(inner[0] != 0, sources[0], sources[2])
        wanted = asked[0][:, 128 * number : 128 * number + capacity]
        return [jnp.take(source, wanted.reshape(-1), axis=0)]

    sent = []

    def fetched(blocks):
        if not direct:
            arrived = swapped(blocks[0].reshape(slabs, capacity, -1), "slab")
            return [arrived.reshape(slabs * capacity, -1)]
        arrived = [blocks[0]] + [None] * (chips - 1)
        for turn in ORDER:
            held = sent[-3:-2]
            block = after(blocks[turn], *held) if held else blocks[turn]
            arrived[turn] = lax.ppermute(block, "slab", turns[turn])
            sent.append(arrived[turn])
        return arrived

    blocks = picks(0, [left, left_other])
    arrived = fetched(blocks)
    first = place(0, places, arrived)
    lender = jnp.where(inner == 1, after(from_middle, *arrived), from_inner)
    near = lax.ppermute(first, "scan", sides)
    arrived = fetched(picks(1, [left, left_other, right, right_other]))
    blocks = picks(2, [lender, other_core(lender)])
    second = place(1, places, [after(arrived[0], blocks[0]), *arrived[1:]])
    hop = lax.ppermute(second, "scan", [(0, 1), (3, 2)])
    far = lax.ppermute(second, "scan", middle)
    arrived = fetched(blocks)
    so_far = left_sums(sign, modulus_table, near, far, voxels, velocity0, modulus_class)
    sums, third = right_sums(inner, sign, places, near, far, hop, voxels, so_far, arrived)

    def scans_of(block):
        routes = [[(p, (p + turn) % scans) for p in range(scans)] for turn in range(1, scans)]
        return [block] + [lax.ppermute(block, "scan", route) for route in routes]

    if direct:
        line = jnp.concatenate([sums] + [lax.ppermute(sums, "slab", route) for route in turns[1:]], axis=0)
        groups = scans_of(line)
        groups += [other_core(group) for group in groups]
    else:
        groups = scans_of(swapped(jnp.broadcast_to(sums[None], (slabs, FIELDS, rows)), "slab"))
    velocity, misfit = finish(
        at, inner, sign, groups, (near, far, hop, third), after(voxels, sums), chips if direct else 0
    )
    return velocity, misfit[None]


def solution(mesh):
    return jax.shard_map(
        on_device,
        mesh=mesh,
        in_specs=(
            P("scan", "slab", None),
            P("scan", "slab"),
            P("scan", None, "slab", None),
            P("scan", None, "slab"),
            P("scan", "slab"),
            P(),
        ),
        out_specs=(P("scan", "slab"), P("scan", "slab", None)),
        check_vma=False,
    )
```

time: 176 us -> 168 us (0.955)
  blocking collectives: 9.17 us -> 0 us
  waiting for transfers between devices: 90.6 us -> 97.4 us
  Pallas kernels: 32.6 us -> 27.3 us
    all_to_all x1 -> x0, blocking collectives: 9.17 us -> none  [swapped(): return lax.all_to_all(block, axis, split_axis=0, concat_axis=0, tiled=True)]
    ppermute x12 -> x18, starting transfers between devices: 14.5 us -> 21.4 us  [the longest x9 7.79 us: fetched(): arrived[turn] = lax.ppermute(block, 'slab', turns[turn])]
    all_to_all x1 -> x0, starting transfers between devices: 4.87 us -> none  [on_device(): lax.all_to_all(table, 'slab', 0, 0, axis_index_groups=same_core, tiled=True)]
    ppermute x12 -> x18, waiting for transfers between devices: 81.2 us -> 85.3 us  [the longest x9 81.4 us: fetched(): arrived[turn] = lax.ppermute(block, 'slab', turns[turn])]
    ppermute x1, waiting for transfers between devices: 6.86 us -> 10.8 us  [on_device(): from_inner = lax.ppermute(right, 'scan', [(1, 0), (2, 3)])]
    pallas_call x3, Pallas kernels: 8.35 us -> 5.63 us  [pick(): pl.pallas_call(functools.partial(pick_kernel, chips, capacity, number), i...]
    all_to_all x1 -> x0, waiting for transfers between devices: 2.54 us -> none  [on_device(): lax.all_to_all(table, 'slab', 0, 0, axis_index_groups=same_core, tiled=True)]
    pallas_call x6, Pallas kernels: 23.3 us -> 20.8 us  [the longest x1 5.61 us: right_sums(): pl.pallas_call(right_sums_kernel, in_specs=[SMEM, SMEM] + [VMEM] * (6 + l...]
  transfers between devices with their start and end apart: 23 -> 32, of which waited for: 10 -> 15; matrix products, arithmetic and copies ran while one was open for 1% -> 0% of each run, Pallas kernels for 11% -> 9%
where the time goes in v3:
time: 168 us; the launch traced here: 167 us
  waiting for transfers between devices  97.4 us (58%)
  starting transfers between devices  38.4 us (23%)
  Pallas kernels  27.3 us (16%)
    ppermute x9, waiting for transfers between devices, fetched(): arrived[turn] = lax.ppermute(block, 'slab', turns[turn])  81.4 us
    ppermute x1, waiting for transfers between devices, on_device(): from_inner = lax.ppermute(right, 'scan', [(1, 0), (2, 3)])  10.8 us
    ppermute x9, starting transfers between devices, fetched(): arrived[turn] = lax.ppermute(block, 'slab', turns[turn])  7.79 us
    pallas_call x3, Pallas kernels, pick(): pl.pallas_call(functools.partial(pick_kernel, chips, capacity, number), i...  5.63 us
    pallas_call x1, Pallas kernels, right_sums(): pl.pallas_call(right_sums_kernel, in_specs=[SMEM, SMEM] + [VMEM] * (6 + l...  5.61 us
    ppermute x3, starting transfers between devices, on_device(): lax.ppermute(tables[turn], 'slab', turns[turn])  5.57 us
    pallas_call x1, Pallas kernels, finish(): pl.pallas_call(functools.partial(final_kernel, chips), in_specs=[SMEM, SM...  5.4 us
    ppermute x3, starting transfers between devices, on_device(): lax.ppermute(sums, 'slab', route)  5.15 us
  transfers between devices with their start and end apart: 32, of which 15 were waited for; matrix products, arithmetic and copies ran while one was open for 0% of the time, Pallas kernels for 9%

profile of v3, /device:TPU:0, one launch (start us, length us, event | category | flops | bytes accessed | tf_op | source)
XLA Modules:
  0.0 166.6 jit_solution(14358978129599114831)
XLA Ops:
  0.6 0.7 bitcast_add_fusion.early_ref
  1.4 3.0 %collective-permute-start = (s32[1,512]{1,0:T(1,128)S(1)}, s32[1,512]{1,0:T(1,128)S(1)}, u32[]{:S(2)}, u32[]{:S(2)}) collective-permute-start(s32[1,512]{1,0:T(1,128)S(1)} %get-tuple-element.71), channel_id=1, source_target_pairs={{0,8},{8,0},{16,24},{24,16},{1,9},{9,1},{17,25},{25,17},{2,10},{10... | collective-permute-start | bytes 6152 | tf_op jit(solution)/shard_map/ppermute | solution.py:490
  4.4 0.6 collective-permute-start.1
  5.0 0.0 copy-start
  5.0 1.6 copy-done
  6.6 2.5 %prefilter.1 = (f32[512,512]{1,0:T(8,128)S(1)}, f32[512,512]{1,0:T(8,128)S(1)}) custom-call(f32[512,1024]{1,0:T(8,128)S(1)} %bitcast.10, s32[2,512]{1,0:T(2,128)S(1)} %bitcast_add_fusion.early_ref), custom_call_target="tpu_custom_call" | custom-call | flops 1610612736 | bytes 4194304 | tf_op jit(solution)/shard_map/prefilter/pallas_call | solution.py:73
  9.2 0.0 collective-permute-done.side_ref
  9.2 0.0 collective-permute-done.1.inward_ref
  9.2 0.9 requests.1
  10.1 0.1 collective-permute-start.5
  10.1 1.6 collective-permute-start.2
  11.8 2.6 %collective-permute-start.3 = (s32[2,384]{1,0:T(2,128)S(1)}, s32[2,384]{1,0:T(2,128)S(1)}, u32[]{:S(2)}, u32[]{:S(2)}) collective-permute-start(s32[2,384]{1,0:T(2,128)S(1)} %get-tuple-element.39), channel_id=1, source_target_pairs={{0,4},{1,5},{2,6},{3,7},{4,0},{5,1},{6,2},{7,3},{8,12},{9,13},{10,... | collective-permute-start | bytes 9224 | tf_op jit(solution)/shard_map/ppermute | solution.py:495
  14.3 1.4 collective-permute-start.4
  15.7 0.7 collective-permute-start.11
  16.4 1.3 collective-permute-start.12
  17.7 0.2 collective-permute-done.4.refs_3_
  17.9 0.0 collective-permute-done.5.refs_5_
  17.9 1.5 pick.3
  19.5 3.2 %collective-permute-start.8 = (f32[192,512]{1,0:T(8,128)S(1)}, f32[192,512]{1,0:T(8,128)S(1)}, u32[]{:S(2)}, u32[]{:S(2)}) collective-permute-start(f32[192,512]{1,0:T(8,128)S(1)} %get-tuple-element.47), channel_id=1, source_target_pairs={{0,6},{1,7},{2,0},{3,1},{4,2},{5,3},{6,4},{7,5},{8,14},{9,15},{10,... | collective-permute-start | bytes 1179656 | tf_op jit(solution)/shard_map/ppermute | solution.py:525
  22.7 0.0 collective-permute-start.6
  22.7 0.0 collective-permute-done.10.refs_7_
  22.7 1.1 collective-permute-start.7
  23.8 1.6 pick.4
  25.4 13.4 %collective-permute-done.8.refs_3_ = f32[192,512]{1,0:T(8,128)S(1)} collective-permute-done((f32[192,512]{1,0:T(8,128)S(1)}, f32[192,512]{1,0:T(8,128)S(1)}, u32[]{:S(2)}, u32[]{:S(2)}) %collective-permute-start.8) | collective-permute-done | bytes 393248 | tf_op jit(solution)/shard_map/ppermute | solution.py:525
  38.8 3.0 %collective-permute-done.6.refs_1_ = f32[192,512]{1,0:T(8,128)S(1)} collective-permute-done((f32[192,512]{1,0:T(8,128)S(1)}, f32[192,512]{1,0:T(8,128)S(1)}, u32[]{:S(2)}, u32[]{:S(2)}) %collective-permute-start.6) | collective-permute-done | bytes 393248 | tf_op jit(solution)/shard_map/ppermute | solution.py:525
  41.8 15.7 %collective-permute-done.7.refs_2_ = f32[192,512]{1,0:T(8,128)S(1)} collective-permute-done((f32[192,512]{1,0:T(8,128)S(1)}, f32[192,512]{1,0:T(8,128)S(1)}, u32[]{:S(2)}, u32[]{:S(2)}) %collective-permute-start.7) | collective-permute-done | bytes 393248 | tf_op jit(solution)/shard_map/ppermute | solution.py:525
  57.5 10.8 %collective-permute-done.12 = f32[512,512]{1,0:T(8,128)S(1)} collective-permute-done((f32[512,512]{1,0:T(8,128)S(1)}, f32[512,512]{1,0:T(8,128)S(1)}, u32[]{:S(2)}, u32[]{:S(2)}) %collective-permute-start.12) | collective-permute-done | bytes 1048608 | tf_op jit(solution)/shard_map/ppermute | solution.py:505
  68.3 0.2 broadcast_select_fusion.refs_4_
  68.5 0.1 collective-permute-start.13
  68.6 0.3 collective-permute-start.15
  68.9 0.8 collective-permute-start.14
  69.7 1.4 place.2
  71.1 3.8 %collective-permute-start.9 = (f32[512,512]{1,0:T(8,128)S(1)}, f32[512,512]{1,0:T(8,128)S(1)}, u32[]{:S(2)}, u32[]{:S(2)}) collective-permute-start(f32[512,512]{1,0:T(8,128)S(1)} %place.2), channel_id=1, source_target_pairs={{0,8},{8,0},{16,24},{24,16},{1,9},{9,1},{17,25},{25,17},{2,10},{10... | collective-permute-start | bytes 3145736 | tf_op jit(solution)/shard_map/ppermute | solution.py:533
  75.0 0.0 collective-permute-done.13.refs_5_
  75.0 2.5 %pick.5 = (f32[192,512]{1,0:T(8,128)S(1)}, f32[192,512]{1,0:T(8,128)}, f32[192,512]{1,0:T(8,128)}, f32[192,512]{1,0:T(8,128)}) custom-call(s32[1]{0:T(128)} %bitcast.1.inner_ref, s32[2,384]{1,0:T(2,128)S(1)} %get-tuple-element.37.refs_0_, s32[2,384]{1,0:T(2,128)S(1)} %collective-permute-done.2.refs_1_, s32[2,384]{1,0:T(2,128)S(1)} %collective-permute-done.3.refs_2_, ...), custom_call_target="tpu_custom_call" | custom-call | flops 19327352832 | bytes 5242880 | tf_op jit(solution)/shard_map/pick/pallas_call | solution.py:183
  77.5 20.4 %collective-permute-done.15.refs_2_ = f32[192,512]{1,0:T(8,128)S(1)} collective-permute-done((f32[192,512]{1,0:T(8,128)S(1)}, f32[192,512]{1,0:T(8,128)S(1)}, u32[]{:S(2)}, u32[]{:S(2)}) %collective-permute-start.15) | collective-permute-done | bytes 393248 | tf_op jit(solution)/shard_map/ppermute | solution.py:525
  97.9 2.4 %place.3 = f32[512,512]{1,0:T(8,128)} custom-call(s32[3,512,128]{2,1,0:T(8,128)S(1)} %get-tuple-element.36.place_ref, f32[192,512]{1,0:T(8,128)S(1)} %get-tuple-element.52.refs_0_, f32[192,512]{1,0:T(8,128)S(1)} %collective-permute-done.14.refs_1_, f32[192,512]{1,0:T(8,128)S(1)} %collective-permute-done.15.refs_2_, ...), custom_call_target="tpu_custom_call" | custom-call | flops 19327352832 | bytes 3145728 | tf_op jit(solution)/shard_map/place/pallas_call | solution.py:221
  100.3 1.7 %collective-permute-start.17 = (f32[512,512]{1,0:T(8,128)}, f32[512,512]{1,0:T(8,128)}, u32[]{:S(2)}, u32[]{:S(2)}) collective-permute-start(f32[512,512]{1,0:T(8,128)} %place.3), channel_id=1, source_target_pairs={{8,16},{16,8},{9,17},{17,9},{10,18},{18,10},{11,19},{19,11},{12,20... | collective-permute-start | bytes 3145736 | tf_op jit(solution)/shard_map/ppermute | solution.py:538
  102.0 5.1 %collective-permute-start.18 = (f32[512,512]{1,0:T(8,128)}, f32[512,512]{1,0:T(8,128)}, u32[]{:S(2)}, u32[]{:S(2)}) collective-permute-start(f32[512,512]{1,0:T(8,128)} %place.3), channel_id=1, source_target_pairs={{0,8},{24,16},{1,9},{25,17},{2,10},{26,18},{3,11},{27,19},{4,12},{... | collective-permute-start | bytes 3145736 | tf_op jit(solution)/shard_map/ppermute | solution.py:537
  107.1 0.0 collective-permute-start.21
  107.1 0.4 collective-permute-start.20
  107.5 0.0 collective-permute-done.9.near_ref.refs_8_
  107.5 2.0 %collective-permute-start.19 = (f32[192,512]{1,0:T(8,128)}, f32[192,512]{1,0:T(8,128)}, u32[]{:S(2)}, u32[]{:S(2)}) collective-permute-start(f32[192,512]{1,0:T(8,128)} %get-tuple-element.60), channel_id=1, source_target_pairs={{0,2},{1,3},{2,4},{3,5},{4,6},{5,7},{6,0},{7,1},{8,10},{9,11},{10,... | collective-permute-start | bytes 1179656 | tf_op jit(solution)/shard_map/ppermute | solution.py:525
  109.6 3.4 %left_sums.1.so_far_ref = f32[8,512]{1,0:T(8,128)S(1)} custom-call(f32[1]{0:T(128)} %bitcast.2.sign_ref, f32[4]{0:T(128)S(1)} %copy-done.6, f32[512,512]{1,0:T(8,128)S(1)} %collective-permute-done.9.near_ref.refs_8_, f32[512,512]{1,0:T(8,128)} %collective-permute-done.17.far_ref.refs_9_, f32[512,1024]{1,0:T(8,128)S(1)} %bitcast.11, f32[1,512]{1,0:T(1,128)S(1)} %copy-done.4, ...), custom_call_target="tpu_custom_call" | custom-call | flops 15728640 | bytes 6291456 | tf_op jit(solution)/shard_map/left_sums/pallas_call | solution.py:308
  113.0 5.6 %collective-permute-done.21.refs_3_ = f32[192,512]{1,0:T(8,128)} collective-permute-done((f32[192,512]{1,0:T(8,128)}, f32[192,512]{1,0:T(8,128)}, u32[]{:S(2)}, u32[]{:S(2)}) %collective-permute-start.21) | collective-permute-done | bytes 393248 | tf_op jit(solution)/shard_map/ppermute | solution.py:525
  118.5 23.3 %collective-permute-done.20.refs_2_ = f32[192,512]{1,0:T(8,128)} collective-permute-done((f32[192,512]{1,0:T(8,128)}, f32[192,512]{1,0:T(8,128)}, u32[]{:S(2)}, u32[]{:S(2)}) %collective-permute-start.20) | collective-permute-done | bytes 393248 | tf_op jit(solution)/shard_map/ppermute | solution.py:525
  141.9 5.6 %right_sums.1 = (f32[8,512]{1,0:T(8,128)S(1)}, f32[512,512]{1,0:T(8,128)S(1)}) custom-call(s32[1]{0:T(128)} %bitcast.1.inner_ref, f32[1]{0:T(128)} %bitcast.2.sign_ref, s32[3,512,128]{2,1,0:T(8,128)S(1)} %copy-done.3, f32[512,512]{1,0:T(8,128)S(1)} %collective-permute-done.9.near_ref.refs_8_, f32[512,512]{1,0:T(8,128)} %collective-permute-done.17.far_ref.refs_9_, ...), custom_call_target="tpu_custom_call" | custom-call | flops 1207959552 | bytes 5242880 | tf_op jit(solution)/shard_map/right_sums/pallas_call | solution.py:344
  147.5 0.3 collective-permute-start.22
  147.8 2.0 %collective-permute-start.23 = (f32[8,512]{1,0:T(8,128)S(1)}, f32[8,512]{1,0:T(8,128)S(1)}, u32[]{:S(2)}, u32[]{:S(2)}) collective-permute-start(f32[8,512]{1,0:T(8,128)S(1)} %get-tuple-element.65), channel_id=1, source_target_pairs={{0,4},{1,5},{2,6},{3,7},{4,0},{5,1},{6,2},{7,3},{8,12},{9,13},{10,... | collective-permute-start | bytes 49160 | tf_op jit(solution)/shard_map/ppermute | solution.py:548
  149.8 2.8 %collective-permute-start.24 = (f32[8,512]{1,0:T(8,128)S(1)}, f32[8,512]{1,0:T(8,128)S(1)}, u32[]{:S(2)}, u32[]{:S(2)}) collective-permute-start(f32[8,512]{1,0:T(8,128)S(1)} %get-tuple-element.65), channel_id=1, source_target_pairs={{0,6},{1,7},{2,0},{3,1},{4,2},{5,3},{6,4},{7,5},{8,14},{9,15},{10,... | collective-permute-start | bytes 49160 | tf_op jit(solution)/shard_map/ppermute | solution.py:548
  152.6 0.6 collective-permute-done.22
  153.2 0.9 collective-permute-done.24
  154.1 0.0 collective-permute-start.25
  154.1 1.0 collective-permute-start.26
  155.1 1.9 %collective-permute-start.27 = (f32[32,512]{1,0:T(8,128)S(1)}, f32[32,512]{1,0:T(8,128)S(1)}, u32[]{:S(2)}, u32[]{:S(2)}) collective-permute-start(f32[32,512]{1,0:T(8,128)S(1)} %constant_dynamic-update-slice_fusion.refs_0_), channel_id=1, source_target_pairs={{0,24},{8,0},{16,8},{24,16},{1,25},{9,1},{17,9},{25,17},{2,26},{10... | collective-permute-start | bytes 196616 | tf_op jit(solution)/shard_map/ppermute | solution.py:545
  157.0 2.2 %collective-permute-done.25.refs_1_ = f32[32,512]{1,0:T(8,128)S(1)} collective-permute-done((f32[32,512]{1,0:T(8,128)S(1)}, f32[32,512]{1,0:T(8,128)S(1)}, u32[]{:S(2)}, u32[]{:S(2)}) %collective-permute-start.25) | collective-permute-done | bytes 65568 | tf_op jit(solution)/shard_map/ppermute | solution.py:545
  159.2 0.0 collective-permute-done.26.refs_2_
  159.3 0.5 collective-permute-start.30
  159.8 0.1 collective-permute-done.27.refs_3_
  159.8 0.0 collective-permute-start.31
  159.8 0.7 collective-permute-done.29.refs_5_
  160.5 0.2 collective-permute-done.30.refs_6_
  160.7 0.4 collective-permute-done.31.refs_7_
  161.1 5.4 %finish.1 = (f32[1,512]{1,0:T(1,128)}, f32[512,1024]{1,0:T(8,128)}) custom-call(s32[1]{0:T(128)} %bitcast.at_ref, s32[1]{0:T(128)} %bitcast.1.inner_ref, f32[1]{0:T(128)} %bitcast.2.sign_ref, f32[32,512]{1,0:T(8,128)S(1)} %constant_dynamic-update-slice_fusion.refs_0_, f32[32,512]{1,0:T(8,128)S(1)} %collective-permute-done.25.refs_1_, ...), custom_call_target="tpu_custom_call" | custom-call | tf_op jit(solution)/shard_map/finish/pallas_call | solution.py:443
  (31 shorter events, 0.1 us)
Async XLA Ops:
  1.4 7.8 %collective-permute-start = (s32[1,512]{1,0:T(1,128)S(1)}, s32[1,512]{1,0:T(1,128)S(1)}, u32[]{:S(2)}, u32[]{:S(2)}) collective-permute-start(s32[1,512]{1,0:T(1,128)S(1)} %get-tuple-element.71), channel_id=1, source_target_pairs={{0,8},{8,0},{16,24},{24,16},{1,9},{9,1},{17,25},{25,17},{2,10},{10... | collective-permute-start | bytes 6152 | tf_op jit(solution)/shard_map/ppermute | solution.py:490
  4.4 4.8 %collective-permute-start.1 = (s32[1,512]{1,0:T(1,128)S(1)}, s32[1,512]{1,0:T(1,128)S(1)}, u32[]{:S(2)}, u32[]{:S(2)}) collective-permute-start(s32[1,512]{1,0:T(1,128)S(1)} %get-tuple-element.70.own_ref), channel_id=1, source_target_pairs={{8,16},{16,8},{9,17},{17,9},{10,18},{18,10},{11,19},{19,11},{12,20... | collective-permute-start | bytes 6152 | tf_op jit(solution)/shard_map/ppermute | solution.py:490
  5.0 1.6 copy-start
  10.1 87.8 %copy-start.2 = (s32[3,512,128]{2,1,0:T(8,128)}, s32[3,512,128]{2,1,0:T(8,128)S(1)}, u32[]{:S(2)}) copy-start(s32[3,512,128]{2,1,0:T(8,128)S(1)} %get-tuple-element.36.place_ref) | copy-start | bytes 2359300
  10.1 7.9 %collective-permute-start.5 = (f32[512,512]{1,0:T(8,128)S(1)}, f32[512,512]{1,0:T(8,128)S(1)}, u32[]{:S(2)}, u32[]{:S(2)}) collective-permute-start(f32[512,512]{1,0:T(8,128)S(1)} %get-tuple-element.43.refs_4_), channel_id=1, source_target_pairs={{0,1},{1,0},{2,3},{3,2},{4,5},{5,4},{6,7},{7,6},{8,9},{9,8},{10,11... | collective-permute-start | bytes 3145736 | tf_op jit(solution)/shard_map/ppermute | solution.py:500
  10.1 5.6 %collective-permute-start.2 = (s32[2,384]{1,0:T(2,128)S(1)}, s32[2,384]{1,0:T(2,128)S(1)}, u32[]{:S(2)}, u32[]{:S(2)}) collective-permute-start(s32[2,384]{1,0:T(2,128)S(1)} %get-tuple-element.38), channel_id=1, source_target_pairs={{0,2},{1,3},{2,4},{3,5},{4,6},{5,7},{6,0},{7,1},{8,10},{9,11},{10,... | collective-permute-start | bytes 9224 | tf_op jit(solution)/shard_map/ppermute | solution.py:495
  11.8 4.7 %collective-permute-start.3 = (s32[2,384]{1,0:T(2,128)S(1)}, s32[2,384]{1,0:T(2,128)S(1)}, u32[]{:S(2)}, u32[]{:S(2)}) collective-permute-start(s32[2,384]{1,0:T(2,128)S(1)} %get-tuple-element.39), channel_id=1, source_target_pairs={{0,4},{1,5},{2,6},{3,7},{4,0},{5,1},{6,2},{7,3},{8,12},{9,13},{10,... | collective-permute-start | bytes 9224 | tf_op jit(solution)/shard_map/ppermute | solution.py:495
  14.3 3.6 %collective-permute-start.4 = (s32[2,384]{1,0:T(2,128)S(1)}, s32[2,384]{1,0:T(2,128)S(1)}, u32[]{:S(2)}, u32[]{:S(2)}) collective-permute-start(s32[2,384]{1,0:T(2,128)S(1)} %get-tuple-element.40), channel_id=1, source_target_pairs={{0,6},{1,7},{2,0},{3,1},{4,2},{5,3},{6,4},{7,5},{8,14},{9,15},{10,... | collective-permute-start | bytes 9224 | tf_op jit(solution)/shard_map/ppermute | solution.py:495
  15.7 7.0 %collective-permute-start.10 = (f32[512,512]{1,0:T(8,128)S(1)}, f32[512,512]{1,0:T(8,128)S(1)}, u32[]{:S(2)}, u32[]{:S(2)}) collective-permute-start(f32[512,512]{1,0:T(8,128)S(1)} %get-tuple-element.48.refs_6_), channel_id=1, source_target_pairs={{0,1},{1,0},{2,3},{3,2},{4,5},{5,4},{6,7},{7,6},{8,9},{9,8},{10,11... | collective-permute-start | bytes 3145736 | tf_op jit(solution)/shard_map/ppermute | solution.py:500
  15.7 23.1 %collective-permute-start.11 = (f32[512,512]{1,0:T(8,128)S(1)}, f32[512,512]{1,0:T(8,128)S(1)}, u32[]{:S(2)}, u32[]{:S(2)}) collective-permute-start(f32[512,512]{1,0:T(8,128)S(1)} %get-tuple-element.48.refs_6_), channel_id=1, source_target_pairs={{8,16},{16,8},{9,17},{17,9},{10,18},{18,10},{11,19},{19,11},{12,20... | collective-permute-start | bytes 3145736 | tf_op jit(solution)/shard_map/ppermute | solution.py:506
  16.4 51.9 %collective-permute-start.12 = (f32[512,512]{1,0:T(8,128)S(1)}, f32[512,512]{1,0:T(8,128)S(1)}, u32[]{:S(2)}, u32[]{:S(2)}) collective-permute-start(f32[512,512]{1,0:T(8,128)S(1)} %get-tuple-element.48.refs_6_), channel_id=1, source_target_pairs={{8,0},{16,24},{9,1},{17,25},{10,2},{18,26},{11,3},{19,27},{12,4},{... | collective-permute-start | bytes 3145736 | tf_op jit(solution)/shard_map/ppermute | solution.py:505
  19.5 19.3 %collective-permute-start.8 = (f32[192,512]{1,0:T(8,128)S(1)}, f32[192,512]{1,0:T(8,128)S(1)}, u32[]{:S(2)}, u32[]{:S(2)}) collective-permute-start(f32[192,512]{1,0:T(8,128)S(1)} %get-tuple-element.47), channel_id=1, source_target_pairs={{0,6},{1,7},{2,0},{3,1},{4,2},{5,3},{6,4},{7,5},{8,14},{9,15},{10,... | collective-permute-start | bytes 1179656 | tf_op jit(solution)/shard_map/ppermute | solution.py:525
  22.7 19.1 %collective-permute-start.6 = (f32[192,512]{1,0:T(8,128)S(1)}, f32[192,512]{1,0:T(8,128)S(1)}, u32[]{:S(2)}, u32[]{:S(2)}) collective-permute-start(f32[192,512]{1,0:T(8,128)S(1)} %get-tuple-element.45), channel_id=1, source_target_pairs={{0,2},{1,3},{2,4},{3,5},{4,6},{5,7},{6,0},{7,1},{8,10},{9,11},{10,... | collective-permute-start | bytes 1179656 | tf_op jit(solution)/shard_map/ppermute | solution.py:525
  22.7 34.8 %collective-permute-start.7 = (f32[192,512]{1,0:T(8,128)S(1)}, f32[192,512]{1,0:T(8,128)S(1)}, u32[]{:S(2)}, u32[]{:S(2)}) collective-permute-start(f32[192,512]{1,0:T(8,128)S(1)} %get-tuple-element.46), channel_id=1, source_target_pairs={{0,4},{1,5},{2,6},{3,7},{4,0},{5,1},{6,2},{7,3},{8,12},{9,13},{10,... | collective-permute-start | bytes 1179656 | tf_op jit(solution)/shard_map/ppermute | solution.py:525
  38.8 38.7 %collective-permute-start.16 = (f32[192,512]{1,0:T(8,128)S(1)}, f32[192,512]{1,0:T(8,128)S(1)}, u32[]{:S(2)}, u32[]{:S(2)}) collective-permute-start(f32[192,512]{1,0:T(8,128)S(1)} %get-tuple-element.58), channel_id=1, source_target_pairs={{0,6},{1,7},{2,0},{3,1},{4,2},{5,3},{6,4},{7,5},{8,14},{9,15},{10,... | collective-permute-start | bytes 1179656 | tf_op jit(solution)/shard_map/ppermute | solution.py:525
  68.5 6.5 %collective-permute-start.13 = (f32[512,512]{1,0:T(8,128)S(1)}, f32[512,512]{1,0:T(8,128)S(1)}, u32[]{:S(2)}, u32[]{:S(2)}) collective-permute-start(f32[512,512]{1,0:T(8,128)S(1)} %broadcast_select_fusion.refs_4_), channel_id=1, source_target_pairs={{0,1},{1,0},{2,3},{3,2},{4,5},{5,4},{6,7},{7,6},{8,9},{9,8},{10,11... | collective-permute-start | bytes 3145736 | tf_op jit(solution)/shard_map/ppermute | solution.py:500
  68.6 29.3 %collective-permute-start.15 = (f32[192,512]{1,0:T(8,128)S(1)}, f32[192,512]{1,0:T(8,128)S(1)}, u32[]{:S(2)}, u32[]{:S(2)}) collective-permute-start(f32[192,512]{1,0:T(8,128)S(1)} %get-tuple-element.56), channel_id=1, source_target_pairs={{0,4},{1,5},{2,6},{3,7},{4,0},{5,1},{6,2},{7,3},{8,12},{9,13},{10,... | collective-permute-start | bytes 1179656 | tf_op jit(solution)/shard_map/ppermute | solution.py:525
  68.9 29.0 %collective-permute-start.14 = (f32[192,512]{1,0:T(8,128)S(1)}, f32[192,512]{1,0:T(8,128)S(1)}, u32[]{:S(2)}, u32[]{:S(2)}) collective-permute-start(f32[192,512]{1,0:T(8,128)S(1)} %get-tuple-element.54), channel_id=1, source_target_pairs={{0,2},{1,3},{2,4},{3,5},{4,6},{5,7},{6,0},{7,1},{8,10},{9,11},{10,... | collective-permute-start | bytes 1179656 | tf_op jit(solution)/shard_map/ppermute | solution.py:525
  71.1 36.3 %collective-permute-start.9 = (f32[512,512]{1,0:T(8,128)S(1)}, f32[512,512]{1,0:T(8,128)S(1)}, u32[]{:S(2)}, u32[]{:S(2)}) collective-permute-start(f32[512,512]{1,0:T(8,128)S(1)} %place.2), channel_id=1, source_target_pairs={{0,8},{8,0},{16,24},{24,16},{1,9},{9,1},{17,25},{25,17},{2,10},{10... | collective-permute-start | bytes 3145736 | tf_op jit(solution)/shard_map/ppermute | solution.py:533
  77.5 32.0 %copy-start.1 = (f32[1,512,1024]{2,1,0:T(8,128)S(1)}, f32[1,512,1024]{2,1,0:T(8,128)}, u32[]{:S(2)}) copy-start(f32[1,512,1024]{2,1,0:T(8,128)} %param.6) | copy-start | bytes 6291460
  77.5 32.0 %copy-start.4 = (f32[1,512]{1,0:T(1,128)S(1)}, f32[1,512]{1,0:T(1,128)}, u32[]{:S(2)}) copy-start(f32[1,512]{1,0:T(1,128)} %start_ref.1) | copy-start | bytes 6148
  77.5 32.0 %copy-start.5 = (s32[1,512]{1,0:T(1,128)S(1)}, s32[1,512]{1,0:T(1,128)}, u32[]{:S(2)}) copy-start(s32[1,512]{1,0:T(1,128)} %class_ref.1) | copy-start | bytes 6148
  77.5 32.0 %copy-start.6 = (f32[4]{0:T(128)S(1)}, f32[4]{0:T(128)}, u32[]{:S(2)}) copy-start(f32[4]{0:T(128)} %table_ref.1) | copy-start | bytes 52
  100.3 9.2 %collective-permute-start.17 = (f32[512,512]{1,0:T(8,128)}, f32[512,512]{1,0:T(8,128)}, u32[]{:S(2)}, u32[]{:S(2)}) collective-permute-start(f32[512,512]{1,0:T(8,128)} %place.3), channel_id=1, source_target_pairs={{8,16},{16,8},{9,17},{17,9},{10,18},{18,10},{11,19},{19,11},{12,20... | collective-permute-start | bytes 3145736 | tf_op jit(solution)/shard_map/ppermute | solution.py:538
  102.0 39.9 %collective-permute-start.18 = (f32[512,512]{1,0:T(8,128)}, f32[512,512]{1,0:T(8,128)}, u32[]{:S(2)}, u32[]{:S(2)}) collective-permute-start(f32[512,512]{1,0:T(8,128)} %place.3), channel_id=1, source_target_pairs={{0,8},{24,16},{1,9},{25,17},{2,10},{26,18},{3,11},{27,19},{4,12},{... | collective-permute-start | bytes 3145736 | tf_op jit(solution)/shard_map/ppermute | solution.py:537
  107.1 11.4 %collective-permute-start.21 = (f32[192,512]{1,0:T(8,128)}, f32[192,512]{1,0:T(8,128)}, u32[]{:S(2)}, u32[]{:S(2)}) collective-permute-start(f32[192,512]{1,0:T(8,128)} %get-tuple-element.64), channel_id=1, source_target_pairs={{0,6},{1,7},{2,0},{3,1},{4,2},{5,3},{6,4},{7,5},{8,14},{9,15},{10,... | collective-permute-start | bytes 1179656 | tf_op jit(solution)/shard_map/ppermute | solution.py:525
  107.1 34.8 %collective-permute-start.20 = (f32[192,512]{1,0:T(8,128)}, f32[192,512]{1,0:T(8,128)}, u32[]{:S(2)}, u32[]{:S(2)}) collective-permute-start(f32[192,512]{1,0:T(8,128)} %get-tuple-element.62), channel_id=1, source_target_pairs={{0,4},{1,5},{2,6},{3,7},{4,0},{5,1},{6,2},{7,3},{8,12},{9,13},{10,... | collective-permute-start | bytes 1179656 | tf_op jit(solution)/shard_map/ppermute | solution.py:525
  107.5 34.4 %collective-permute-start.19 = (f32[192,512]{1,0:T(8,128)}, f32[192,512]{1,0:T(8,128)}, u32[]{:S(2)}, u32[]{:S(2)}) collective-permute-start(f32[192,512]{1,0:T(8,128)} %get-tuple-element.60), channel_id=1, source_target_pairs={{0,2},{1,3},{2,4},{3,5},{4,6},{5,7},{6,0},{7,1},{8,10},{9,11},{10,... | collective-permute-start | bytes 1179656 | tf_op jit(solution)/shard_map/ppermute | solution.py:525
  109.5 32.3 %copy-start.3 = (s32[3,512,128]{2,1,0:T(8,128)S(1)}, s32[3,512,128]{2,1,0:T(8,128)}, u32[]{:S(2)}) copy-start(s32[3,512,128]{2,1,0:T(8,128)} %copy-done.2) | copy-start | bytes 2359300
  147.5 5.7 %collective-permute-start.22 = (f32[8,512]{1,0:T(8,128)S(1)}, f32[8,512]{1,0:T(8,128)S(1)}, u32[]{:S(2)}, u32[]{:S(2)}) collective-permute-start(f32[8,512]{1,0:T(8,128)S(1)} %get-tuple-element.65), channel_id=1, source_target_pairs={{0,2},{1,3},{2,4},{3,5},{4,6},{5,7},{6,0},{7,1},{8,10},{9,11},{10,... | collective-permute-start | bytes 49160 | tf_op jit(solution)/shard_map/ppermute | solution.py:548
  147.8 5.4 %collective-permute-start.23 = (f32[8,512]{1,0:T(8,128)S(1)}, f32[8,512]{1,0:T(8,128)S(1)}, u32[]{:S(2)}, u32[]{:S(2)}) collective-permute-start(f32[8,512]{1,0:T(8,128)S(1)} %get-tuple-element.65), channel_id=1, source_target_pairs={{0,4},{1,5},{2,6},{3,7},{4,0},{5,1},{6,2},{7,3},{8,12},{9,13},{10,... | collective-permute-start | bytes 49160 | tf_op jit(solution)/shard_map/ppermute | solution.py:548
  149.8 4.3 %collective-permute-start.24 = (f32[8,512]{1,0:T(8,128)S(1)}, f32[8,512]{1,0:T(8,128)S(1)}, u32[]{:S(2)}, u32[]{:S(2)}) collective-permute-start(f32[8,512]{1,0:T(8,128)S(1)} %get-tuple-element.65), channel_id=1, source_target_pairs={{0,6},{1,7},{2,0},{3,1},{4,2},{5,3},{6,4},{7,5},{8,14},{9,15},{10,... | collective-permute-start | bytes 49160 | tf_op jit(solution)/shard_map/ppermute | solution.py:548
  154.1 5.2 %collective-permute-start.25 = (f32[32,512]{1,0:T(8,128)S(1)}, f32[32,512]{1,0:T(8,128)S(1)}, u32[]{:S(2)}, u32[]{:S(2)}) collective-permute-start(f32[32,512]{1,0:T(8,128)S(1)} %constant_dynamic-update-slice_fusion.refs_0_), channel_id=1, source_target_pairs={{0,8},{8,16},{16,24},{24,0},{1,9},{9,17},{17,25},{25,1},{2,10},{10... | collective-permute-start | bytes 196616 | tf_op jit(solution)/shard_map/ppermute | solution.py:545
  154.1 5.2 %collective-permute-start.26 = (f32[32,512]{1,0:T(8,128)S(1)}, f32[32,512]{1,0:T(8,128)S(1)}, u32[]{:S(2)}, u32[]{:S(2)}) collective-permute-start(f32[32,512]{1,0:T(8,128)S(1)} %constant_dynamic-update-slice_fusion.refs_0_), channel_id=1, source_target_pairs={{0,16},{8,24},{16,0},{24,8},{1,17},{9,25},{17,1},{25,9},{2,18},{10... | collective-permute-start | bytes 196616 | tf_op jit(solution)/shard_map/ppermute | solution.py:545
  155.1 4.7 %collective-permute-start.27 = (f32[32,512]{1,0:T(8,128)S(1)}, f32[32,512]{1,0:T(8,128)S(1)}, u32[]{:S(2)}, u32[]{:S(2)}) collective-permute-start(f32[32,512]{1,0:T(8,128)S(1)} %constant_dynamic-update-slice_fusion.refs_0_), channel_id=1, source_target_pairs={{0,24},{8,0},{16,8},{24,16},{1,25},{9,1},{17,9},{25,17},{2,26},{10... | collective-permute-start | bytes 196616 | tf_op jit(solution)/shard_map/ppermute | solution.py:545
  157.0 2.8 %collective-permute-start.28 = (f32[32,512]{1,0:T(8,128)S(1)}, f32[32,512]{1,0:T(8,128)S(1)}, u32[]{:S(2)}, u32[]{:S(2)}) collective-permute-start(f32[32,512]{1,0:T(8,128)S(1)} %constant_dynamic-update-slice_fusion.refs_0_), channel_id=1, source_target_pairs={{0,1},{1,0},{2,3},{3,2},{4,5},{5,4},{6,7},{7,6},{8,9},{9,8},{10,11... | collective-permute-start | bytes 196616 | tf_op jit(solution)/shard_map/ppermute | solution.py:500
  159.2 1.3 collective-permute-start.29
  159.3 1.4 collective-permute-start.30
  159.8 1.3 collective-permute-start.31

commit v4 on v3

--- a/solution.py
+++ b/solution.py
@@ -263,36 +263,32 @@
     return jnp.concatenate(sums, axis=1)
 
 
-def row_sums(sign, near, far, voxels, counted):
-    voxels = counted(voxels)
-    value, slope, bend = taylor(near, counted)
-    other_value, other_slope, other_bend = taylor(far, counted)
-    value = value - voxels
-    other_value = other_value - voxels
+def row_sums(sign, stream, voxels, counted):
+    value, slope, bend = taylor(stream, counted)
+    value = value - counted(voxels)
     slope = sign * slope
-    other_slope = -sign * other_slope
-    c0 = slope * slope + other_slope * other_slope
+    c0 = slope * slope
     return (
-        lanes(slope * value + other_slope * other_value),
-        lanes(c0 + bend * value + other_bend * other_value),
+        lanes(slope * value),
+        lanes(c0 + bend * value),
         lanes(c0),
-        lanes(2.0 * (slope * bend + other_slope * other_bend)),
-        lanes(bend * bend + other_bend * other_bend),
+        lanes(2.0 * (slope * bend)),
+        lanes(bend * bend),
     )
 
 
 STEP = 128
 
 
-def left_sums_kernel(sign_ref, table_ref, near_ref, far_ref, vol_ref, start_ref, class_ref, out_ref):
+def all_but_last(values):
+    return on_tile(values, values.shape[1] - 128, cleared(127))
+
+
+def near_sums_kernel(sign_ref, table_ref, near_ref, vol_ref, start_ref, class_ref, out_ref):
     rows, half = near_ref.shape
-
-    def counted(values):
-        return on_tile(values, half - 128, cleared(127))
-
     for start in range(0, rows, STEP):
         at = slice(start, start + STEP)
-        lines = row_sums(sign_ref[0], near_ref[at], far_ref[at], vol_ref[at, :half], counted)
+        lines = row_sums(sign_ref[0], near_ref[at], vol_ref[at, :half], all_but_last)
         for number, line in enumerate(lines):
             out_ref[number : number + 1, at] = line
     weight = jnp.zeros(start_ref.shape, jnp.float32)
@@ -303,17 +299,40 @@
     out_ref[7:8, :] = jnp.zeros(start_ref.shape, jnp.float32)
 
 
-def left_sums(sign, table, near, far, voxels, start, classes):
+def near_sums(sign, table, near, voxels, start, classes):
     rows, half = near.shape
     return pl.pallas_call(
-        left_sums_kernel,
-        in_specs=[SMEM, SMEM] + [VMEM] * 5,
+        near_sums_kernel,
+        in_specs=[SMEM, SMEM] + [VMEM] * 4,
         out_specs=VMEM,
         out_shape=jax.ShapeDtypeStruct((FIELDS, rows), jnp.float32),
-        cost_estimate=cost(60 * rows * half, 6 * rows * half),
-        compiler_params=LIMIT,
-        name="left_sums",
-    )(sign, table, near, far, voxels, start, classes)
+        cost_estimate=cost(HINT * 5000 * rows * half, 5 * rows * half),
+        compiler_params=LIMIT,
+        name="near_sums",
+    )(sign, table, near, voxels, start, classes)
+
+
+def far_sums_kernel(sign_ref, far_ref, vol_ref, so_far_ref, out_ref):
+    rows, half = far_ref.shape
+    for start in range(0, rows, STEP):
+        at = slice(start, start + STEP)
+        lines = row_sums(-sign_ref[0], far_ref[at], vol_ref[at, :half], all_but_last)
+        for number, line in enumerate(lines):
+            out_ref[number : number + 1, at] = so_far_ref[number : number + 1, at] + line
+    out_ref[5:8, :] = so_far_ref[5:8, :]
+
+
+def far_sums(sign, far, voxels, so_far):
+    rows, half = far.shape
+    return pl.pallas_call(
+        far_sums_kernel,
+        in_specs=[SMEM] + [VMEM] * 3,
+        out_specs=VMEM,
+        out_shape=jax.ShapeDtypeStruct((FIELDS, rows), jnp.float32),
+        cost_estimate=cost(60 * rows * half, 5 * rows * half),
+        compiler_params=LIMIT,
+        name="far_sums",
+    )(sign, far, voxels, so_far)
 
 
 def right_sums_kernel(inner_ref, sign_ref, place_ref, near_ref, far_ref, hop_ref, vol_ref, so_far_ref, *refs):
@@ -332,9 +351,10 @@
         third = third_ref[at]
         near = jnp.concatenate([near_ref[at, half - 128 :], jnp.where(inner, hop_ref[at], third)], axis=1)
         far = jnp.concatenate([far_ref[at, half - 128 :], jnp.where(inner, third, 0.0)], axis=1)
-        lines = row_sums(sign_ref[0], near, far, vol_ref[at, half - 128 :], counted)
-        for number, line in enumerate(lines):
-            fields_ref[number : number + 1, at] = so_far_ref[number : number + 1, at] + line
+        voxels = vol_ref[at, half - 128 :]
+        lines = zip(row_sums(sign_ref[0], near, voxels, counted), row_sums(-sign_ref[0], far, voxels, counted))
+        for number, (line, other) in enumerate(lines):
+            fields_ref[number : number + 1, at] = so_far_ref[number : number + 1, at] + line + other
     fields_ref[5:8, :] = so_far_ref[5:8, :]
 
 
@@ -395,11 +415,37 @@
     return velocities[0]
 
 
-def final_kernel(chips, at_ref, inner_ref, sign_ref, *refs):
-    fields_refs = refs[:-10]
-    near_ref, far_ref, hop_ref, third_ref, vol_ref, velocity_ref, misfit_ref = refs[-10:-3]
-    fields_ref, tile_ref, sent = refs[-3:]
-    rows, half = near_ref.shape
+def shape_kernel(inner_ref, sign_ref, near_ref, far_ref, hop_ref, third_ref, vol_ref, flat_ref, tilt_ref, curl_ref):
+    inner = inner_ref[0] != 0
+    for start in range(0, near_ref.shape[0], STEP):
+        at = slice(start, start + STEP)
+        third = third_ref[at]
+        near = jnp.concatenate([near_ref[at], jnp.where(inner, hop_ref[at], third)], axis=1)
+        far = jnp.concatenate([far_ref[at], jnp.where(inner, third, 0.0)], axis=1)
+        both, drift = near + far, (0.5 * sign_ref[0]) * (near - far)
+        bend = after_of(both) - 2.0 * both + before_of(both)
+        flat_ref[at] = both + bend * (1.0 / 6.0) - 2.0 * vol_ref[at]
+        tilt_ref[at] = after_of(drift) - before_of(drift)
+        curl_ref[at] = 0.5 * bend
+
+
+def shapes(inner, sign, streams, voxels):
+    rows, columns = voxels.shape
+    return pl.pallas_call(
+        shape_kernel,
+        in_specs=[SMEM, SMEM] + [VMEM] * 5,
+        out_specs=[VMEM] * 3,
+        out_shape=[jax.ShapeDtypeStruct((rows, columns), jnp.float32)] * 3,
+        cost_estimate=cost(30 * rows * columns, 7 * rows * columns),
+        compiler_params=LIMIT,
+        name="shapes",
+    )(inner, sign, *streams, voxels)
+
+
+def final_kernel(chips, at_ref, *refs):
+    fields_refs = refs[:-8]
+    flat_ref, tilt_ref, curl_ref, velocity_ref, misfit_ref, fields_ref, tile_ref, sent = refs[-8:]
+    rows, columns = flat_ref.shape
     if chips:
         scans = len(fields_refs) // 2
         for number, ref in enumerate(fields_refs):
@@ -415,34 +461,24 @@
     own = jnp.sum(jnp.where(slab == at_ref[0], velocity, 0.0), axis=0, keepdims=True)
     velocity_ref[...] = own
 
-    inner = inner_ref[0] != 0
     copies = []
     for number, start in enumerate(range(0, rows, STEP)):
         at = slice(start, start + STEP)
-        moved = column(own[:, at])
-        weight = 1.0 / 6.0 + 0.5 * moved * moved
-        drift = (0.5 * sign_ref[0]) * moved
-        wide = lambda tile: jnp.concatenate([tile] * (2 * half // 128), axis=1)
-        up, down, middle = wide(weight + drift), wide(weight - drift), wide(1.0 - 2.0 * weight)
-        third = third_ref[at]
-        near = jnp.concatenate([near_ref[at], jnp.where(inner, hop_ref[at], third)], axis=1)
-        far = jnp.concatenate([far_ref[at], jnp.where(inner, third, 0.0)], axis=1)
-        after = after_of(up * near + down * far)
-        before = before_of(down * near + up * far)
-        tile_ref[number] = middle * (near + far) + after + before - 2.0 * vol_ref[at]
+        moved = jnp.concatenate([column(own[:, at])] * (columns // 128), axis=1)
+        tile_ref[number] = flat_ref[at] + moved * (tilt_ref[at] + moved * curl_ref[at])
         copies.append(pltpu.make_async_copy(tile_ref.at[number], misfit_ref.at[pl.ds(start, STEP)], sent.at[number]))
         copies[-1].start()
     for copy in copies:
         copy.wait()
 
 
-def finish(at, inner, sign, groups, streams, voxels, chips):
-    rows, columns = voxels.shape
+def finish(at, groups, parts, chips):
+    rows, columns = parts[0].shape
     steps = rows // STEP
     shape = (len(groups) // 2, 2 * chips, FIELDS, rows) if chips else (1, 1, 8, 128)
     return pl.pallas_call(
         functools.partial(final_kernel, chips),
-        in_specs=[SMEM, SMEM, SMEM] + [VMEM] * (len(groups) + 5),
+        in_specs=[SMEM] + [VMEM] * (len(groups) + 3),
         out_specs=[VMEM, pl.BlockSpec(memory_space=pl.ANY)],
         out_shape=[
             jax.ShapeDtypeStruct((1, rows), jnp.float32),
@@ -455,7 +491,7 @@
         ],
         compiler_params=LIMIT,
         name="finish",
-    )(at, inner, sign, *groups, *streams, voxels)
+    )(at, *groups, *parts)
 
 
 def swapped(block, axis):
@@ -464,9 +500,6 @@
 
 def after(block, *earlier):
     return lax.optimization_barrier((block, *earlier))[0]
-
-
-ORDER = (2, 1, 3)
 
 
 def on_device(volume, velocity0, fetch_slab, fetch_row, modulus_class, modulus_table):
@@ -514,45 +547,48 @@
 
     sent = []
 
-    def fetched(blocks):
+    def fetched(blocks, order, before_last=()):
         if not direct:
             arrived = swapped(blocks[0].reshape(slabs, capacity, -1), "slab")
             return [arrived.reshape(slabs * capacity, -1)]
         arrived = [blocks[0]] + [None] * (chips - 1)
-        for turn in ORDER:
-            held = sent[-3:-2]
+        for turn in order:
+            held = sent[-3:-2] + (list(before_last) if turn == order[-1] else [])
             block = after(blocks[turn], *held) if held else blocks[turn]
             arrived[turn] = lax.ppermute(block, "slab", turns[turn])
             sent.append(arrived[turn])
         return arrived
 
-    blocks = picks(0, [left, left_other])
-    arrived = fetched(blocks)
+    order = (2, 1, 3)
+    arrived = fetched(picks(0, [left, left_other]), order)
     first = place(0, places, arrived)
     lender = jnp.where(inner == 1, after(from_middle, *arrived), from_inner)
     near = lax.ppermute(first, "scan", sides)
-    arrived = fetched(picks(1, [left, left_other, right, right_other]))
+    arrived2 = fetched(picks(1, [left, left_other, right, right_other]), order)
     blocks = picks(2, [lender, other_core(lender)])
-    second = place(1, places, [after(arrived[0], blocks[0]), *arrived[1:]])
+    second = place(1, places, [after(arrived2[0], blocks[0]), *arrived2[1:]])
+    order = (1, 2, 3)
+    arrived = fetched(blocks, order)
     hop = lax.ppermute(second, "scan", [(0, 1), (3, 2)])
     far = lax.ppermute(second, "scan", middle)
-    arrived = fetched(blocks)
-    so_far = left_sums(sign, modulus_table, near, far, voxels, velocity0, modulus_class)
+    begun = arrived[1:2] if direct else arrived
+    so_far = near_sums(sign, modulus_table, after(near, *begun), voxels, velocity0, modulus_class)
+    so_far = far_sums(sign, far, voxels, so_far)
     sums, third = right_sums(inner, sign, places, near, far, hop, voxels, so_far, arrived)
 
     def scans_of(block):
         routes = [[(p, (p + turn) % scans) for p in range(scans)] for turn in range(1, scans)]
         return [block] + [lax.ppermute(block, "scan", route) for route in routes]
 
+    parts = shapes(inner, sign, (near, far, hop, third), voxels)
     if direct:
         line = jnp.concatenate([sums] + [lax.ppermute(sums, "slab", route) for route in turns[1:]], axis=0)
+        line = after(line, parts[0])
         groups = scans_of(line)
         groups += [other_core(group) for group in groups]
     else:
         groups = scans_of(swapped(jnp.broadcast_to(sums[None], (slabs, FIELDS, rows)), "slab"))
-    velocity, misfit = finish(
-        at, inner, sign, groups, (near, far, hop, third), after(voxels, sums), chips if direct else 0
-    )
+    velocity, misfit = finish(at, groups, parts, chips if direct else 0)
     return velocity, misfit[None]
 
 

time: 168 us -> 160 us (0.952)
  waiting for transfers between devices: 97.4 us -> 84.9 us
  starting transfers between devices: 38.4 us -> 45 us
    ppermute x9, waiting for transfers between devices: 81.4 us -> 71.6 us  [fetched(): arrived[turn] = lax.ppermute(block, 'slab', turns[turn])]
    ppermute x1, starting transfers between devices: 5.11 us -> 8.01 us  [on_device(): hop = lax.ppermute(second, 'scan', [(0, 1), (3, 2)])]
    pallas_call x2 -> x4, Pallas kernels: 8.81 us -> 8.99 us  [the longest x1 3.02 us: finish(): pl.pallas_call(functools.partial(final_kernel, chips), in_specs=[SMEM] +...]
  transfers between devices with their start and end apart: 32 -> 32, of which waited for: 15 -> 14; matrix products, arithmetic and copies ran while one was open for 0% -> 0% of each run, Pallas kernels for 9% -> 12%
where the time goes in v4:
time: 160 us
  waiting for transfers between devices  84.9 us (53%)
  starting transfers between devices  45 us (28%)
  Pallas kernels  26.4 us (16%)
  local copies, waits for them, and re-layouts  1.6 us (1%)
    ppermute x9, waiting for transfers between devices, fetched(): arrived[turn] = lax.ppermute(block, 'slab', turns[turn])  71.6 us
    ppermute x1, waiting for transfers between devices, on_device(): from_inner = lax.ppermute(right, 'scan', [(1, 0), (2, 3)])  9.57 us
    ppermute x9, starting transfers between devices, fetched(): arrived[turn] = lax.ppermute(block, 'slab', turns[turn])  9.41 us
    ppermute x1, starting transfers between devices, on_device(): hop = lax.ppermute(second, 'scan', [(0, 1), (3, 2)])  8.01 us
    pallas_call x3, Pallas kernels, pick(): pl.pallas_call(functools.partial(pick_kernel, chips, capacity, number), i...  7.1 us
    ppermute x3, starting transfers between devices, on_device(): lax.ppermute(tables[turn], 'slab', turns[turn])  5.57 us
    ppermute x3, starting transfers between devices, on_device(): lax.ppermute(sums, 'slab', route)  5.37 us
    ppermute x1, starting transfers between devices, on_device(): near = lax.ppermute(first, 'scan', sides)  5.05 us
  transfers between devices with their start and end apart: 32, of which 14 were waited for; matrix products, arithmetic and copies ran while one was open for 0% of the time, Pallas kernels for 12%

profile of v4, /device:TPU:0, one launch (start us, length us, event | category | flops | bytes accessed | tf_op | source)
XLA Modules:
  0.0 160.0 jit_solution(8244586370874116431)
XLA Ops:
  0.6 0.7 bitcast_add_fusion.early_ref
  1.4 3.0 %collective-permute-start = (s32[1,512]{1,0:T(1,128)S(1)}, s32[1,512]{1,0:T(1,128)S(1)}, u32[]{:S(2)}, u32[]{:S(2)}) collective-permute-start(s32[1,512]{1,0:T(1,128)S(1)} %get-tuple-element.79), channel_id=1, source_target_pairs={{0,8},{8,0},{16,24},{24,16},{1,9},{9,1},{17,25},{25,17},{2,10},{10... | collective-permute-start | bytes 6152 | tf_op jit(solution)/shard_map/ppermute | solution.py:523
  4.4 0.6 collective-permute-start.1
  5.0 0.0 copy-start
  5.0 1.6 copy-done
  6.6 2.5 %prefilter.1 = (f32[512,512]{1,0:T(8,128)S(1)}, f32[512,512]{1,0:T(8,128)S(1)}) custom-call(f32[512,1024]{1,0:T(8,128)S(1)} %bitcast.10, s32[2,512]{1,0:T(2,128)S(1)} %bitcast_add_fusion.early_ref), custom_call_target="tpu_custom_call" | custom-call | flops 1610612736 | bytes 4194304 | tf_op jit(solution)/shard_map/prefilter/pallas_call | solution.py:73
  9.2 0.0 collective-permute-done.1.inward_ref
  9.2 0.9 requests.1
  10.1 0.0 collective-permute-start.5
  10.1 1.6 %collective-permute-start.2 = (s32[2,384]{1,0:T(2,128)S(1)}, s32[2,384]{1,0:T(2,128)S(1)}, u32[]{:S(2)}, u32[]{:S(2)}) collective-permute-start(s32[2,384]{1,0:T(2,128)S(1)} %get-tuple-element.42), channel_id=1, source_target_pairs={{0,2},{1,3},{2,4},{3,5},{4,6},{5,7},{6,0},{7,1},{8,10},{9,11},{10,... | collective-permute-start | bytes 9224 | tf_op jit(solution)/shard_map/ppermute | solution.py:528
  11.7 2.6 %collective-permute-start.3 = (s32[2,384]{1,0:T(2,128)S(1)}, s32[2,384]{1,0:T(2,128)S(1)}, u32[]{:S(2)}, u32[]{:S(2)}) collective-permute-start(s32[2,384]{1,0:T(2,128)S(1)} %get-tuple-element.43), channel_id=1, source_target_pairs={{0,4},{1,5},{2,6},{3,7},{4,0},{5,1},{6,2},{7,3},{8,12},{9,13},{10,... | collective-permute-start | bytes 9224 | tf_op jit(solution)/shard_map/ppermute | solution.py:528
  14.3 1.4 collective-permute-start.4
  15.7 0.0 collective-permute-start.10
  15.7 0.0 collective-permute-done.2.refs_1_
  15.7 0.7 collective-permute-start.11
  16.4 0.0 collective-permute-done.3.refs_2_
  16.4 1.3 collective-permute-start.12
  17.7 0.2 collective-permute-done.4.refs_3_
  17.9 0.0 collective-permute-done.5.refs_5_
  17.9 2.8 %pick.3 = (f32[192,512]{1,0:T(8,128)S(1)}, f32[192,512]{1,0:T(8,128)S(1)}, f32[192,512]{1,0:T(8,128)S(1)}, f32[192,512]{1,0:T(8,128)S(1)}) custom-call(s32[1]{0:T(128)} %bitcast.1.inner_ref, s32[2,384]{1,0:T(2,128)S(1)} %get-tuple-element.41.refs_0_, s32[2,384]{1,0:T(2,128)S(1)} %collective-permute-done.2.refs_1_, ...), custom_call_target="tpu_custom_call" | custom-call | flops 19327352832 | bytes 5242880 | tf_op jit(solution)/shard_map/pick/pallas_call | solution.py:183
  20.7 3.2 %collective-permute-start.8 = (f32[192,512]{1,0:T(8,128)S(1)}, f32[192,512]{1,0:T(8,128)S(1)}, u32[]{:S(2)}, u32[]{:S(2)}) collective-permute-start(f32[192,512]{1,0:T(8,128)S(1)} %get-tuple-element.51), channel_id=1, source_target_pairs={{0,6},{1,7},{2,0},{3,1},{4,2},{5,3},{6,4},{7,5},{8,14},{9,15},{10,... | collective-permute-start | bytes 1179656 | tf_op jit(solution)/shard_map/ppermute | solution.py:558
  23.9 0.0 collective-permute-start.6
  23.9 0.0 collective-permute-done.10.refs_7_
  23.9 1.1 collective-permute-start.7
  25.0 2.8 %pick.4 = (f32[192,512]{1,0:T(8,128)S(1)}, f32[192,512]{1,0:T(8,128)S(1)}, f32[192,512]{1,0:T(8,128)S(1)}, f32[192,512]{1,0:T(8,128)S(1)}) custom-call(s32[1]{0:T(128)} %bitcast.1.inner_ref, s32[2,384]{1,0:T(2,128)S(1)} %get-tuple-element.41.refs_0_, s32[2,384]{1,0:T(2,128)S(1)} %collective-permute-done.2.refs_1_, ...), custom_call_target="tpu_custom_call" | custom-call | flops 19327352832 | bytes 5242880 | tf_op jit(solution)/shard_map/pick/pallas_call | solution.py:183
  27.8 12.2 %collective-permute-done.8.refs_3_ = f32[192,512]{1,0:T(8,128)S(1)} collective-permute-done((f32[192,512]{1,0:T(8,128)S(1)}, f32[192,512]{1,0:T(8,128)S(1)}, u32[]{:S(2)}, u32[]{:S(2)}) %collective-permute-start.8) | collective-permute-done | bytes 393248 | tf_op jit(solution)/shard_map/ppermute | solution.py:558
  40.0 0.0 collective-permute-start.16
  40.0 0.0 collective-permute-done.11
  40.0 3.0 %collective-permute-done.6.refs_1_ = f32[192,512]{1,0:T(8,128)S(1)} collective-permute-done((f32[192,512]{1,0:T(8,128)S(1)}, f32[192,512]{1,0:T(8,128)S(1)}, u32[]{:S(2)}, u32[]{:S(2)}) %collective-permute-start.6) | collective-permute-done | bytes 393248 | tf_op jit(solution)/shard_map/ppermute | solution.py:558
  43.0 15.7 %collective-permute-done.7.refs_2_ = f32[192,512]{1,0:T(8,128)S(1)} collective-permute-done((f32[192,512]{1,0:T(8,128)S(1)}, f32[192,512]{1,0:T(8,128)S(1)}, u32[]{:S(2)}, u32[]{:S(2)}) %collective-permute-start.7) | collective-permute-done | bytes 393248 | tf_op jit(solution)/shard_map/ppermute | solution.py:558
  58.7 9.6 %collective-permute-done.12 = f32[512,512]{1,0:T(8,128)S(1)} collective-permute-done((f32[512,512]{1,0:T(8,128)S(1)}, f32[512,512]{1,0:T(8,128)S(1)}, u32[]{:S(2)}, u32[]{:S(2)}) %collective-permute-start.12) | collective-permute-done | bytes 1048608 | tf_op jit(solution)/shard_map/ppermute | solution.py:538
  68.3 0.2 broadcast_select_fusion.refs_4_
  68.5 0.1 collective-permute-start.13
  68.6 0.7 collective-permute-start.14
  69.3 0.3 collective-permute-start.15
  69.7 1.4 place.2
  71.1 5.0 %collective-permute-start.9 = (f32[512,512]{1,0:T(8,128)S(1)}, f32[512,512]{1,0:T(8,128)S(1)}, u32[]{:S(2)}, u32[]{:S(2)}) collective-permute-start(f32[512,512]{1,0:T(8,128)S(1)} %place.2), channel_id=1, source_target_pairs={{0,8},{8,0},{16,24},{24,16},{1,9},{9,1},{17,25},{25,17},{2,10},{10... | collective-permute-start | bytes 3145736 | tf_op jit(solution)/shard_map/ppermute | solution.py:566
  76.2 1.5 pick.5
  77.7 20.5 %collective-permute-done.15.refs_2_ = f32[192,512]{1,0:T(8,128)S(1)} collective-permute-done((f32[192,512]{1,0:T(8,128)S(1)}, f32[192,512]{1,0:T(8,128)S(1)}, u32[]{:S(2)}, u32[]{:S(2)}) %collective-permute-start.15) | collective-permute-done | bytes 393248 | tf_op jit(solution)/shard_map/ppermute | solution.py:558
  98.2 0.0 collective-permute-start.19
  98.3 0.0 copy-start.4
  98.3 1.4 place.3
  99.8 0.7 collective-permute-start.17
  100.5 8.0 %collective-permute-start.18 = (f32[512,512]{1,0:T(8,128)S(1)}, f32[512,512]{1,0:T(8,128)S(1)}, u32[]{:S(2)}, u32[]{:S(2)}) collective-permute-start(f32[512,512]{1,0:T(8,128)S(1)} %place.3), channel_id=1, source_target_pairs={{0,8},{24,16},{1,9},{25,17},{2,10},{26,18},{3,11},{27,19},{4,12},{... | collective-permute-start | bytes 3145736 | tf_op jit(solution)/shard_map/ppermute | solution.py:572
  108.5 4.0 %collective-permute-start.21 = (f32[192,512]{1,0:T(8,128)S(1)}, f32[192,512]{1,0:T(8,128)S(1)}, u32[]{:S(2)}, u32[]{:S(2)}) collective-permute-start(f32[192,512]{1,0:T(8,128)S(1)} %get-tuple-element.69), channel_id=1, source_target_pairs={{0,6},{1,7},{2,0},{3,1},{4,2},{5,3},{6,4},{7,5},{8,14},{9,15},{10,... | collective-permute-start | bytes 1179656 | tf_op jit(solution)/shard_map/ppermute | solution.py:558
  112.6 1.8 %near_sums.1.so_far_ref = f32[8,512]{1,0:T(8,128)S(1)} custom-call(f32[1]{0:T(128)} %bitcast.2.sign_ref, f32[4]{0:T(128)S(1)} %copy-done.4, f32[512,512]{1,0:T(8,128)S(1)} %collective-permute-done.9.near_ref, f32[512,1024]{1,0:T(8,128)S(1)} %bitcast.11, f32[1,512]{1,0:T(1,128)S(1)} %copy-done.2, s32[1,512]{1,0:T(1,128)S(1)} %copy-done.3), custom_call_target="tpu_custom_call" | custom-call | flops 20971520000 | bytes 5242880 | tf_op jit(solution)/shard_map/near_sums/pallas_call | solution.py:304
  114.4 1.3 far_sums.1.so_far_ref
  115.7 6.4 %collective-permute-done.21.refs_3_ = f32[192,512]{1,0:T(8,128)S(1)} collective-permute-done((f32[192,512]{1,0:T(8,128)S(1)}, f32[192,512]{1,0:T(8,128)S(1)}, u32[]{:S(2)}, u32[]{:S(2)}) %collective-permute-start.21) | collective-permute-done | bytes 393248 | tf_op jit(solution)/shard_map/ppermute | solution.py:558
  122.1 13.8 %collective-permute-done.20.refs_2_ = f32[192,512]{1,0:T(8,128)S(1)} collective-permute-done((f32[192,512]{1,0:T(8,128)S(1)}, f32[192,512]{1,0:T(8,128)S(1)}, u32[]{:S(2)}, u32[]{:S(2)}) %collective-permute-start.20) | collective-permute-done | bytes 393248 | tf_op jit(solution)/shard_map/ppermute | solution.py:558
  135.9 4.0 %right_sums.1 = (f32[8,512]{1,0:T(8,128)S(1)}, f32[512,512]{1,0:T(8,128)S(1)}) custom-call(s32[1]{0:T(128)} %bitcast.1.inner_ref, f32[1]{0:T(128)} %bitcast.2.sign_ref, s32[3,512,128]{2,1,0:T(8,128)S(1)} %get-tuple-element.40.place_ref, f32[512,512]{1,0:T(8,128)S(1)} %collective-permute-done.9.near_ref, f32[512,512]{1,0:T(8,128)S(1)} %collective-permute-done.17.far_ref, ...), custom_call_target="tpu_custom_call" | custom-call | flops 1207959552 | bytes 5242880 | tf_op jit(solution)/shard_map/right_sums/pallas_call | solution.py:364
  139.9 2.0 %collective-permute-start.22 = (f32[8,512]{1,0:T(8,128)S(1)}, f32[8,512]{1,0:T(8,128)S(1)}, u32[]{:S(2)}, u32[]{:S(2)}) collective-permute-start(f32[8,512]{1,0:T(8,128)S(1)} %get-tuple-element.70), channel_id=1, source_target_pairs={{0,2},{1,3},{2,4},{3,5},{4,6},{5,7},{6,0},{7,1},{8,10},{9,11},{10,... | collective-permute-start | bytes 49160 | tf_op jit(solution)/shard_map/ppermute | solution.py:585
  141.9 3.4 %collective-permute-start.23 = (f32[8,512]{1,0:T(8,128)S(1)}, f32[8,512]{1,0:T(8,128)S(1)}, u32[]{:S(2)}, u32[]{:S(2)}) collective-permute-start(f32[8,512]{1,0:T(8,128)S(1)} %get-tuple-element.70), channel_id=1, source_target_pairs={{0,4},{1,5},{2,6},{3,7},{4,0},{5,1},{6,2},{7,3},{8,12},{9,13},{10,... | collective-permute-start | bytes 49160 | tf_op jit(solution)/shard_map/ppermute | solution.py:585
  145.3 2.9 %shapes.1 = (f32[512,1024]{1,0:T(8,128)S(1)}, f32[512,1024]{1,0:T(8,128)S(1)}, f32[512,1024]{1,0:T(8,128)S(1)}) custom-call(s32[1]{0:T(128)} %bitcast.1.inner_ref, f32[1]{0:T(128)} %bitcast.2.sign_ref, f32[512,512]{1,0:T(8,128)S(1)} %collective-permute-done.9.near_ref, f32[512,512]{1,0:T(8,128)S(1)} %collective-permute-done.17.far_ref, ...), custom_call_target="tpu_custom_call" | custom-call | flops 15728640 | bytes 14680064 | tf_op jit(solution)/shard_map/shapes/pallas_call | solution.py:434
  148.2 0.8 collective-permute-done.24
  149.0 0.7 collective-permute-start.25
  149.7 1.1 collective-permute-start.26
  150.8 2.8 %collective-permute-start.27 = (f32[32,512]{1,0:T(8,128)S(1)}, f32[32,512]{1,0:T(8,128)S(1)}, u32[]{:S(2)}, u32[]{:S(2)}) collective-permute-start(f32[32,512]{1,0:T(8,128)S(1)} %pad_maximum_fusion.refs_0_), channel_id=1, source_target_pairs={{0,24},{8,0},{16,8},{24,16},{1,25},{9,1},{17,9},{25,17},{2,26},{10... | collective-permute-start | bytes 196616 | tf_op jit(solution)/shard_map/ppermute | solution.py:581
  153.6 1.1 collective-permute-done.25.refs_1_
  154.8 0.5 collective-permute-start.30
  155.3 0.2 collective-permute-done.27.refs_3_
  155.5 0.5 collective-permute-done.29.refs_5_
  156.0 0.2 collective-permute-done.30.refs_6_
  156.2 0.6 collective-permute-done.31.refs_7_
  156.8 3.0 %finish.1 = (f32[1,512]{1,0:T(1,128)}, f32[512,1024]{1,0:T(8,128)}) custom-call(s32[1]{0:T(128)} %bitcast.at_ref, f32[32,512]{1,0:T(8,128)S(1)} %pad_maximum_fusion.refs_0_, f32[32,512]{1,0:T(8,128)S(1)} %collective-permute-done.25.refs_1_, f32[32,512]{1,0:T(8,128)S(1)} %collective-permute-done.26.refs_2_, f32[32,512]{1,0:T(8,128)S(1)} %collective-permute-done.27.refs_3_, ...), custom_call_target="tpu_custom_call" | custom-call | tf_op jit(solution)/shard_map/finish/pallas_call | solution.py:479
  (26 shorter events, 0.1 us)
Async XLA Ops:
  1.4 7.8 %collective-permute-start = (s32[1,512]{1,0:T(1,128)S(1)}, s32[1,512]{1,0:T(1,128)S(1)}, u32[]{:S(2)}, u32[]{:S(2)}) collective-permute-start(s32[1,512]{1,0:T(1,128)S(1)} %get-tuple-element.79), channel_id=1, source_target_pairs={{0,8},{8,0},{16,24},{24,16},{1,9},{9,1},{17,25},{25,17},{2,10},{10... | collective-permute-start | bytes 6152 | tf_op jit(solution)/shard_map/ppermute | solution.py:523
  4.4 4.8 %collective-permute-start.1 = (s32[1,512]{1,0:T(1,128)S(1)}, s32[1,512]{1,0:T(1,128)S(1)}, u32[]{:S(2)}, u32[]{:S(2)}) collective-permute-start(s32[1,512]{1,0:T(1,128)S(1)} %get-tuple-element.78.own_ref), channel_id=1, source_target_pairs={{8,16},{16,8},{9,17},{17,9},{10,18},{18,10},{11,19},{19,11},{12,20... | collective-permute-start | bytes 6152 | tf_op jit(solution)/shard_map/ppermute | solution.py:523
  5.0 1.6 copy-start
  10.1 7.9 %collective-permute-start.5 = (f32[512,512]{1,0:T(8,128)S(1)}, f32[512,512]{1,0:T(8,128)}, u32[]{:S(2)}, u32[]{:S(2)}) collective-permute-start(f32[512,512]{1,0:T(8,128)S(1)} %get-tuple-element.47.refs_4_), channel_id=1, source_target_pairs={{0,1},{1,0},{2,3},{3,2},{4,5},{5,4},{6,7},{7,6},{8,9},{9,8},{10,11... | collective-permute-start | bytes 3145736 | tf_op jit(solution)/shard_map/ppermute | solution.py:533
  10.1 5.6 %collective-permute-start.2 = (s32[2,384]{1,0:T(2,128)S(1)}, s32[2,384]{1,0:T(2,128)S(1)}, u32[]{:S(2)}, u32[]{:S(2)}) collective-permute-start(s32[2,384]{1,0:T(2,128)S(1)} %get-tuple-element.42), channel_id=1, source_target_pairs={{0,2},{1,3},{2,4},{3,5},{4,6},{5,7},{6,0},{7,1},{8,10},{9,11},{10,... | collective-permute-start | bytes 9224 | tf_op jit(solution)/shard_map/ppermute | solution.py:528
  11.7 4.7 %collective-permute-start.3 = (s32[2,384]{1,0:T(2,128)S(1)}, s32[2,384]{1,0:T(2,128)S(1)}, u32[]{:S(2)}, u32[]{:S(2)}) collective-permute-start(s32[2,384]{1,0:T(2,128)S(1)} %get-tuple-element.43), channel_id=1, source_target_pairs={{0,4},{1,5},{2,6},{3,7},{4,0},{5,1},{6,2},{7,3},{8,12},{9,13},{10,... | collective-permute-start | bytes 9224 | tf_op jit(solution)/shard_map/ppermute | solution.py:528
  14.3 3.6 %collective-permute-start.4 = (s32[2,384]{1,0:T(2,128)S(1)}, s32[2,384]{1,0:T(2,128)S(1)}, u32[]{:S(2)}, u32[]{:S(2)}) collective-permute-start(s32[2,384]{1,0:T(2,128)S(1)} %get-tuple-element.44), channel_id=1, source_target_pairs={{0,6},{1,7},{2,0},{3,1},{4,2},{5,3},{6,4},{7,5},{8,14},{9,15},{10,... | collective-permute-start | bytes 9224 | tf_op jit(solution)/shard_map/ppermute | solution.py:528
  15.7 8.2 %collective-permute-start.10 = (f32[512,512]{1,0:T(8,128)S(1)}, f32[512,512]{1,0:T(8,128)S(1)}, u32[]{:S(2)}, u32[]{:S(2)}) collective-permute-start(f32[512,512]{1,0:T(8,128)S(1)} %get-tuple-element.52.refs_6_), channel_id=1, source_target_pairs={{0,1},{1,0},{2,3},{3,2},{4,5},{5,4},{6,7},{7,6},{8,9},{9,8},{10,11... | collective-permute-start | bytes 3145736 | tf_op jit(solution)/shard_map/ppermute | solution.py:533
  15.7 24.3 %collective-permute-start.11 = (f32[512,512]{1,0:T(8,128)S(1)}, f32[512,512]{1,0:T(8,128)S(1)}, u32[]{:S(2)}, u32[]{:S(2)}) collective-permute-start(f32[512,512]{1,0:T(8,128)S(1)} %get-tuple-element.52.refs_6_), channel_id=1, source_target_pairs={{8,16},{16,8},{9,17},{17,9},{10,18},{18,10},{11,19},{19,11},{12,20... | collective-permute-start | bytes 3145736 | tf_op jit(solution)/shard_map/ppermute | solution.py:539
  16.4 51.9 %collective-permute-start.12 = (f32[512,512]{1,0:T(8,128)S(1)}, f32[512,512]{1,0:T(8,128)S(1)}, u32[]{:S(2)}, u32[]{:S(2)}) collective-permute-start(f32[512,512]{1,0:T(8,128)S(1)} %get-tuple-element.52.refs_6_), channel_id=1, source_target_pairs={{8,0},{16,24},{9,1},{17,25},{10,2},{18,26},{11,3},{19,27},{12,4},{... | collective-permute-start | bytes 3145736 | tf_op jit(solution)/shard_map/ppermute | solution.py:538
  20.7 19.3 %collective-permute-start.8 = (f32[192,512]{1,0:T(8,128)S(1)}, f32[192,512]{1,0:T(8,128)S(1)}, u32[]{:S(2)}, u32[]{:S(2)}) collective-permute-start(f32[192,512]{1,0:T(8,128)S(1)} %get-tuple-element.51), channel_id=1, source_target_pairs={{0,6},{1,7},{2,0},{3,1},{4,2},{5,3},{6,4},{7,5},{8,14},{9,15},{10,... | collective-permute-start | bytes 1179656 | tf_op jit(solution)/shard_map/ppermute | solution.py:558
  23.9 19.1 %collective-permute-start.6 = (f32[192,512]{1,0:T(8,128)S(1)}, f32[192,512]{1,0:T(8,128)S(1)}, u32[]{:S(2)}, u32[]{:S(2)}) collective-permute-start(f32[192,512]{1,0:T(8,128)S(1)} %get-tuple-element.49), channel_id=1, source_target_pairs={{0,2},{1,3},{2,4},{3,5},{4,6},{5,7},{6,0},{7,1},{8,10},{9,11},{10,... | collective-permute-start | bytes 1179656 | tf_op jit(solution)/shard_map/ppermute | solution.py:558
  23.9 34.8 %collective-permute-start.7 = (f32[192,512]{1,0:T(8,128)S(1)}, f32[192,512]{1,0:T(8,128)S(1)}, u32[]{:S(2)}, u32[]{:S(2)}) collective-permute-start(f32[192,512]{1,0:T(8,128)S(1)} %get-tuple-element.50), channel_id=1, source_target_pairs={{0,4},{1,5},{2,6},{3,7},{4,0},{5,1},{6,2},{7,3},{8,12},{9,13},{10,... | collective-permute-start | bytes 1179656 | tf_op jit(solution)/shard_map/ppermute | solution.py:558
  40.0 58.3 %collective-permute-start.16 = (f32[192,512]{1,0:T(8,128)S(1)}, f32[192,512]{1,0:T(8,128)S(1)}, u32[]{:S(2)}, u32[]{:S(2)}) collective-permute-start(f32[192,512]{1,0:T(8,128)S(1)} %get-tuple-element.62), channel_id=1, source_target_pairs={{0,6},{1,7},{2,0},{3,1},{4,2},{5,3},{6,4},{7,5},{8,14},{9,15},{10,... | collective-permute-start | bytes 1179656 | tf_op jit(solution)/shard_map/ppermute | solution.py:558
  68.5 7.7 %collective-permute-start.13 = (f32[512,512]{1,0:T(8,128)S(1)}, f32[512,512]{1,0:T(8,128)S(1)}, u32[]{:S(2)}, u32[]{:S(2)}) collective-permute-start(f32[512,512]{1,0:T(8,128)S(1)} %broadcast_select_fusion.refs_4_), channel_id=1, source_target_pairs={{0,1},{1,0},{2,3},{3,2},{4,5},{5,4},{6,7},{7,6},{8,9},{9,8},{10,11... | collective-permute-start | bytes 3145736 | tf_op jit(solution)/shard_map/ppermute | solution.py:533
  68.6 29.7 %collective-permute-start.14 = (f32[192,512]{1,0:T(8,128)S(1)}, f32[192,512]{1,0:T(8,128)S(1)}, u32[]{:S(2)}, u32[]{:S(2)}) collective-permute-start(f32[192,512]{1,0:T(8,128)S(1)} %get-tuple-element.58), channel_id=1, source_target_pairs={{0,2},{1,3},{2,4},{3,5},{4,6},{5,7},{6,0},{7,1},{8,10},{9,11},{10,... | collective-permute-start | bytes 1179656 | tf_op jit(solution)/shard_map/ppermute | solution.py:558
  69.3 28.9 %collective-permute-start.15 = (f32[192,512]{1,0:T(8,128)S(1)}, f32[192,512]{1,0:T(8,128)S(1)}, u32[]{:S(2)}, u32[]{:S(2)}) collective-permute-start(f32[192,512]{1,0:T(8,128)S(1)} %get-tuple-element.60), channel_id=1, source_target_pairs={{0,4},{1,5},{2,6},{3,7},{4,0},{5,1},{6,2},{7,3},{8,12},{9,13},{10,... | collective-permute-start | bytes 1179656 | tf_op jit(solution)/shard_map/ppermute | solution.py:558
  71.1 41.4 %collective-permute-start.9 = (f32[512,512]{1,0:T(8,128)S(1)}, f32[512,512]{1,0:T(8,128)S(1)}, u32[]{:S(2)}, u32[]{:S(2)}) collective-permute-start(f32[512,512]{1,0:T(8,128)S(1)} %place.2), channel_id=1, source_target_pairs={{0,8},{8,0},{16,24},{24,16},{1,9},{9,1},{17,25},{25,17},{2,10},{10... | collective-permute-start | bytes 3145736 | tf_op jit(solution)/shard_map/ppermute | solution.py:566
  98.2 14.3 %collective-permute-start.19 = (f32[192,512]{1,0:T(8,128)S(1)}, f32[192,512]{1,0:T(8,128)S(1)}, u32[]{:S(2)}, u32[]{:S(2)}) collective-permute-start(f32[192,512]{1,0:T(8,128)S(1)} %get-tuple-element.64), channel_id=1, source_target_pairs={{0,2},{1,3},{2,4},{3,5},{4,6},{5,7},{6,0},{7,1},{8,10},{9,11},{10,... | collective-permute-start | bytes 1179656 | tf_op jit(solution)/shard_map/ppermute | solution.py:558
  98.3 14.3 %copy-start.1 = (f32[1,512,1024]{2,1,0:T(8,128)S(1)}, f32[1,512,1024]{2,1,0:T(8,128)}, u32[]{:S(2)}) copy-start(f32[1,512,1024]{2,1,0:T(8,128)} %param.6) | copy-start | bytes 6291460
  98.3 14.3 %copy-start.2 = (f32[1,512]{1,0:T(1,128)S(1)}, f32[1,512]{1,0:T(1,128)}, u32[]{:S(2)}) copy-start(f32[1,512]{1,0:T(1,128)} %start_ref.1) | copy-start | bytes 6148
  98.3 14.3 %copy-start.3 = (s32[1,512]{1,0:T(1,128)S(1)}, s32[1,512]{1,0:T(1,128)}, u32[]{:S(2)}) copy-start(s32[1,512]{1,0:T(1,128)} %class_ref.1) | copy-start | bytes 6148
  98.3 14.3 %copy-start.4 = (f32[4]{0:T(128)S(1)}, f32[4]{0:T(128)}, u32[]{:S(2)}) copy-start(f32[4]{0:T(128)} %table_ref.1) | copy-start | bytes 52
  99.8 14.7 %collective-permute-start.17 = (f32[512,512]{1,0:T(8,128)S(1)}, f32[512,512]{1,0:T(8,128)S(1)}, u32[]{:S(2)}, u32[]{:S(2)}) collective-permute-start(f32[512,512]{1,0:T(8,128)S(1)} %place.3), channel_id=1, source_target_pairs={{8,16},{16,8},{9,17},{17,9},{10,18},{18,10},{11,19},{19,11},{12,20... | collective-permute-start | bytes 3145736 | tf_op jit(solution)/shard_map/ppermute | solution.py:573
  100.5 35.4 %collective-permute-start.18 = (f32[512,512]{1,0:T(8,128)S(1)}, f32[512,512]{1,0:T(8,128)S(1)}, u32[]{:S(2)}, u32[]{:S(2)}) collective-permute-start(f32[512,512]{1,0:T(8,128)S(1)} %place.3), channel_id=1, source_target_pairs={{0,8},{24,16},{1,9},{25,17},{2,10},{26,18},{3,11},{27,19},{4,12},{... | collective-permute-start | bytes 3145736 | tf_op jit(solution)/shard_map/ppermute | solution.py:572
  108.5 13.6 %collective-permute-start.21 = (f32[192,512]{1,0:T(8,128)S(1)}, f32[192,512]{1,0:T(8,128)S(1)}, u32[]{:S(2)}, u32[]{:S(2)}) collective-permute-start(f32[192,512]{1,0:T(8,128)S(1)} %get-tuple-element.69), channel_id=1, source_target_pairs={{0,6},{1,7},{2,0},{3,1},{4,2},{5,3},{6,4},{7,5},{8,14},{9,15},{10,... | collective-permute-start | bytes 1179656 | tf_op jit(solution)/shard_map/ppermute | solution.py:558
  112.5 23.3 %collective-permute-start.20 = (f32[192,512]{1,0:T(8,128)S(1)}, f32[192,512]{1,0:T(8,128)S(1)}, u32[]{:S(2)}, u32[]{:S(2)}) collective-permute-start(f32[192,512]{1,0:T(8,128)S(1)} %get-tuple-element.67), channel_id=1, source_target_pairs={{0,4},{1,5},{2,6},{3,7},{4,0},{5,1},{6,2},{7,3},{8,12},{9,13},{10,... | collective-permute-start | bytes 1179656 | tf_op jit(solution)/shard_map/ppermute | solution.py:558
  139.9 8.2 %collective-permute-start.22 = (f32[8,512]{1,0:T(8,128)S(1)}, f32[8,512]{1,0:T(8,128)S(1)}, u32[]{:S(2)}, u32[]{:S(2)}) collective-permute-start(f32[8,512]{1,0:T(8,128)S(1)} %get-tuple-element.70), channel_id=1, source_target_pairs={{0,2},{1,3},{2,4},{3,5},{4,6},{5,7},{6,0},{7,1},{8,10},{9,11},{10,... | collective-permute-start | bytes 49160 | tf_op jit(solution)/shard_map/ppermute | solution.py:585
  141.9 6.3 %collective-permute-start.23 = (f32[8,512]{1,0:T(8,128)S(1)}, f32[8,512]{1,0:T(8,128)S(1)}, u32[]{:S(2)}, u32[]{:S(2)}) collective-permute-start(f32[8,512]{1,0:T(8,128)S(1)} %get-tuple-element.70), channel_id=1, source_target_pairs={{0,4},{1,5},{2,6},{3,7},{4,0},{5,1},{6,2},{7,3},{8,12},{9,13},{10,... | collective-permute-start | bytes 49160 | tf_op jit(solution)/shard_map/ppermute | solution.py:585
  145.3 3.7 %collective-permute-start.24 = (f32[8,512]{1,0:T(8,128)S(1)}, f32[8,512]{1,0:T(8,128)S(1)}, u32[]{:S(2)}, u32[]{:S(2)}) collective-permute-start(f32[8,512]{1,0:T(8,128)S(1)} %get-tuple-element.70), channel_id=1, source_target_pairs={{0,6},{1,7},{2,0},{3,1},{4,2},{5,3},{6,4},{7,5},{8,14},{9,15},{10,... | collective-permute-start | bytes 49160 | tf_op jit(solution)/shard_map/ppermute | solution.py:585
  149.0 5.7 %collective-permute-start.25 = (f32[32,512]{1,0:T(8,128)S(1)}, f32[32,512]{1,0:T(8,128)S(1)}, u32[]{:S(2)}, u32[]{:S(2)}) collective-permute-start(f32[32,512]{1,0:T(8,128)S(1)} %pad_maximum_fusion.refs_0_), channel_id=1, source_target_pairs={{0,8},{8,16},{16,24},{24,0},{1,9},{9,17},{17,25},{25,1},{2,10},{10... | collective-permute-start | bytes 196616 | tf_op jit(solution)/shard_map/ppermute | solution.py:581
  149.7 5.1 %collective-permute-start.26 = (f32[32,512]{1,0:T(8,128)S(1)}, f32[32,512]{1,0:T(8,128)S(1)}, u32[]{:S(2)}, u32[]{:S(2)}) collective-permute-start(f32[32,512]{1,0:T(8,128)S(1)} %pad_maximum_fusion.refs_0_), channel_id=1, source_target_pairs={{0,16},{8,24},{16,0},{24,8},{1,17},{9,25},{17,1},{25,9},{2,18},{10... | collective-permute-start | bytes 196616 | tf_op jit(solution)/shard_map/ppermute | solution.py:581
  150.8 4.8 %collective-permute-start.27 = (f32[32,512]{1,0:T(8,128)S(1)}, f32[32,512]{1,0:T(8,128)S(1)}, u32[]{:S(2)}, u32[]{:S(2)}) collective-permute-start(f32[32,512]{1,0:T(8,128)S(1)} %pad_maximum_fusion.refs_0_), channel_id=1, source_target_pairs={{0,24},{8,0},{16,8},{24,16},{1,25},{9,1},{17,9},{25,17},{2,26},{10... | collective-permute-start | bytes 196616 | tf_op jit(solution)/shard_map/ppermute | solution.py:581
  153.6 1.9 %collective-permute-start.28 = (f32[32,512]{1,0:T(8,128)S(1)}, f32[32,512]{1,0:T(8,128)S(1)}, u32[]{:S(2)}, u32[]{:S(2)}) collective-permute-start(f32[32,512]{1,0:T(8,128)S(1)} %pad_maximum_fusion.refs_0_), channel_id=1, source_target_pairs={{0,1},{1,0},{2,3},{3,2},{4,5},{5,4},{6,7},{7,6},{8,9},{9,8},{10,11... | collective-permute-start | bytes 196616 | tf_op jit(solution)/shard_map/ppermute | solution.py:533
  154.8 1.3 collective-permute-start.29
  154.8 1.4 collective-permute-start.30
  155.5 1.3 collective-permute-start.31

commit v5 on v4

--- a/solution.py
+++ b/solution.py
@@ -312,58 +312,62 @@
     )(sign, table, near, voxels, start, classes)
 
 
-def far_sums_kernel(sign_ref, far_ref, vol_ref, so_far_ref, out_ref):
+def only_last(values):
+    lane = lax.broadcasted_iota(jnp.int32, (values.shape[0], 128), 1)
+    return on_tile(values, 0, lambda tile: jnp.where(lane == 127, tile, 0.0))
+
+
+def far_sums_kernel(inner_ref, sign_ref, near_ref, far_ref, hop_ref, vol_ref, so_far_ref, out_ref):
     rows, half = far_ref.shape
+    inner = inner_ref[0] != 0
+    sign = sign_ref[0]
     for start in range(0, rows, STEP):
         at = slice(start, start + STEP)
-        lines = row_sums(-sign_ref[0], far_ref[at], vol_ref[at, :half], all_but_last)
-        for number, line in enumerate(lines):
+        near, far, voxels = near_ref[at], far_ref[at], vol_ref[at, :half]
+        lines = row_sums(-sign, far, voxels, all_but_last)
+        wide = jnp.concatenate([near[:, half - 128 :], hop_ref[at]], axis=1)
+        others = row_sums(sign, wide, vol_ref[at, half - 128 :], only_last)
+        for number, (line, other) in enumerate(zip(lines, others)):
+            line = line + jnp.where(inner, other, 0.0)
             out_ref[number : number + 1, at] = so_far_ref[number : number + 1, at] + line
     out_ref[5:8, :] = so_far_ref[5:8, :]
 
 
-def far_sums(sign, far, voxels, so_far):
+def far_sums(inner, sign, near, far, hop, voxels, so_far):
     rows, half = far.shape
     return pl.pallas_call(
         far_sums_kernel,
-        in_specs=[SMEM] + [VMEM] * 3,
+        in_specs=[SMEM, SMEM] + [VMEM] * 5,
         out_specs=VMEM,
         out_shape=jax.ShapeDtypeStruct((FIELDS, rows), jnp.float32),
         cost_estimate=cost(60 * rows * half, 5 * rows * half),
         compiler_params=LIMIT,
         name="far_sums",
-    )(sign, far, voxels, so_far)
-
-
-def right_sums_kernel(inner_ref, sign_ref, place_ref, near_ref, far_ref, hop_ref, vol_ref, so_far_ref, *refs):
+    )(inner, sign, near, far, hop, voxels, so_far)
+
+
+def right_sums_kernel(inner_ref, sign_ref, place_ref, near_ref, far_ref, vol_ref, so_far_ref, *refs):
     blocks, fields_ref, third_ref, terms_ref = refs[:-3], refs[-3], refs[-2], refs[-1]
     rows, half = near_ref.shape
     inner = inner_ref[0] != 0
+    sign = jnp.where(inner, -sign_ref[0], sign_ref[0])
     store_terms(blocks, terms_ref)
     third_ref[...] = placed(place_ref[2], terms_ref)
-
-    def counted(values):
-        lane = lax.broadcasted_iota(jnp.int32, (STEP, 128), 1)
-        return on_tile(values, 0, lambda tile: jnp.where(lane == 127, tile, 0.0))
-
     for start in range(0, rows, STEP):
         at = slice(start, start + STEP)
-        third = third_ref[at]
-        near = jnp.concatenate([near_ref[at, half - 128 :], jnp.where(inner, hop_ref[at], third)], axis=1)
-        far = jnp.concatenate([far_ref[at, half - 128 :], jnp.where(inner, third, 0.0)], axis=1)
-        voxels = vol_ref[at, half - 128 :]
-        lines = zip(row_sums(sign_ref[0], near, voxels, counted), row_sums(-sign_ref[0], far, voxels, counted))
-        for number, (line, other) in enumerate(lines):
-            fields_ref[number : number + 1, at] = so_far_ref[number : number + 1, at] + line + other
+        rim = jnp.where(inner, far_ref[at, half - 128 :], near_ref[at, half - 128 :])
+        stream = jnp.concatenate([rim, third_ref[at]], axis=1)
+        for number, line in enumerate(row_sums(sign, stream, vol_ref[at, half - 128 :], only_last)):
+            fields_ref[number : number + 1, at] = so_far_ref[number : number + 1, at] + line
     fields_ref[5:8, :] = so_far_ref[5:8, :]
 
 
-def right_sums(inner, sign, places, near, far, hop, voxels, so_far, blocks):
+def right_sums(inner, sign, places, near, far, voxels, so_far, blocks):
     rows, half = near.shape
     total = sum(block.shape[0] for block in blocks)
     return pl.pallas_call(
         right_sums_kernel,
-        in_specs=[SMEM, SMEM] + [VMEM] * (6 + len(blocks)),
+        in_specs=[SMEM, SMEM] + [VMEM] * (5 + len(blocks)),
         out_specs=[VMEM, VMEM],
         out_shape=[
             jax.ShapeDtypeStruct((FIELDS, rows), jnp.float32),
@@ -373,7 +377,7 @@
         cost_estimate=cost(3 * 2 * total * rows * half, 5 * rows * half),
         compiler_params=LIMIT,
         name="right_sums",
-    )(inner, sign, places, near, far, hop, voxels, so_far, *blocks)
+    )(inner, sign, places, near, far, voxels, so_far, *blocks)
 
 
 def plane_stencil(field):
@@ -559,22 +563,20 @@
             sent.append(arrived[turn])
         return arrived
 
-    order = (2, 1, 3)
-    arrived = fetched(picks(0, [left, left_other]), order)
+    arrived = fetched(picks(0, [left, left_other]), (3, 1, 2))
     first = place(0, places, arrived)
     lender = jnp.where(inner == 1, after(from_middle, *arrived), from_inner)
     near = lax.ppermute(first, "scan", sides)
-    arrived2 = fetched(picks(1, [left, left_other, right, right_other]), order)
+    arrived2 = fetched(picks(1, [left, left_other, right, right_other]), (3, 1, 2))
     blocks = picks(2, [lender, other_core(lender)])
     second = place(1, places, [after(arrived2[0], blocks[0]), *arrived2[1:]])
-    order = (1, 2, 3)
-    arrived = fetched(blocks, order)
+    arrived = fetched(blocks, (3, 1, 2))
     hop = lax.ppermute(second, "scan", [(0, 1), (3, 2)])
     far = lax.ppermute(second, "scan", middle)
-    begun = arrived[1:2] if direct else arrived
+    begun = arrived[3:4] if direct else arrived
     so_far = near_sums(sign, modulus_table, after(near, *begun), voxels, velocity0, modulus_class)
-    so_far = far_sums(sign, far, voxels, so_far)
-    sums, third = right_sums(inner, sign, places, near, far, hop, voxels, so_far, arrived)
+    so_far = far_sums(inner, sign, near, far, hop, voxels, so_far)
+    sums, third = right_sums(inner, sign, places, near, far, voxels, so_far, arrived)
 
     def scans_of(block):
         routes = [[(p, (p + turn) % scans) for p in range(scans)] for turn in range(1, scans)]

time: 160 us -> 155 us (0.969)
  waiting for transfers between devices: 84.9 us -> 78.3 us
    ppermute x9, waiting for transfers between devices: 71.6 us -> 40.2 us  [fetched(): arrived[turn] = lax.ppermute(block, 'slab', turns[turn])]
    ppermute x1, waiting for transfers between devices: 0.01 us -> 18.1 us  [on_device(): hop = lax.ppermute(second, 'scan', [(0, 1), (3, 2)])]
    ppermute x1, waiting for transfers between devices: 9.57 us -> 17 us  [on_device(): from_inner = lax.ppermute(right, 'scan', [(1, 0), (2, 3)])]
    ppermute x1, starting transfers between devices: 5.05 us -> 1.14 us  [on_device(): near = lax.ppermute(first, 'scan', sides)]
    ppermute x1, starting transfers between devices: 8.01 us -> 11.2 us  [on_device(): hop = lax.ppermute(second, 'scan', [(0, 1), (3, 2)])]
    ppermute x9, starting transfers between devices: 9.41 us -> 12.3 us  [fetched(): arrived[turn] = lax.ppermute(block, 'slab', turns[turn])]
  transfers between devices with their start and end apart: 32 -> 32, of which waited for: 14 -> 12; matrix products, arithmetic and copies ran while one was open for 0% -> 0% of each run, Pallas kernels for 12% -> 13%
where the time goes in v5:
time: 155 us; the launch traced here: 154 us
  waiting for transfers between devices  78.3 us (51%)
  starting transfers between devices  45.4 us (29%)
  Pallas kernels  26.9 us (17%)
  local copies, waits for them, and re-layouts  1.6 us (1%)
    ppermute x9, waiting for transfers between devices, fetched(): arrived[turn] = lax.ppermute(block, 'slab', turns[turn])  40.2 us
    ppermute x1, waiting for transfers between devices, on_device(): hop = lax.ppermute(second, 'scan', [(0, 1), (3, 2)])  18.1 us
    ppermute x1, waiting for transfers between devices, on_device(): from_inner = lax.ppermute(right, 'scan', [(1, 0), (2, 3)])  17 us
    ppermute x9, starting transfers between devices, fetched(): arrived[turn] = lax.ppermute(block, 'slab', turns[turn])  12.3 us
    ppermute x1, starting transfers between devices, on_device(): hop = lax.ppermute(second, 'scan', [(0, 1), (3, 2)])  11.2 us
    pallas_call x3, Pallas kernels, pick(): pl.pallas_call(functools.partial(pick_kernel, chips, capacity, number), i...  7.1 us
    ppermute x3, starting transfers between devices, on_device(): lax.ppermute(tables[turn], 'slab', turns[turn])  5.57 us
    ppermute x3, starting transfers between devices, scans_of(): return [block] + [lax.ppermute(block, 'scan', route) for route in routes]  4.42 us
  transfers between devices with their start and end apart: 32, of which 12 were waited for; matrix products, arithmetic and copies ran while one was open for 0% of the time, Pallas kernels for 13%

profile of v5, /device:TPU:0, one launch (start us, length us, event | category | flops | bytes accessed | tf_op | source)
XLA Modules:
  0.0 154.2 jit_solution(11408788759925213723)
XLA Ops:
  0.6 0.7 bitcast_add_fusion.early_ref
  1.4 3.0 %collective-permute-start = (s32[1,512]{1,0:T(1,128)S(1)}, s32[1,512]{1,0:T(1,128)S(1)}, u32[]{:S(2)}, u32[]{:S(2)}) collective-permute-start(s32[1,512]{1,0:T(1,128)S(1)} %get-tuple-element.79), channel_id=1, source_target_pairs={{0,8},{8,0},{16,24},{24,16},{1,9},{9,1},{17,25},{25,17},{2,10},{10... | collective-permute-start | bytes 6152 | tf_op jit(solution)/shard_map/ppermute | solution.py:527
  4.4 0.6 collective-permute-start.1
  5.0 0.0 copy-start
  5.0 1.6 %copy-done = f32[1,512,1024]{2,1,0:T(8,128)S(1)} copy-done((f32[1,512,1024]{2,1,0:T(8,128)S(1)}, f32[1,512,1024]{2,1,0:T(8,128)}, u32[]{:S(2)}) %copy-start) | copy-done | bytes 2097176
  6.6 2.5 %prefilter.1 = (f32[512,512]{1,0:T(8,128)S(1)}, f32[512,512]{1,0:T(8,128)S(1)}) custom-call(f32[512,1024]{1,0:T(8,128)S(1)} %bitcast.10, s32[2,512]{1,0:T(2,128)S(1)} %bitcast_add_fusion.early_ref), custom_call_target="tpu_custom_call" | custom-call | flops 1610612736 | bytes 4194304 | tf_op jit(solution)/shard_map/prefilter/pallas_call | solution.py:73
  9.2 0.0 collective-permute-done.side_ref
  9.2 0.0 collective-permute-done.1.inward_ref
  9.2 0.9 requests.1
  10.1 0.0 collective-permute-start.5
  10.1 1.6 %collective-permute-start.2 = (s32[2,384]{1,0:T(2,128)S(1)}, s32[2,384]{1,0:T(2,128)S(1)}, u32[]{:S(2)}, u32[]{:S(2)}) collective-permute-start(s32[2,384]{1,0:T(2,128)S(1)} %get-tuple-element.42), channel_id=1, source_target_pairs={{0,2},{1,3},{2,4},{3,5},{4,6},{5,7},{6,0},{7,1},{8,10},{9,11},{10,... | collective-permute-start | bytes 9224 | tf_op jit(solution)/shard_map/ppermute | solution.py:532
  11.7 2.6 %collective-permute-start.3 = (s32[2,384]{1,0:T(2,128)S(1)}, s32[2,384]{1,0:T(2,128)S(1)}, u32[]{:S(2)}, u32[]{:S(2)}) collective-permute-start(s32[2,384]{1,0:T(2,128)S(1)} %get-tuple-element.43), channel_id=1, source_target_pairs={{0,4},{1,5},{2,6},{3,7},{4,0},{5,1},{6,2},{7,3},{8,12},{9,13},{10,... | collective-permute-start | bytes 9224 | tf_op jit(solution)/shard_map/ppermute | solution.py:532
  14.3 1.4 collective-permute-start.4
  15.7 0.7 collective-permute-start.11
  16.4 1.3 collective-permute-start.12
  17.7 0.2 collective-permute-done.4.refs_3_
  17.9 0.0 collective-permute-done.5.refs_5_
  17.9 2.8 %pick.3 = (f32[192,512]{1,0:T(8,128)S(1)}, f32[192,512]{1,0:T(8,128)S(1)}, f32[192,512]{1,0:T(8,128)S(1)}, f32[192,512]{1,0:T(8,128)S(1)}) custom-call(s32[1]{0:T(128)} %bitcast.1.inner_ref, s32[2,384]{1,0:T(2,128)S(1)} %get-tuple-element.41.refs_0_, s32[2,384]{1,0:T(2,128)S(1)} %collective-permute-done.2.refs_1_, ...), custom_call_target="tpu_custom_call" | custom-call | flops 19327352832 | bytes 5242880 | tf_op jit(solution)/shard_map/pick/pallas_call | solution.py:183
  20.7 2.3 %collective-permute-start.7 = (f32[192,512]{1,0:T(8,128)S(1)}, f32[192,512]{1,0:T(8,128)S(1)}, u32[]{:S(2)}, u32[]{:S(2)}) collective-permute-start(f32[192,512]{1,0:T(8,128)S(1)} %get-tuple-element.50), channel_id=1, source_target_pairs={{0,4},{1,5},{2,6},{3,7},{4,0},{5,1},{6,2},{7,3},{8,12},{9,13},{10,... | collective-permute-start | bytes 1179656 | tf_op jit(solution)/shard_map/ppermute | solution.py:562
  23.0 1.5 collective-permute-start.6
  24.5 2.3 %collective-permute-start.8 = (f32[192,512]{1,0:T(8,128)S(1)}, f32[192,512]{1,0:T(8,128)S(1)}, u32[]{:S(2)}, u32[]{:S(2)}) collective-permute-start(f32[192,512]{1,0:T(8,128)S(1)} %get-tuple-element.51), channel_id=1, source_target_pairs={{0,6},{1,7},{2,0},{3,1},{4,2},{5,3},{6,4},{7,5},{8,14},{9,15},{10,... | collective-permute-start | bytes 1179656 | tf_op jit(solution)/shard_map/ppermute | solution.py:562
  26.8 2.8 %pick.4 = (f32[192,512]{1,0:T(8,128)S(1)}, f32[192,512]{1,0:T(8,128)S(1)}, f32[192,512]{1,0:T(8,128)S(1)}, f32[192,512]{1,0:T(8,128)S(1)}) custom-call(s32[1]{0:T(128)} %bitcast.1.inner_ref, s32[2,384]{1,0:T(2,128)S(1)} %get-tuple-element.41.refs_0_, s32[2,384]{1,0:T(2,128)S(1)} %collective-permute-done.2.refs_1_, ...), custom_call_target="tpu_custom_call" | custom-call | flops 19327352832 | bytes 5242880 | tf_op jit(solution)/shard_map/pick/pallas_call | solution.py:183
  29.6 21.7 %collective-permute-done.7.refs_2_ = f32[192,512]{1,0:T(8,128)S(1)} collective-permute-done((f32[192,512]{1,0:T(8,128)S(1)}, f32[192,512]{1,0:T(8,128)S(1)}, u32[]{:S(2)}, u32[]{:S(2)}) %collective-permute-start.7) | collective-permute-done | bytes 393248 | tf_op jit(solution)/shard_map/ppermute | solution.py:562
  51.3 0.0 collective-permute-start.15
  51.3 0.0 collective-permute-done.11
  51.3 17.0 %collective-permute-done.12 = f32[512,512]{1,0:T(8,128)S(1)} collective-permute-done((f32[512,512]{1,0:T(8,128)S(1)}, f32[512,512]{1,0:T(8,128)S(1)}, u32[]{:S(2)}, u32[]{:S(2)}) %collective-permute-start.12) | collective-permute-done | bytes 1048608 | tf_op jit(solution)/shard_map/ppermute | solution.py:542
  68.3 0.2 broadcast_select_fusion.refs_4_
  68.5 0.1 collective-permute-start.13
  68.6 0.7 collective-permute-start.14
  69.3 3.1 %collective-permute-start.16 = (f32[192,512]{1,0:T(8,128)S(1)}, f32[192,512]{1,0:T(8,128)S(1)}, u32[]{:S(2)}, u32[]{:S(2)}) collective-permute-start(f32[192,512]{1,0:T(8,128)S(1)} %get-tuple-element.62), channel_id=1, source_target_pairs={{0,6},{1,7},{2,0},{3,1},{4,2},{5,3},{6,4},{7,5},{8,14},{9,15},{10,... | collective-permute-start | bytes 1179656 | tf_op jit(solution)/shard_map/ppermute | solution.py:562
  72.5 1.4 place.2
  73.9 1.1 collective-permute-start.9
  75.1 0.0 collective-permute-done.13.refs_5_
  75.1 1.5 %pick.5 = (f32[192,512]{1,0:T(8,128)S(1)}, f32[192,512]{1,0:T(8,128)S(1)}, f32[192,512]{1,0:T(8,128)S(1)}, f32[192,512]{1,0:T(8,128)S(1)}) custom-call(s32[1]{0:T(128)} %bitcast.1.inner_ref, s32[2,384]{1,0:T(2,128)S(1)} %get-tuple-element.41.refs_0_, s32[2,384]{1,0:T(2,128)S(1)} %collective-permute-done.2.refs_1_, ...), custom_call_target="tpu_custom_call" | custom-call | flops 19327352832 | bytes 5242880 | tf_op jit(solution)/shard_map/pick/pallas_call | solution.py:183
  76.6 15.4 %collective-permute-done.16.refs_3_ = f32[192,512]{1,0:T(8,128)S(1)} collective-permute-done((f32[192,512]{1,0:T(8,128)S(1)}, f32[192,512]{1,0:T(8,128)S(1)}, u32[]{:S(2)}, u32[]{:S(2)}) %collective-permute-start.16) | collective-permute-done | bytes 393248 | tf_op jit(solution)/shard_map/ppermute | solution.py:562
  92.1 0.0 copy-start.4
  92.1 0.0 collective-permute-done.14.refs_1_
  92.1 1.4 place.3
  93.5 0.7 collective-permute-start.17
  94.3 11.2 %collective-permute-start.18 = (f32[512,512]{1,0:T(8,128)S(1)}, f32[512,512]{1,0:T(8,128)S(1)}, u32[]{:S(2)}, u32[]{:S(2)}) collective-permute-start(f32[512,512]{1,0:T(8,128)S(1)} %place.3), channel_id=1, source_target_pairs={{0,8},{24,16},{1,9},{25,17},{2,10},{26,18},{3,11},{27,19},{4,12},{... | collective-permute-start | bytes 3145736 | tf_op jit(solution)/shard_map/ppermute | solution.py:574
  105.5 2.1 %collective-permute-start.21 = (f32[192,512]{1,0:T(8,128)S(1)}, f32[192,512]{1,0:T(8,128)S(1)}, u32[]{:S(2)}, u32[]{:S(2)}) collective-permute-start(f32[192,512]{1,0:T(8,128)S(1)} %get-tuple-element.69), channel_id=1, source_target_pairs={{0,4},{1,5},{2,6},{3,7},{4,0},{5,1},{6,2},{7,3},{8,12},{9,13},{10,... | collective-permute-start | bytes 1179656 | tf_op jit(solution)/shard_map/ppermute | solution.py:562
  107.7 0.0 collective-permute-done.9.near_ref
  107.7 0.2 collective-permute-start.20
  107.9 1.8 %near_sums.1.so_far_ref = f32[8,512]{1,0:T(8,128)S(1)} custom-call(f32[1]{0:T(128)} %bitcast.2.sign_ref, f32[4]{0:T(128)S(1)} %copy-done.4, f32[512,512]{1,0:T(8,128)S(1)} %collective-permute-done.9.near_ref, f32[512,1024]{1,0:T(8,128)S(1)} %bitcast.11, f32[1,512]{1,0:T(1,128)S(1)} %copy-done.2, s32[1,512]{1,0:T(1,128)S(1)} %copy-done.3), custom_call_target="tpu_custom_call" | custom-call | flops 20971520000 | bytes 5242880 | tf_op jit(solution)/shard_map/near_sums/pallas_call | solution.py:304
  109.7 18.1 %collective-permute-done.18.hop_ref = f32[512,512]{1,0:T(8,128)S(1)} collective-permute-done((f32[512,512]{1,0:T(8,128)S(1)}, f32[512,512]{1,0:T(8,128)S(1)}, u32[]{:S(2)}, u32[]{:S(2)}) %collective-permute-start.18) | collective-permute-done | bytes 1048608 | tf_op jit(solution)/shard_map/ppermute | solution.py:574
  127.8 3.0 %far_sums.1.so_far_ref = f32[8,512]{1,0:T(8,128)S(1)} custom-call(s32[1]{0:T(128)} %bitcast.1.inner_ref, f32[1]{0:T(128)} %bitcast.2.sign_ref, f32[512,512]{1,0:T(8,128)S(1)} %collective-permute-done.9.near_ref, f32[512,512]{1,0:T(8,128)S(1)} %collective-permute-done.17.far_ref, f32[512,512]{1,0:T(8,128)S(1)} %collective-permute-done.18.hop_ref, ...), custom_call_target="tpu_custom_call" | custom-call | flops 15728640 | bytes 5242880 | tf_op jit(solution)/shard_map/far_sums/pallas_call | solution.py:338
  130.8 3.1 %collective-permute-done.21.refs_2_ = f32[192,512]{1,0:T(8,128)S(1)} collective-permute-done((f32[192,512]{1,0:T(8,128)S(1)}, f32[192,512]{1,0:T(8,128)S(1)}, u32[]{:S(2)}, u32[]{:S(2)}) %collective-permute-start.21) | collective-permute-done | bytes 393248 | tf_op jit(solution)/shard_map/ppermute | solution.py:562
  133.9 2.8 %right_sums.1 = (f32[8,512]{1,0:T(8,128)S(1)}, f32[512,512]{1,0:T(8,128)S(1)}) custom-call(s32[1]{0:T(128)} %bitcast.1.inner_ref, f32[1]{0:T(128)} %bitcast.2.sign_ref, s32[3,512,128]{2,1,0:T(8,128)S(1)} %get-tuple-element.40.place_ref, f32[512,512]{1,0:T(8,128)S(1)} %collective-permute-done.9.near_ref, f32[512,512]{1,0:T(8,128)S(1)} %collective-permute-done.17.far_ref, ...), custom_call_target="tpu_custom_call" | custom-call | flops 1207959552 | bytes 5242880 | tf_op jit(solution)/shard_map/right_sums/pallas_call | solution.py:368
  136.7 0.1 collective-permute-start.22
  136.7 0.7 collective-permute-start.23
  137.4 3.1 %collective-permute-start.24 = (f32[8,512]{1,0:T(8,128)S(1)}, f32[8,512]{1,0:T(8,128)S(1)}, u32[]{:S(2)}, u32[]{:S(2)}) collective-permute-start(f32[8,512]{1,0:T(8,128)S(1)} %get-tuple-element.70), channel_id=1, source_target_pairs={{0,6},{1,7},{2,0},{3,1},{4,2},{5,3},{6,4},{7,5},{8,14},{9,15},{10,... | collective-permute-start | bytes 49160 | tf_op jit(solution)/shard_map/ppermute | solution.py:587
  140.5 2.9 %shapes.1 = (f32[512,1024]{1,0:T(8,128)S(1)}, f32[512,1024]{1,0:T(8,128)S(1)}, f32[512,1024]{1,0:T(8,128)S(1)}) custom-call(s32[1]{0:T(128)} %bitcast.1.inner_ref, f32[1]{0:T(128)} %bitcast.2.sign_ref, f32[512,512]{1,0:T(8,128)S(1)} %collective-permute-done.9.near_ref, f32[512,512]{1,0:T(8,128)S(1)} %collective-permute-done.17.far_ref, ...), custom_call_target="tpu_custom_call" | custom-call | flops 15728640 | bytes 14680064 | tf_op jit(solution)/shard_map/shapes/pallas_call | solution.py:438
  143.4 0.0 collective-permute-done.22
  143.5 0.6 collective-permute-start.25
  144.0 1.0 collective-permute-start.26
  145.0 2.8 %collective-permute-start.27 = (f32[32,512]{1,0:T(8,128)S(1)}, f32[32,512]{1,0:T(8,128)S(1)}, u32[]{:S(2)}, u32[]{:S(2)}) collective-permute-start(f32[32,512]{1,0:T(8,128)S(1)} %pad_maximum_fusion.refs_0_), channel_id=1, source_target_pairs={{0,24},{8,0},{16,8},{24,16},{1,25},{9,1},{17,9},{25,17},{2,26},{10... | collective-permute-start | bytes 196616 | tf_op jit(solution)/shard_map/ppermute | solution.py:583
  147.9 0.9 collective-permute-done.25.refs_1_
  148.8 0.2 collective-permute-done.26.refs_2_
  149.0 0.3 collective-permute-start.30
  149.3 0.5 collective-permute-done.27.refs_3_
  149.8 0.3 collective-permute-done.29.refs_5_
  150.1 0.2 collective-permute-done.30.refs_6_
  150.2 0.8 collective-permute-done.31.refs_7_
  151.0 3.0 %finish.1 = (f32[1,512]{1,0:T(1,128)}, f32[512,1024]{1,0:T(8,128)}) custom-call(s32[1]{0:T(128)} %bitcast.at_ref, f32[32,512]{1,0:T(8,128)S(1)} %pad_maximum_fusion.refs_0_, f32[32,512]{1,0:T(8,128)S(1)} %collective-permute-done.25.refs_1_, f32[32,512]{1,0:T(8,128)S(1)} %collective-permute-done.26.refs_2_, f32[32,512]{1,0:T(8,128)S(1)} %collective-permute-done.27.refs_3_, ...), custom_call_target="tpu_custom_call" | custom-call | tf_op jit(solution)/shard_map/finish/pallas_call | solution.py:483
  (26 shorter events, 0.1 us)
Async XLA Ops:
  1.4 7.8 %collective-permute-start = (s32[1,512]{1,0:T(1,128)S(1)}, s32[1,512]{1,0:T(1,128)S(1)}, u32[]{:S(2)}, u32[]{:S(2)}) collective-permute-start(s32[1,512]{1,0:T(1,128)S(1)} %get-tuple-element.79), channel_id=1, source_target_pairs={{0,8},{8,0},{16,24},{24,16},{1,9},{9,1},{17,25},{25,17},{2,10},{10... | collective-permute-start | bytes 6152 | tf_op jit(solution)/shard_map/ppermute | solution.py:527
  4.4 4.8 %collective-permute-start.1 = (s32[1,512]{1,0:T(1,128)S(1)}, s32[1,512]{1,0:T(1,128)S(1)}, u32[]{:S(2)}, u32[]{:S(2)}) collective-permute-start(s32[1,512]{1,0:T(1,128)S(1)} %get-tuple-element.78.own_ref), channel_id=1, source_target_pairs={{8,16},{16,8},{9,17},{17,9},{10,18},{18,10},{11,19},{19,11},{12,20... | collective-permute-start | bytes 6152 | tf_op jit(solution)/shard_map/ppermute | solution.py:527
  5.0 1.6 %copy-start = (f32[1,512,1024]{2,1,0:T(8,128)S(1)}, f32[1,512,1024]{2,1,0:T(8,128)}, u32[]{:S(2)}) copy-start(f32[1,512,1024]{2,1,0:T(8,128)} %param.6) | copy-start | bytes 6291460
  10.1 7.9 %collective-permute-start.5 = (f32[512,512]{1,0:T(8,128)S(1)}, f32[512,512]{1,0:T(8,128)}, u32[]{:S(2)}, u32[]{:S(2)}) collective-permute-start(f32[512,512]{1,0:T(8,128)S(1)} %get-tuple-element.47.refs_4_), channel_id=1, source_target_pairs={{0,1},{1,0},{2,3},{3,2},{4,5},{5,4},{6,7},{7,6},{8,9},{9,8},{10,11... | collective-permute-start | bytes 3145736 | tf_op jit(solution)/shard_map/ppermute | solution.py:537
  10.1 5.6 %collective-permute-start.2 = (s32[2,384]{1,0:T(2,128)S(1)}, s32[2,384]{1,0:T(2,128)S(1)}, u32[]{:S(2)}, u32[]{:S(2)}) collective-permute-start(s32[2,384]{1,0:T(2,128)S(1)} %get-tuple-element.42), channel_id=1, source_target_pairs={{0,2},{1,3},{2,4},{3,5},{4,6},{5,7},{6,0},{7,1},{8,10},{9,11},{10,... | collective-permute-start | bytes 9224 | tf_op jit(solution)/shard_map/ppermute | solution.py:532
  11.7 4.7 %collective-permute-start.3 = (s32[2,384]{1,0:T(2,128)S(1)}, s32[2,384]{1,0:T(2,128)S(1)}, u32[]{:S(2)}, u32[]{:S(2)}) collective-permute-start(s32[2,384]{1,0:T(2,128)S(1)} %get-tuple-element.43), channel_id=1, source_target_pairs={{0,4},{1,5},{2,6},{3,7},{4,0},{5,1},{6,2},{7,3},{8,12},{9,13},{10,... | collective-permute-start | bytes 9224 | tf_op jit(solution)/shard_map/ppermute | solution.py:532
  14.3 3.6 %collective-permute-start.4 = (s32[2,384]{1,0:T(2,128)S(1)}, s32[2,384]{1,0:T(2,128)S(1)}, u32[]{:S(2)}, u32[]{:S(2)}) collective-permute-start(s32[2,384]{1,0:T(2,128)S(1)} %get-tuple-element.44), channel_id=1, source_target_pairs={{0,6},{1,7},{2,0},{3,1},{4,2},{5,3},{6,4},{7,5},{8,14},{9,15},{10,... | collective-permute-start | bytes 9224 | tf_op jit(solution)/shard_map/ppermute | solution.py:532
  15.7 8.8 %collective-permute-start.10 = (f32[512,512]{1,0:T(8,128)S(1)}, f32[512,512]{1,0:T(8,128)S(1)}, u32[]{:S(2)}, u32[]{:S(2)}) collective-permute-start(f32[512,512]{1,0:T(8,128)S(1)} %get-tuple-element.52.refs_6_), channel_id=1, source_target_pairs={{0,1},{1,0},{2,3},{3,2},{4,5},{5,4},{6,7},{7,6},{8,9},{9,8},{10,11... | collective-permute-start | bytes 3145736 | tf_op jit(solution)/shard_map/ppermute | solution.py:537
  15.7 35.6 %collective-permute-start.11 = (f32[512,512]{1,0:T(8,128)S(1)}, f32[512,512]{1,0:T(8,128)S(1)}, u32[]{:S(2)}, u32[]{:S(2)}) collective-permute-start(f32[512,512]{1,0:T(8,128)S(1)} %get-tuple-element.52.refs_6_), channel_id=1, source_target_pairs={{8,16},{16,8},{9,17},{17,9},{10,18},{18,10},{11,19},{19,11},{12,20... | collective-permute-start | bytes 3145736 | tf_op jit(solution)/shard_map/ppermute | solution.py:543
  16.4 51.9 %collective-permute-start.12 = (f32[512,512]{1,0:T(8,128)S(1)}, f32[512,512]{1,0:T(8,128)S(1)}, u32[]{:S(2)}, u32[]{:S(2)}) collective-permute-start(f32[512,512]{1,0:T(8,128)S(1)} %get-tuple-element.52.refs_6_), channel_id=1, source_target_pairs={{8,0},{16,24},{9,1},{17,25},{10,2},{18,26},{11,3},{19,27},{12,4},{... | collective-permute-start | bytes 3145736 | tf_op jit(solution)/shard_map/ppermute | solution.py:542
  20.7 30.6 %collective-permute-start.7 = (f32[192,512]{1,0:T(8,128)S(1)}, f32[192,512]{1,0:T(8,128)S(1)}, u32[]{:S(2)}, u32[]{:S(2)}) collective-permute-start(f32[192,512]{1,0:T(8,128)S(1)} %get-tuple-element.50), channel_id=1, source_target_pairs={{0,4},{1,5},{2,6},{3,7},{4,0},{5,1},{6,2},{7,3},{8,12},{9,13},{10,... | collective-permute-start | bytes 1179656 | tf_op jit(solution)/shard_map/ppermute | solution.py:562
  23.0 28.3 %collective-permute-start.6 = (f32[192,512]{1,0:T(8,128)S(1)}, f32[192,512]{1,0:T(8,128)S(1)}, u32[]{:S(2)}, u32[]{:S(2)}) collective-permute-start(f32[192,512]{1,0:T(8,128)S(1)} %get-tuple-element.49), channel_id=1, source_target_pairs={{0,2},{1,3},{2,4},{3,5},{4,6},{5,7},{6,0},{7,1},{8,10},{9,11},{10,... | collective-permute-start | bytes 1179656 | tf_op jit(solution)/shard_map/ppermute | solution.py:562
  24.5 26.8 %collective-permute-start.8 = (f32[192,512]{1,0:T(8,128)S(1)}, f32[192,512]{1,0:T(8,128)S(1)}, u32[]{:S(2)}, u32[]{:S(2)}) collective-permute-start(f32[192,512]{1,0:T(8,128)S(1)} %get-tuple-element.51), channel_id=1, source_target_pairs={{0,6},{1,7},{2,0},{3,1},{4,2},{5,3},{6,4},{7,5},{8,14},{9,15},{10,... | collective-permute-start | bytes 1179656 | tf_op jit(solution)/shard_map/ppermute | solution.py:562
  51.3 40.8 %collective-permute-start.15 = (f32[192,512]{1,0:T(8,128)S(1)}, f32[192,512]{1,0:T(8,128)S(1)}, u32[]{:S(2)}, u32[]{:S(2)}) collective-permute-start(f32[192,512]{1,0:T(8,128)S(1)} %get-tuple-element.60), channel_id=1, source_target_pairs={{0,4},{1,5},{2,6},{3,7},{4,0},{5,1},{6,2},{7,3},{8,12},{9,13},{10,... | collective-permute-start | bytes 1179656 | tf_op jit(solution)/shard_map/ppermute | solution.py:562
  68.5 6.6 %collective-permute-start.13 = (f32[512,512]{1,0:T(8,128)S(1)}, f32[512,512]{1,0:T(8,128)S(1)}, u32[]{:S(2)}, u32[]{:S(2)}) collective-permute-start(f32[512,512]{1,0:T(8,128)S(1)} %broadcast_select_fusion.refs_4_), channel_id=1, source_target_pairs={{0,1},{1,0},{2,3},{3,2},{4,5},{5,4},{6,7},{7,6},{8,9},{9,8},{10,11... | collective-permute-start | bytes 3145736 | tf_op jit(solution)/shard_map/ppermute | solution.py:537
  68.6 23.5 %collective-permute-start.14 = (f32[192,512]{1,0:T(8,128)S(1)}, f32[192,512]{1,0:T(8,128)S(1)}, u32[]{:S(2)}, u32[]{:S(2)}) collective-permute-start(f32[192,512]{1,0:T(8,128)S(1)} %get-tuple-element.58), channel_id=1, source_target_pairs={{0,2},{1,3},{2,4},{3,5},{4,6},{5,7},{6,0},{7,1},{8,10},{9,11},{10,... | collective-permute-start | bytes 1179656 | tf_op jit(solution)/shard_map/ppermute | solution.py:562
  69.3 22.7 %collective-permute-start.16 = (f32[192,512]{1,0:T(8,128)S(1)}, f32[192,512]{1,0:T(8,128)S(1)}, u32[]{:S(2)}, u32[]{:S(2)}) collective-permute-start(f32[192,512]{1,0:T(8,128)S(1)} %get-tuple-element.62), channel_id=1, source_target_pairs={{0,6},{1,7},{2,0},{3,1},{4,2},{5,3},{6,4},{7,5},{8,14},{9,15},{10,... | collective-permute-start | bytes 1179656 | tf_op jit(solution)/shard_map/ppermute | solution.py:562
  73.9 33.7 %collective-permute-start.9 = (f32[512,512]{1,0:T(8,128)S(1)}, f32[512,512]{1,0:T(8,128)S(1)}, u32[]{:S(2)}, u32[]{:S(2)}) collective-permute-start(f32[512,512]{1,0:T(8,128)S(1)} %place.2), channel_id=1, source_target_pairs={{0,8},{8,0},{16,24},{24,16},{1,9},{9,1},{17,25},{25,17},{2,10},{10... | collective-permute-start | bytes 3145736 | tf_op jit(solution)/shard_map/ppermute | solution.py:569
  92.0 15.8 %collective-permute-start.19 = (f32[192,512]{1,0:T(8,128)S(1)}, f32[192,512]{1,0:T(8,128)S(1)}, u32[]{:S(2)}, u32[]{:S(2)}) collective-permute-start(f32[192,512]{1,0:T(8,128)S(1)} %get-tuple-element.64), channel_id=1, source_target_pairs={{0,6},{1,7},{2,0},{3,1},{4,2},{5,3},{6,4},{7,5},{8,14},{9,15},{10,... | collective-permute-start | bytes 1179656 | tf_op jit(solution)/shard_map/ppermute | solution.py:562
  92.0 15.8 %copy-start.1 = (f32[1,512,1024]{2,1,0:T(8,128)S(1)}, f32[1,512,1024]{2,1,0:T(8,128)}, u32[]{:S(2)}) copy-start(f32[1,512,1024]{2,1,0:T(8,128)} %param.6) | copy-start | bytes 6291460
  92.0 15.8 %copy-start.2 = (f32[1,512]{1,0:T(1,128)S(1)}, f32[1,512]{1,0:T(1,128)}, u32[]{:S(2)}) copy-start(f32[1,512]{1,0:T(1,128)} %start_ref.1) | copy-start | bytes 6148
  92.1 15.8 %copy-start.3 = (s32[1,512]{1,0:T(1,128)S(1)}, s32[1,512]{1,0:T(1,128)}, u32[]{:S(2)}) copy-start(s32[1,512]{1,0:T(1,128)} %class_ref.1) | copy-start | bytes 6148
  92.1 15.8 %copy-start.4 = (f32[4]{0:T(128)S(1)}, f32[4]{0:T(128)}, u32[]{:S(2)}) copy-start(f32[4]{0:T(128)} %table_ref.1) | copy-start | bytes 52
  93.5 16.2 %collective-permute-start.17 = (f32[512,512]{1,0:T(8,128)S(1)}, f32[512,512]{1,0:T(8,128)S(1)}, u32[]{:S(2)}, u32[]{:S(2)}) collective-permute-start(f32[512,512]{1,0:T(8,128)S(1)} %place.3), channel_id=1, source_target_pairs={{8,16},{16,8},{9,17},{17,9},{10,18},{18,10},{11,19},{19,11},{12,20... | collective-permute-start | bytes 3145736 | tf_op jit(solution)/shard_map/ppermute | solution.py:575
  94.3 33.5 %collective-permute-start.18 = (f32[512,512]{1,0:T(8,128)S(1)}, f32[512,512]{1,0:T(8,128)S(1)}, u32[]{:S(2)}, u32[]{:S(2)}) collective-permute-start(f32[512,512]{1,0:T(8,128)S(1)} %place.3), channel_id=1, source_target_pairs={{0,8},{24,16},{1,9},{25,17},{2,10},{26,18},{3,11},{27,19},{4,12},{... | collective-permute-start | bytes 3145736 | tf_op jit(solution)/shard_map/ppermute | solution.py:574
  105.5 28.3 %collective-permute-start.21 = (f32[192,512]{1,0:T(8,128)S(1)}, f32[192,512]{1,0:T(8,128)S(1)}, u32[]{:S(2)}, u32[]{:S(2)}) collective-permute-start(f32[192,512]{1,0:T(8,128)S(1)} %get-tuple-element.69), channel_id=1, source_target_pairs={{0,4},{1,5},{2,6},{3,7},{4,0},{5,1},{6,2},{7,3},{8,12},{9,13},{10,... | collective-permute-start | bytes 1179656 | tf_op jit(solution)/shard_map/ppermute | solution.py:562
  107.7 26.2 %collective-permute-start.20 = (f32[192,512]{1,0:T(8,128)S(1)}, f32[192,512]{1,0:T(8,128)S(1)}, u32[]{:S(2)}, u32[]{:S(2)}) collective-permute-start(f32[192,512]{1,0:T(8,128)S(1)} %get-tuple-element.67), channel_id=1, source_target_pairs={{0,2},{1,3},{2,4},{3,5},{4,6},{5,7},{6,0},{7,1},{8,10},{9,11},{10,... | collective-permute-start | bytes 1179656 | tf_op jit(solution)/shard_map/ppermute | solution.py:562
  136.7 6.8 %collective-permute-start.22 = (f32[8,512]{1,0:T(8,128)S(1)}, f32[8,512]{1,0:T(8,128)S(1)}, u32[]{:S(2)}, u32[]{:S(2)}) collective-permute-start(f32[8,512]{1,0:T(8,128)S(1)} %get-tuple-element.70), channel_id=1, source_target_pairs={{0,2},{1,3},{2,4},{3,5},{4,6},{5,7},{6,0},{7,1},{8,10},{9,11},{10,... | collective-permute-start | bytes 49160 | tf_op jit(solution)/shard_map/ppermute | solution.py:587
  136.7 6.7 %collective-permute-start.23 = (f32[8,512]{1,0:T(8,128)S(1)}, f32[8,512]{1,0:T(8,128)S(1)}, u32[]{:S(2)}, u32[]{:S(2)}) collective-permute-start(f32[8,512]{1,0:T(8,128)S(1)} %get-tuple-element.70), channel_id=1, source_target_pairs={{0,4},{1,5},{2,6},{3,7},{4,0},{5,1},{6,2},{7,3},{8,12},{9,13},{10,... | collective-permute-start | bytes 49160 | tf_op jit(solution)/shard_map/ppermute | solution.py:587
  137.4 6.1 %collective-permute-start.24 = (f32[8,512]{1,0:T(8,128)S(1)}, f32[8,512]{1,0:T(8,128)S(1)}, u32[]{:S(2)}, u32[]{:S(2)}) collective-permute-start(f32[8,512]{1,0:T(8,128)S(1)} %get-tuple-element.70), channel_id=1, source_target_pairs={{0,6},{1,7},{2,0},{3,1},{4,2},{5,3},{6,4},{7,5},{8,14},{9,15},{10,... | collective-permute-start | bytes 49160 | tf_op jit(solution)/shard_map/ppermute | solution.py:587
  143.5 5.3 %collective-permute-start.25 = (f32[32,512]{1,0:T(8,128)S(1)}, f32[32,512]{1,0:T(8,128)S(1)}, u32[]{:S(2)}, u32[]{:S(2)}) collective-permute-start(f32[32,512]{1,0:T(8,128)S(1)} %pad_maximum_fusion.refs_0_), channel_id=1, source_target_pairs={{0,8},{8,16},{16,24},{24,0},{1,9},{9,17},{17,25},{25,1},{2,10},{10... | collective-permute-start | bytes 196616 | tf_op jit(solution)/shard_map/ppermute | solution.py:583
  144.0 5.0 %collective-permute-start.26 = (f32[32,512]{1,0:T(8,128)S(1)}, f32[32,512]{1,0:T(8,128)S(1)}, u32[]{:S(2)}, u32[]{:S(2)}) collective-permute-start(f32[32,512]{1,0:T(8,128)S(1)} %pad_maximum_fusion.refs_0_), channel_id=1, source_target_pairs={{0,16},{8,24},{16,0},{24,8},{1,17},{9,25},{17,1},{25,9},{2,18},{10... | collective-permute-start | bytes 196616 | tf_op jit(solution)/shard_map/ppermute | solution.py:583
  145.0 4.8 %collective-permute-start.27 = (f32[32,512]{1,0:T(8,128)S(1)}, f32[32,512]{1,0:T(8,128)S(1)}, u32[]{:S(2)}, u32[]{:S(2)}) collective-permute-start(f32[32,512]{1,0:T(8,128)S(1)} %pad_maximum_fusion.refs_0_), channel_id=1, source_target_pairs={{0,24},{8,0},{16,8},{24,16},{1,25},{9,1},{17,9},{25,17},{2,26},{10... | collective-permute-start | bytes 196616 | tf_op jit(solution)/shard_map/ppermute | solution.py:583
  147.9 1.9 %collective-permute-start.28 = (f32[32,512]{1,0:T(8,128)S(1)}, f32[32,512]{1,0:T(8,128)S(1)}, u32[]{:S(2)}, u32[]{:S(2)}) collective-permute-start(f32[32,512]{1,0:T(8,128)S(1)} %pad_maximum_fusion.refs_0_), channel_id=1, source_target_pairs={{0,1},{1,0},{2,3},{3,2},{4,5},{5,4},{6,7},{7,6},{8,9},{9,8},{10,11... | collective-permute-start | bytes 196616 | tf_op jit(solution)/shard_map/ppermute | solution.py:537
  148.8 1.3 collective-permute-start.29
  149.0 1.3 collective-permute-start.30
  149.8 1.3 collective-permute-start.31

commit v6 on v5

--- a/solution.py
+++ b/solution.py
@@ -565,14 +565,14 @@
 
     arrived = fetched(picks(0, [left, left_other]), (3, 1, 2))
     first = place(0, places, arrived)
-    lender = jnp.where(inner == 1, after(from_middle, *arrived), from_inner)
+    lender = jnp.where(inner == 1, after(from_middle, *arrived[1::2]), from_inner)
     near = lax.ppermute(first, "scan", sides)
     arrived2 = fetched(picks(1, [left, left_other, right, right_other]), (3, 1, 2))
     blocks = picks(2, [lender, other_core(lender)])
     second = place(1, places, [after(arrived2[0], blocks[0]), *arrived2[1:]])
     arrived = fetched(blocks, (3, 1, 2))
+    far = lax.ppermute(second, "scan", middle)
     hop = lax.ppermute(second, "scan", [(0, 1), (3, 2)])
-    far = lax.ppermute(second, "scan", middle)
     begun = arrived[3:4] if direct else arrived
     so_far = near_sums(sign, modulus_table, after(near, *begun), voxels, velocity0, modulus_class)
     so_far = far_sums(inner, sign, near, far, hop, voxels, so_far)

time: 155 us -> 155 us (level)
  no operation moved by 1% of the time
where the time goes in v6:
time: 155 us; the launch traced here: 154 us
  waiting for transfers between devices  78.3 us (51%)
  starting transfers between devices  45.4 us (29%)
  Pallas kernels  26.9 us (17%)
  local copies, waits for them, and re-layouts  1.6 us (1%)
    ppermute x9, waiting for transfers between devices, fetched(): arrived[turn] = lax.ppermute(block, 'slab', turns[turn])  40.2 us
    ppermute x1, waiting for transfers between devices, on_device(): hop = lax.ppermute(second, 'scan', [(0, 1), (3, 2)])  18.1 us
    ppermute x1, waiting for transfers between devices, on_device(): from_inner = lax.ppermute(right, 'scan', [(1, 0), (2, 3)])  17 us
    ppermute x9, starting transfers between devices, fetched(): arrived[turn] = lax.ppermute(block, 'slab', turns[turn])  12.3 us
    ppermute x1, starting transfers between devices, on_device(): hop = lax.ppermute(second, 'scan', [(0, 1), (3, 2)])  11.2 us
    pallas_call x3, Pallas kernels, pick(): pl.pallas_call(functools.partial(pick_kernel, chips, capacity, number), i...  7.1 us
    ppermute x3, starting transfers between devices, on_device(): lax.ppermute(tables[turn], 'slab', turns[turn])  5.57 us
    ppermute x3, starting transfers between devices, scans_of(): return [block] + [lax.ppermute(block, 'scan', route) for route in routes]  4.42 us
  transfers between devices with their start and end apart: 32, of which 12 were waited for; matrix products, arithmetic and copies ran while one was open for 0% of the time, Pallas kernels for 13%

profile of v6, /device:TPU:0, one launch (start us, length us, event | category | flops | bytes accessed | tf_op | source)
XLA Modules:
  0.0 154.2 jit_solution(7749826265910313868)
XLA Ops:
  0.6 0.7 bitcast_add_fusion.early_ref
  1.4 3.0 %collective-permute-start = (s32[1,512]{1,0:T(1,128)S(1)}, s32[1,512]{1,0:T(1,128)S(1)}, u32[]{:S(2)}, u32[]{:S(2)}) collective-permute-start(s32[1,512]{1,0:T(1,128)S(1)} %get-tuple-element.79), channel_id=1, source_target_pairs={{0,8},{8,0},{16,24},{24,16},{1,9},{9,1},{17,25},{25,17},{2,10},{10... | collective-permute-start | bytes 6152 | tf_op jit(solution)/shard_map/ppermute | solution.py:527
  4.4 0.6 collective-permute-start.1
  5.0 0.0 copy-start
  5.0 1.6 %copy-done = f32[1,512,1024]{2,1,0:T(8,128)S(1)} copy-done((f32[1,512,1024]{2,1,0:T(8,128)S(1)}, f32[1,512,1024]{2,1,0:T(8,128)}, u32[]{:S(2)}) %copy-start) | copy-done | bytes 2097176
  6.6 2.5 %prefilter.1 = (f32[512,512]{1,0:T(8,128)S(1)}, f32[512,512]{1,0:T(8,128)S(1)}) custom-call(f32[512,1024]{1,0:T(8,128)S(1)} %bitcast.10, s32[2,512]{1,0:T(2,128)S(1)} %bitcast_add_fusion.early_ref), custom_call_target="tpu_custom_call" | custom-call | flops 1610612736 | bytes 4194304 | tf_op jit(solution)/shard_map/prefilter/pallas_call | solution.py:73
  9.2 0.0 collective-permute-done.side_ref
  9.2 0.0 collective-permute-done.1.inward_ref
  9.2 0.9 requests.1
  10.1 0.0 collective-permute-start.5
  10.1 1.6 %collective-permute-start.2 = (s32[2,384]{1,0:T(2,128)S(1)}, s32[2,384]{1,0:T(2,128)S(1)}, u32[]{:S(2)}, u32[]{:S(2)}) collective-permute-start(s32[2,384]{1,0:T(2,128)S(1)} %get-tuple-element.42), channel_id=1, source_target_pairs={{0,2},{1,3},{2,4},{3,5},{4,6},{5,7},{6,0},{7,1},{8,10},{9,11},{10,... | collective-permute-start | bytes 9224 | tf_op jit(solution)/shard_map/ppermute | solution.py:532
  11.7 2.6 %collective-permute-start.3 = (s32[2,384]{1,0:T(2,128)S(1)}, s32[2,384]{1,0:T(2,128)S(1)}, u32[]{:S(2)}, u32[]{:S(2)}) collective-permute-start(s32[2,384]{1,0:T(2,128)S(1)} %get-tuple-element.43), channel_id=1, source_target_pairs={{0,4},{1,5},{2,6},{3,7},{4,0},{5,1},{6,2},{7,3},{8,12},{9,13},{10,... | collective-permute-start | bytes 9224 | tf_op jit(solution)/shard_map/ppermute | solution.py:532
  14.3 1.4 collective-permute-start.4
  15.7 0.7 collective-permute-start.11
  16.4 1.3 collective-permute-start.12
  17.7 0.2 collective-permute-done.4.refs_3_
  17.9 0.0 collective-permute-done.5.refs_5_
  17.9 2.8 %pick.3 = (f32[192,512]{1,0:T(8,128)S(1)}, f32[192,512]{1,0:T(8,128)S(1)}, f32[192,512]{1,0:T(8,128)S(1)}, f32[192,512]{1,0:T(8,128)S(1)}) custom-call(s32[1]{0:T(128)} %bitcast.1.inner_ref, s32[2,384]{1,0:T(2,128)S(1)} %get-tuple-element.41.refs_0_, s32[2,384]{1,0:T(2,128)S(1)} %collective-permute-done.2.refs_1_, ...), custom_call_target="tpu_custom_call" | custom-call | flops 19327352832 | bytes 5242880 | tf_op jit(solution)/shard_map/pick/pallas_call | solution.py:183
  20.7 2.3 %collective-permute-start.7 = (f32[192,512]{1,0:T(8,128)S(1)}, f32[192,512]{1,0:T(8,128)S(1)}, u32[]{:S(2)}, u32[]{:S(2)}) collective-permute-start(f32[192,512]{1,0:T(8,128)S(1)} %get-tuple-element.50), channel_id=1, source_target_pairs={{0,4},{1,5},{2,6},{3,7},{4,0},{5,1},{6,2},{7,3},{8,12},{9,13},{10,... | collective-permute-start | bytes 1179656 | tf_op jit(solution)/shard_map/ppermute | solution.py:562
  23.0 1.5 collective-permute-start.6
  24.5 2.3 %collective-permute-start.8 = (f32[192,512]{1,0:T(8,128)S(1)}, f32[192,512]{1,0:T(8,128)S(1)}, u32[]{:S(2)}, u32[]{:S(2)}) collective-permute-start(f32[192,512]{1,0:T(8,128)S(1)} %get-tuple-element.51), channel_id=1, source_target_pairs={{0,6},{1,7},{2,0},{3,1},{4,2},{5,3},{6,4},{7,5},{8,14},{9,15},{10,... | collective-permute-start | bytes 1179656 | tf_op jit(solution)/shard_map/ppermute | solution.py:562
  26.8 2.8 %pick.4 = (f32[192,512]{1,0:T(8,128)S(1)}, f32[192,512]{1,0:T(8,128)S(1)}, f32[192,512]{1,0:T(8,128)S(1)}, f32[192,512]{1,0:T(8,128)S(1)}) custom-call(s32[1]{0:T(128)} %bitcast.1.inner_ref, s32[2,384]{1,0:T(2,128)S(1)} %get-tuple-element.41.refs_0_, s32[2,384]{1,0:T(2,128)S(1)} %collective-permute-done.2.refs_1_, ...), custom_call_target="tpu_custom_call" | custom-call | flops 19327352832 | bytes 5242880 | tf_op jit(solution)/shard_map/pick/pallas_call | solution.py:183
  29.6 21.7 %collective-permute-done.7.refs_2_ = f32[192,512]{1,0:T(8,128)S(1)} collective-permute-done((f32[192,512]{1,0:T(8,128)S(1)}, f32[192,512]{1,0:T(8,128)S(1)}, u32[]{:S(2)}, u32[]{:S(2)}) %collective-permute-start.7) | collective-permute-done | bytes 393248 | tf_op jit(solution)/shard_map/ppermute | solution.py:562
  51.3 0.0 collective-permute-start.15
  51.3 0.0 collective-permute-done.11
  51.3 17.0 %collective-permute-done.12 = f32[512,512]{1,0:T(8,128)S(1)} collective-permute-done((f32[512,512]{1,0:T(8,128)S(1)}, f32[512,512]{1,0:T(8,128)S(1)}, u32[]{:S(2)}, u32[]{:S(2)}) %collective-permute-start.12) | collective-permute-done | bytes 1048608 | tf_op jit(solution)/shard_map/ppermute | solution.py:542
  68.3 0.2 broadcast_select_fusion.refs_4_
  68.5 0.1 collective-permute-start.13
  68.6 0.7 collective-permute-start.14
  69.3 3.1 %collective-permute-start.16 = (f32[192,512]{1,0:T(8,128)S(1)}, f32[192,512]{1,0:T(8,128)S(1)}, u32[]{:S(2)}, u32[]{:S(2)}) collective-permute-start(f32[192,512]{1,0:T(8,128)S(1)} %get-tuple-element.62), channel_id=1, source_target_pairs={{0,6},{1,7},{2,0},{3,1},{4,2},{5,3},{6,4},{7,5},{8,14},{9,15},{10,... | collective-permute-start | bytes 1179656 | tf_op jit(solution)/shard_map/ppermute | solution.py:562
  72.5 1.4 place.2
  73.9 1.1 collective-permute-start.9
  75.1 0.0 collective-permute-done.13.refs_5_
  75.1 1.5 %pick.5 = (f32[192,512]{1,0:T(8,128)S(1)}, f32[192,512]{1,0:T(8,128)S(1)}, f32[192,512]{1,0:T(8,128)S(1)}, f32[192,512]{1,0:T(8,128)S(1)}) custom-call(s32[1]{0:T(128)} %bitcast.1.inner_ref, s32[2,384]{1,0:T(2,128)S(1)} %get-tuple-element.41.refs_0_, s32[2,384]{1,0:T(2,128)S(1)} %collective-permute-done.2.refs_1_, ...), custom_call_target="tpu_custom_call" | custom-call | flops 19327352832 | bytes 5242880 | tf_op jit(solution)/shard_map/pick/pallas_call | solution.py:183
  76.6 15.4 %collective-permute-done.16.refs_3_ = f32[192,512]{1,0:T(8,128)S(1)} collective-permute-done((f32[192,512]{1,0:T(8,128)S(1)}, f32[192,512]{1,0:T(8,128)S(1)}, u32[]{:S(2)}, u32[]{:S(2)}) %collective-permute-start.16) | collective-permute-done | bytes 393248 | tf_op jit(solution)/shard_map/ppermute | solution.py:562
  92.1 0.0 copy-start.4
  92.1 0.0 collective-permute-done.14.refs_1_
  92.1 1.4 place.3
  93.5 0.7 collective-permute-start.17
  94.3 11.2 %collective-permute-start.18 = (f32[512,512]{1,0:T(8,128)S(1)}, f32[512,512]{1,0:T(8,128)S(1)}, u32[]{:S(2)}, u32[]{:S(2)}) collective-permute-start(f32[512,512]{1,0:T(8,128)S(1)} %place.3), channel_id=1, source_target_pairs={{0,8},{24,16},{1,9},{25,17},{2,10},{26,18},{3,11},{27,19},{4,12},{... | collective-permute-start | bytes 3145736 | tf_op jit(solution)/shard_map/ppermute | solution.py:575
  105.5 2.1 %collective-permute-start.21 = (f32[192,512]{1,0:T(8,128)S(1)}, f32[192,512]{1,0:T(8,128)S(1)}, u32[]{:S(2)}, u32[]{:S(2)}) collective-permute-start(f32[192,512]{1,0:T(8,128)S(1)} %get-tuple-element.69), channel_id=1, source_target_pairs={{0,4},{1,5},{2,6},{3,7},{4,0},{5,1},{6,2},{7,3},{8,12},{9,13},{10,... | collective-permute-start | bytes 1179656 | tf_op jit(solution)/shard_map/ppermute | solution.py:562
  107.7 0.0 collective-permute-done.9.near_ref
  107.7 0.2 collective-permute-start.20
  107.9 1.8 %near_sums.1.so_far_ref = f32[8,512]{1,0:T(8,128)S(1)} custom-call(f32[1]{0:T(128)} %bitcast.2.sign_ref, f32[4]{0:T(128)S(1)} %copy-done.4, f32[512,512]{1,0:T(8,128)S(1)} %collective-permute-done.9.near_ref, f32[512,1024]{1,0:T(8,128)S(1)} %bitcast.11, f32[1,512]{1,0:T(1,128)S(1)} %copy-done.2, s32[1,512]{1,0:T(1,128)S(1)} %copy-done.3), custom_call_target="tpu_custom_call" | custom-call | flops 20971520000 | bytes 5242880 | tf_op jit(solution)/shard_map/near_sums/pallas_call | solution.py:304
  109.7 18.1 %collective-permute-done.18.hop_ref = f32[512,512]{1,0:T(8,128)S(1)} collective-permute-done((f32[512,512]{1,0:T(8,128)S(1)}, f32[512,512]{1,0:T(8,128)S(1)}, u32[]{:S(2)}, u32[]{:S(2)}) %collective-permute-start.18) | collective-permute-done | bytes 1048608 | tf_op jit(solution)/shard_map/ppermute | solution.py:575
  127.8 3.0 %far_sums.1.so_far_ref = f32[8,512]{1,0:T(8,128)S(1)} custom-call(s32[1]{0:T(128)} %bitcast.1.inner_ref, f32[1]{0:T(128)} %bitcast.2.sign_ref, f32[512,512]{1,0:T(8,128)S(1)} %collective-permute-done.9.near_ref, f32[512,512]{1,0:T(8,128)S(1)} %collective-permute-done.17.far_ref, f32[512,512]{1,0:T(8,128)S(1)} %collective-permute-done.18.hop_ref, ...), custom_call_target="tpu_custom_call" | custom-call | flops 15728640 | bytes 5242880 | tf_op jit(solution)/shard_map/far_sums/pallas_call | solution.py:338
  130.8 3.1 %collective-permute-done.21.refs_2_ = f32[192,512]{1,0:T(8,128)S(1)} collective-permute-done((f32[192,512]{1,0:T(8,128)S(1)}, f32[192,512]{1,0:T(8,128)S(1)}, u32[]{:S(2)}, u32[]{:S(2)}) %collective-permute-start.21) | collective-permute-done | bytes 393248 | tf_op jit(solution)/shard_map/ppermute | solution.py:562
  133.9 2.8 %right_sums.1 = (f32[8,512]{1,0:T(8,128)S(1)}, f32[512,512]{1,0:T(8,128)S(1)}) custom-call(s32[1]{0:T(128)} %bitcast.1.inner_ref, f32[1]{0:T(128)} %bitcast.2.sign_ref, s32[3,512,128]{2,1,0:T(8,128)S(1)} %get-tuple-element.40.place_ref, f32[512,512]{1,0:T(8,128)S(1)} %collective-permute-done.9.near_ref, f32[512,512]{1,0:T(8,128)S(1)} %collective-permute-done.17.far_ref, ...), custom_call_target="tpu_custom_call" | custom-call | flops 1207959552 | bytes 5242880 | tf_op jit(solution)/shard_map/right_sums/pallas_call | solution.py:368
  136.7 0.1 collective-permute-start.22
  136.7 0.7 collective-permute-start.23
  137.4 3.1 %collective-permute-start.24 = (f32[8,512]{1,0:T(8,128)S(1)}, f32[8,512]{1,0:T(8,128)S(1)}, u32[]{:S(2)}, u32[]{:S(2)}) collective-permute-start(f32[8,512]{1,0:T(8,128)S(1)} %get-tuple-element.70), channel_id=1, source_target_pairs={{0,6},{1,7},{2,0},{3,1},{4,2},{5,3},{6,4},{7,5},{8,14},{9,15},{10,... | collective-permute-start | bytes 49160 | tf_op jit(solution)/shard_map/ppermute | solution.py:587
  140.5 2.9 %shapes.1 = (f32[512,1024]{1,0:T(8,128)S(1)}, f32[512,1024]{1,0:T(8,128)S(1)}, f32[512,1024]{1,0:T(8,128)S(1)}) custom-call(s32[1]{0:T(128)} %bitcast.1.inner_ref, f32[1]{0:T(128)} %bitcast.2.sign_ref, f32[512,512]{1,0:T(8,128)S(1)} %collective-permute-done.9.near_ref, f32[512,512]{1,0:T(8,128)S(1)} %collective-permute-done.17.far_ref, ...), custom_call_target="tpu_custom_call" | custom-call | flops 15728640 | bytes 14680064 | tf_op jit(solution)/shard_map/shapes/pallas_call | solution.py:438
  143.4 0.0 collective-permute-done.22
  143.5 0.6 collective-permute-start.25
  144.0 1.0 collective-permute-start.26
  145.0 2.8 %collective-permute-start.27 = (f32[32,512]{1,0:T(8,128)S(1)}, f32[32,512]{1,0:T(8,128)S(1)}, u32[]{:S(2)}, u32[]{:S(2)}) collective-permute-start(f32[32,512]{1,0:T(8,128)S(1)} %pad_maximum_fusion.refs_0_), channel_id=1, source_target_pairs={{0,24},{8,0},{16,8},{24,16},{1,25},{9,1},{17,9},{25,17},{2,26},{10... | collective-permute-start | bytes 196616 | tf_op jit(solution)/shard_map/ppermute | solution.py:583
  147.9 0.9 collective-permute-done.25.refs_1_
  148.8 0.2 collective-permute-done.26.refs_2_
  149.0 0.3 collective-permute-start.30
  149.3 0.5 collective-permute-done.27.refs_3_
  149.8 0.3 collective-permute-done.29.refs_5_
  150.1 0.2 collective-permute-done.30.refs_6_
  150.2 0.8 collective-permute-done.31.refs_7_
  151.0 3.0 %finish.1 = (f32[1,512]{1,0:T(1,128)}, f32[512,1024]{1,0:T(8,128)}) custom-call(s32[1]{0:T(128)} %bitcast.at_ref, f32[32,512]{1,0:T(8,128)S(1)} %pad_maximum_fusion.refs_0_, f32[32,512]{1,0:T(8,128)S(1)} %collective-permute-done.25.refs_1_, f32[32,512]{1,0:T(8,128)S(1)} %collective-permute-done.26.refs_2_, f32[32,512]{1,0:T(8,128)S(1)} %collective-permute-done.27.refs_3_, ...), custom_call_target="tpu_custom_call" | custom-call | tf_op jit(solution)/shard_map/finish/pallas_call | solution.py:483
  (26 shorter events, 0.1 us)
Async XLA Ops:
  1.4 7.8 %collective-permute-start = (s32[1,512]{1,0:T(1,128)S(1)}, s32[1,512]{1,0:T(1,128)S(1)}, u32[]{:S(2)}, u32[]{:S(2)}) collective-permute-start(s32[1,512]{1,0:T(1,128)S(1)} %get-tuple-element.79), channel_id=1, source_target_pairs={{0,8},{8,0},{16,24},{24,16},{1,9},{9,1},{17,25},{25,17},{2,10},{10... | collective-permute-start | bytes 6152 | tf_op jit(solution)/shard_map/ppermute | solution.py:527
  4.4 4.8 %collective-permute-start.1 = (s32[1,512]{1,0:T(1,128)S(1)}, s32[1,512]{1,0:T(1,128)S(1)}, u32[]{:S(2)}, u32[]{:S(2)}) collective-permute-start(s32[1,512]{1,0:T(1,128)S(1)} %get-tuple-element.78.own_ref), channel_id=1, source_target_pairs={{8,16},{16,8},{9,17},{17,9},{10,18},{18,10},{11,19},{19,11},{12,20... | collective-permute-start | bytes 6152 | tf_op jit(solution)/shard_map/ppermute | solution.py:527
  5.0 1.6 %copy-start = (f32[1,512,1024]{2,1,0:T(8,128)S(1)}, f32[1,512,1024]{2,1,0:T(8,128)}, u32[]{:S(2)}) copy-start(f32[1,512,1024]{2,1,0:T(8,128)} %param.6) | copy-start | bytes 6291460
  10.1 7.9 %collective-permute-start.5 = (f32[512,512]{1,0:T(8,128)S(1)}, f32[512,512]{1,0:T(8,128)}, u32[]{:S(2)}, u32[]{:S(2)}) collective-permute-start(f32[512,512]{1,0:T(8,128)S(1)} %get-tuple-element.47.refs_4_), channel_id=1, source_target_pairs={{0,1},{1,0},{2,3},{3,2},{4,5},{5,4},{6,7},{7,6},{8,9},{9,8},{10,11... | collective-permute-start | bytes 3145736 | tf_op jit(solution)/shard_map/ppermute | solution.py:537
  10.1 5.6 %collective-permute-start.2 = (s32[2,384]{1,0:T(2,128)S(1)}, s32[2,384]{1,0:T(2,128)S(1)}, u32[]{:S(2)}, u32[]{:S(2)}) collective-permute-start(s32[2,384]{1,0:T(2,128)S(1)} %get-tuple-element.42), channel_id=1, source_target_pairs={{0,2},{1,3},{2,4},{3,5},{4,6},{5,7},{6,0},{7,1},{8,10},{9,11},{10,... | collective-permute-start | bytes 9224 | tf_op jit(solution)/shard_map/ppermute | solution.py:532
  11.7 4.7 %collective-permute-start.3 = (s32[2,384]{1,0:T(2,128)S(1)}, s32[2,384]{1,0:T(2,128)S(1)}, u32[]{:S(2)}, u32[]{:S(2)}) collective-permute-start(s32[2,384]{1,0:T(2,128)S(1)} %get-tuple-element.43), channel_id=1, source_target_pairs={{0,4},{1,5},{2,6},{3,7},{4,0},{5,1},{6,2},{7,3},{8,12},{9,13},{10,... | collective-permute-start | bytes 9224 | tf_op jit(solution)/shard_map/ppermute | solution.py:532
  14.3 3.6 %collective-permute-start.4 = (s32[2,384]{1,0:T(2,128)S(1)}, s32[2,384]{1,0:T(2,128)S(1)}, u32[]{:S(2)}, u32[]{:S(2)}) collective-permute-start(s32[2,384]{1,0:T(2,128)S(1)} %get-tuple-element.44), channel_id=1, source_target_pairs={{0,6},{1,7},{2,0},{3,1},{4,2},{5,3},{6,4},{7,5},{8,14},{9,15},{10,... | collective-permute-start | bytes 9224 | tf_op jit(solution)/shard_map/ppermute | solution.py:532
  15.7 8.8 %collective-permute-start.10 = (f32[512,512]{1,0:T(8,128)S(1)}, f32[512,512]{1,0:T(8,128)S(1)}, u32[]{:S(2)}, u32[]{:S(2)}) collective-permute-start(f32[512,512]{1,0:T(8,128)S(1)} %get-tuple-element.52.refs_6_), channel_id=1, source_target_pairs={{0,1},{1,0},{2,3},{3,2},{4,5},{5,4},{6,7},{7,6},{8,9},{9,8},{10,11... | collective-permute-start | bytes 3145736 | tf_op jit(solution)/shard_map/ppermute | solution.py:537
  15.7 35.6 %collective-permute-start.11 = (f32[512,512]{1,0:T(8,128)S(1)}, f32[512,512]{1,0:T(8,128)S(1)}, u32[]{:S(2)}, u32[]{:S(2)}) collective-permute-start(f32[512,512]{1,0:T(8,128)S(1)} %get-tuple-element.52.refs_6_), channel_id=1, source_target_pairs={{8,16},{16,8},{9,17},{17,9},{10,18},{18,10},{11,19},{19,11},{12,20... | collective-permute-start | bytes 3145736 | tf_op jit(solution)/shard_map/ppermute | solution.py:543
  16.4 51.9 %collective-permute-start.12 = (f32[512,512]{1,0:T(8,128)S(1)}, f32[512,512]{1,0:T(8,128)S(1)}, u32[]{:S(2)}, u32[]{:S(2)}) collective-permute-start(f32[512,512]{1,0:T(8,128)S(1)} %get-tuple-element.52.refs_6_), channel_id=1, source_target_pairs={{8,0},{16,24},{9,1},{17,25},{10,2},{18,26},{11,3},{19,27},{12,4},{... | collective-permute-start | bytes 3145736 | tf_op jit(solution)/shard_map/ppermute | solution.py:542
  20.7 30.6 %collective-permute-start.7 = (f32[192,512]{1,0:T(8,128)S(1)}, f32[192,512]{1,0:T(8,128)S(1)}, u32[]{:S(2)}, u32[]{:S(2)}) collective-permute-start(f32[192,512]{1,0:T(8,128)S(1)} %get-tuple-element.50), channel_id=1, source_target_pairs={{0,4},{1,5},{2,6},{3,7},{4,0},{5,1},{6,2},{7,3},{8,12},{9,13},{10,... | collective-permute-start | bytes 1179656 | tf_op jit(solution)/shard_map/ppermute | solution.py:562
  23.0 28.3 %collective-permute-start.6 = (f32[192,512]{1,0:T(8,128)S(1)}, f32[192,512]{1,0:T(8,128)S(1)}, u32[]{:S(2)}, u32[]{:S(2)}) collective-permute-start(f32[192,512]{1,0:T(8,128)S(1)} %get-tuple-element.49), channel_id=1, source_target_pairs={{0,2},{1,3},{2,4},{3,5},{4,6},{5,7},{6,0},{7,1},{8,10},{9,11},{10,... | collective-permute-start | bytes 1179656 | tf_op jit(solution)/shard_map/ppermute | solution.py:562
  24.5 26.8 %collective-permute-start.8 = (f32[192,512]{1,0:T(8,128)S(1)}, f32[192,512]{1,0:T(8,128)S(1)}, u32[]{:S(2)}, u32[]{:S(2)}) collective-permute-start(f32[192,512]{1,0:T(8,128)S(1)} %get-tuple-element.51), channel_id=1, source_target_pairs={{0,6},{1,7},{2,0},{3,1},{4,2},{5,3},{6,4},{7,5},{8,14},{9,15},{10,... | collective-permute-start | bytes 1179656 | tf_op jit(solution)/shard_map/ppermute | solution.py:562
  51.3 40.8 %collective-permute-start.15 = (f32[192,512]{1,0:T(8,128)S(1)}, f32[192,512]{1,0:T(8,128)S(1)}, u32[]{:S(2)}, u32[]{:S(2)}) collective-permute-start(f32[192,512]{1,0:T(8,128)S(1)} %get-tuple-element.60), channel_id=1, source_target_pairs={{0,4},{1,5},{2,6},{3,7},{4,0},{5,1},{6,2},{7,3},{8,12},{9,13},{10,... | collective-permute-start | bytes 1179656 | tf_op jit(solution)/shard_map/ppermute | solution.py:562
  68.5 6.6 %collective-permute-start.13 = (f32[512,512]{1,0:T(8,128)S(1)}, f32[512,512]{1,0:T(8,128)S(1)}, u32[]{:S(2)}, u32[]{:S(2)}) collective-permute-start(f32[512,512]{1,0:T(8,128)S(1)} %broadcast_select_fusion.refs_4_), channel_id=1, source_target_pairs={{0,1},{1,0},{2,3},{3,2},{4,5},{5,4},{6,7},{7,6},{8,9},{9,8},{10,11... | collective-permute-start | bytes 3145736 | tf_op jit(solution)/shard_map/ppermute | solution.py:537
  68.6 23.5 %collective-permute-start.14 = (f32[192,512]{1,0:T(8,128)S(1)}, f32[192,512]{1,0:T(8,128)S(1)}, u32[]{:S(2)}, u32[]{:S(2)}) collective-permute-start(f32[192,512]{1,0:T(8,128)S(1)} %get-tuple-element.58), channel_id=1, source_target_pairs={{0,2},{1,3},{2,4},{3,5},{4,6},{5,7},{6,0},{7,1},{8,10},{9,11},{10,... | collective-permute-start | bytes 1179656 | tf_op jit(solution)/shard_map/ppermute | solution.py:562
  69.3 22.7 %collective-permute-start.16 = (f32[192,512]{1,0:T(8,128)S(1)}, f32[192,512]{1,0:T(8,128)S(1)}, u32[]{:S(2)}, u32[]{:S(2)}) collective-permute-start(f32[192,512]{1,0:T(8,128)S(1)} %get-tuple-element.62), channel_id=1, source_target_pairs={{0,6},{1,7},{2,0},{3,1},{4,2},{5,3},{6,4},{7,5},{8,14},{9,15},{10,... | collective-permute-start | bytes 1179656 | tf_op jit(solution)/shard_map/ppermute | solution.py:562
  73.9 33.7 %collective-permute-start.9 = (f32[512,512]{1,0:T(8,128)S(1)}, f32[512,512]{1,0:T(8,128)S(1)}, u32[]{:S(2)}, u32[]{:S(2)}) collective-permute-start(f32[512,512]{1,0:T(8,128)S(1)} %place.2), channel_id=1, source_target_pairs={{0,8},{8,0},{16,24},{24,16},{1,9},{9,1},{17,25},{25,17},{2,10},{10... | collective-permute-start | bytes 3145736 | tf_op jit(solution)/shard_map/ppermute | solution.py:569
  92.0 15.8 %collective-permute-start.19 = (f32[192,512]{1,0:T(8,128)S(1)}, f32[192,512]{1,0:T(8,128)S(1)}, u32[]{:S(2)}, u32[]{:S(2)}) collective-permute-start(f32[192,512]{1,0:T(8,128)S(1)} %get-tuple-element.64), channel_id=1, source_target_pairs={{0,6},{1,7},{2,0},{3,1},{4,2},{5,3},{6,4},{7,5},{8,14},{9,15},{10,... | collective-permute-start | bytes 1179656 | tf_op jit(solution)/shard_map/ppermute | solution.py:562
  92.0 15.8 %copy-start.1 = (f32[1,512,1024]{2,1,0:T(8,128)S(1)}, f32[1,512,1024]{2,1,0:T(8,128)}, u32[]{:S(2)}) copy-start(f32[1,512,1024]{2,1,0:T(8,128)} %param.6) | copy-start | bytes 6291460
  92.0 15.8 %copy-start.2 = (f32[1,512]{1,0:T(1,128)S(1)}, f32[1,512]{1,0:T(1,128)}, u32[]{:S(2)}) copy-start(f32[1,512]{1,0:T(1,128)} %start_ref.1) | copy-start | bytes 6148
  92.1 15.8 %copy-start.3 = (s32[1,512]{1,0:T(1,128)S(1)}, s32[1,512]{1,0:T(1,128)}, u32[]{:S(2)}) copy-start(s32[1,512]{1,0:T(1,128)} %class_ref.1) | copy-start | bytes 6148
  92.1 15.8 %copy-start.4 = (f32[4]{0:T(128)S(1)}, f32[4]{0:T(128)}, u32[]{:S(2)}) copy-start(f32[4]{0:T(128)} %table_ref.1) | copy-start | bytes 52
  93.5 16.2 %collective-permute-start.17 = (f32[512,512]{1,0:T(8,128)S(1)}, f32[512,512]{1,0:T(8,128)S(1)}, u32[]{:S(2)}, u32[]{:S(2)}) collective-permute-start(f32[512,512]{1,0:T(8,128)S(1)} %place.3), channel_id=1, source_target_pairs={{8,16},{16,8},{9,17},{17,9},{10,18},{18,10},{11,19},{19,11},{12,20... | collective-permute-start | bytes 3145736 | tf_op jit(solution)/shard_map/ppermute | solution.py:574
  94.3 33.5 %collective-permute-start.18 = (f32[512,512]{1,0:T(8,128)S(1)}, f32[512,512]{1,0:T(8,128)S(1)}, u32[]{:S(2)}, u32[]{:S(2)}) collective-permute-start(f32[512,512]{1,0:T(8,128)S(1)} %place.3), channel_id=1, source_target_pairs={{0,8},{24,16},{1,9},{25,17},{2,10},{26,18},{3,11},{27,19},{4,12},{... | collective-permute-start | bytes 3145736 | tf_op jit(solution)/shard_map/ppermute | solution.py:575
  105.5 28.3 %collective-permute-start.21 = (f32[192,512]{1,0:T(8,128)S(1)}, f32[192,512]{1,0:T(8,128)S(1)}, u32[]{:S(2)}, u32[]{:S(2)}) collective-permute-start(f32[192,512]{1,0:T(8,128)S(1)} %get-tuple-element.69), channel_id=1, source_target_pairs={{0,4},{1,5},{2,6},{3,7},{4,0},{5,1},{6,2},{7,3},{8,12},{9,13},{10,... | collective-permute-start | bytes 1179656 | tf_op jit(solution)/shard_map/ppermute | solution.py:562
  107.7 26.2 %collective-permute-start.20 = (f32[192,512]{1,0:T(8,128)S(1)}, f32[192,512]{1,0:T(8,128)S(1)}, u32[]{:S(2)}, u32[]{:S(2)}) collective-permute-start(f32[192,512]{1,0:T(8,128)S(1)} %get-tuple-element.67), channel_id=1, source_target_pairs={{0,2},{1,3},{2,4},{3,5},{4,6},{5,7},{6,0},{7,1},{8,10},{9,11},{10,... | collective-permute-start | bytes 1179656 | tf_op jit(solution)/shard_map/ppermute | solution.py:562
  136.7 6.8 %collective-permute-start.22 = (f32[8,512]{1,0:T(8,128)S(1)}, f32[8,512]{1,0:T(8,128)S(1)}, u32[]{:S(2)}, u32[]{:S(2)}) collective-permute-start(f32[8,512]{1,0:T(8,128)S(1)} %get-tuple-element.70), channel_id=1, source_target_pairs={{0,2},{1,3},{2,4},{3,5},{4,6},{5,7},{6,0},{7,1},{8,10},{9,11},{10,... | collective-permute-start | bytes 49160 | tf_op jit(solution)/shard_map/ppermute | solution.py:587
  136.7 6.7 %collective-permute-start.23 = (f32[8,512]{1,0:T(8,128)S(1)}, f32[8,512]{1,0:T(8,128)S(1)}, u32[]{:S(2)}, u32[]{:S(2)}) collective-permute-start(f32[8,512]{1,0:T(8,128)S(1)} %get-tuple-element.70), channel_id=1, source_target_pairs={{0,4},{1,5},{2,6},{3,7},{4,0},{5,1},{6,2},{7,3},{8,12},{9,13},{10,... | collective-permute-start | bytes 49160 | tf_op jit(solution)/shard_map/ppermute | solution.py:587
  137.4 6.1 %collective-permute-start.24 = (f32[8,512]{1,0:T(8,128)S(1)}, f32[8,512]{1,0:T(8,128)S(1)}, u32[]{:S(2)}, u32[]{:S(2)}) collective-permute-start(f32[8,512]{1,0:T(8,128)S(1)} %get-tuple-element.70), channel_id=1, source_target_pairs={{0,6},{1,7},{2,0},{3,1},{4,2},{5,3},{6,4},{7,5},{8,14},{9,15},{10,... | collective-permute-start | bytes 49160 | tf_op jit(solution)/shard_map/ppermute | solution.py:587
  143.5 5.3 %collective-permute-start.25 = (f32[32,512]{1,0:T(8,128)S(1)}, f32[32,512]{1,0:T(8,128)S(1)}, u32[]{:S(2)}, u32[]{:S(2)}) collective-permute-start(f32[32,512]{1,0:T(8,128)S(1)} %pad_maximum_fusion.refs_0_), channel_id=1, source_target_pairs={{0,8},{8,16},{16,24},{24,0},{1,9},{9,17},{17,25},{25,1},{2,10},{10... | collective-permute-start | bytes 196616 | tf_op jit(solution)/shard_map/ppermute | solution.py:583
  144.0 5.0 %collective-permute-start.26 = (f32[32,512]{1,0:T(8,128)S(1)}, f32[32,512]{1,0:T(8,128)S(1)}, u32[]{:S(2)}, u32[]{:S(2)}) collective-permute-start(f32[32,512]{1,0:T(8,128)S(1)} %pad_maximum_fusion.refs_0_), channel_id=1, source_target_pairs={{0,16},{8,24},{16,0},{24,8},{1,17},{9,25},{17,1},{25,9},{2,18},{10... | collective-permute-start | bytes 196616 | tf_op jit(solution)/shard_map/ppermute | solution.py:583
  145.0 4.8 %collective-permute-start.27 = (f32[32,512]{1,0:T(8,128)S(1)}, f32[32,512]{1,0:T(8,128)S(1)}, u32[]{:S(2)}, u32[]{:S(2)}) collective-permute-start(f32[32,512]{1,0:T(8,128)S(1)} %pad_maximum_fusion.refs_0_), channel_id=1, source_target_pairs={{0,24},{8,0},{16,8},{24,16},{1,25},{9,1},{17,9},{25,17},{2,26},{10... | collective-permute-start | bytes 196616 | tf_op jit(solution)/shard_map/ppermute | solution.py:583
  147.9 1.9 %collective-permute-start.28 = (f32[32,512]{1,0:T(8,128)S(1)}, f32[32,512]{1,0:T(8,128)S(1)}, u32[]{:S(2)}, u32[]{:S(2)}) collective-permute-start(f32[32,512]{1,0:T(8,128)S(1)} %pad_maximum_fusion.refs_0_), channel_id=1, source_target_pairs={{0,1},{1,0},{2,3},{3,2},{4,5},{5,4},{6,7},{7,6},{8,9},{9,8},{10,11... | collective-permute-start | bytes 196616 | tf_op jit(solution)/shard_map/ppermute | solution.py:537
  148.8 1.3 collective-permute-start.29
  149.0 1.3 collective-permute-start.30
  149.8 1.3 collective-permute-start.31
